TPU v7x, 256 devices: a whole 4x4x8 slice. The times are simulated.
256 devices in a mesh: dp: 16 (over z_lo, x), tensor: 16 (over y, z_hi, core).
Axes of the slice: x: 4, y: 4, z: 8 (z_hi: 2, z_lo: 4; z = z_hi * 4 + z_lo), core: 2. Of those that a mesh axis runs over, the one named last changes fastest.
Arguments:
- hidden_rows: bfloat16 [16, 256, 14336], P('dp', 'tensor'), may hold values from -6 to 6
- out_grad: bfloat16 [16, 256, 4096], P('dp', None, 'tensor'), may hold values from -0.5 to 0.5
- down_weight: bfloat16 [14336, 4096], P('dp', 'tensor'), may hold values from -4 to 4
- query_init: float32 [64, 4096], P(None, 'tensor'), may hold values from -6 to 6
Outputs:
- input_grad: bfloat16 [16, 256, 14336], P('dp', 'tensor')
- q_factor: float32 [64, 4096], P(None, 'tensor')
- error_new: bfloat16 [16, 14336, 4096], P('dp', None, 'tensor')
All inputs are finite; a program needn't handle non-finite values.
Results may differ from a plain program's by a relative error of at most 0.017.
Values may be sent and summed in bfloat16 or wider, within the bound.
No kernel may reach another device: no remote copies, remote signals or barrier semaphores. Data moves between devices by JAX's collectives and lax.ppermute only.
A program may use at most 128 MiB of HBM per device.

v0:
```python
import jax
import jax.numpy as jnp
from jax import lax
from jax.sharding import PartitionSpec as P


def on_device(hidden_rows, out_grad, down_weight, query_init):
    grad_local = out_grad[0]
    groups = lax.axis_size("dp")
    highest = lax.Precision.HIGHEST
    full_weight = lax.all_gather(down_weight, "dp", axis=0, tiled=True)
    block = grad_local
    summed = lax.psum_scatter(
        jnp.einsum("td,fd->tf", block, full_weight, preferred_element_type=jnp.float32).astype(
            jnp.bfloat16
        ),
        "tensor",
        scatter_dimension=0,
        tiled=True,
    )
    input_grad = summed[None]
    block = grad_local
    merged = jnp.einsum(
        "tf,td->fd",
        lax.all_gather(hidden_rows, "tensor", axis=1, tiled=True)[0],
        block,
        preferred_element_type=jnp.float32,
    )
    local_left = jnp.einsum("rd,fd->rf", query_init, merged, precision=highest)
    left = lax.psum(local_left.astype(jnp.bfloat16), "dp").astype(jnp.float32) / groups
    gram = jnp.einsum("rf,sf->rs", left, left, precision=highest)
    lower = jnp.linalg.cholesky(gram)
    ortho = lax.linalg.triangular_solve(lower, left, left_side=True, lower=True)
    local_right = jnp.einsum("rf,fd->rd", ortho, merged, precision=highest)
    right = lax.psum(local_right.astype(jnp.bfloat16), "dp").astype(jnp.float32) / groups
    approx = jnp.einsum("rf,rd->fd", ortho, right, precision=highest)
    error_new = (merged - approx).astype(jnp.bfloat16)[None]
    return (input_grad, right, error_new)


def solution(mesh):
    placed = (
        P("dp", "tensor", None),
        P("dp", None, "tensor"),
        P("dp", "tensor"),
        P(None, "tensor"),
    )
    return jax.shard_map(
        on_device,
        mesh=mesh,
        in_specs=placed,
        out_specs=(P("dp", "tensor", None), P(None, "tensor"), P("dp", None, "tensor")),
        check_vma=False,
    )
```

profile of v0, /device:TPU:16, one launch (start us, length us, event | category | flops | bytes accessed | tf_op | source)
XLA Modules:
  0.0 521.6 jit_solution(8252653464518810899)
XLA Ops:
  7.2 0.0 copy-start
  7.2 0.0 all-gather.5.cloned.1.call-start
  7.2 0.7 all-gather.5.cloned.1.call-update
  7.9 0.0 all-gather.3.cloned.1.call-start
  8.0 0.7 all-gather.3.cloned.1.call-update
  8.7 0.0 copy-start.4
  8.7 0.0 all-reduce.2.cloned.1.call-start
  8.7 103.9 %all-gather.5.cloned.1.call-done = bf16[1,256,14336]{2,1,0:T(8,128)(2,1)} async-done(((bf16[1,16,14336]{2,1,0:T(8,128)(2,1)}), bf16[1,256,14336]{2,1,0:T(8,128)(2,1)}) %all-gather.5.cloned.1.call-update) | async-done | bytes 7340048 | tf_op jit(solution)/shard_map/all_gather | solution.py:25
  112.6 0.0 copy-done
  112.6 5.2 fusion.3
  117.8 0.0 copy-start.1
  117.8 5.2 copy-done.1
  123.0 0.0 copy-done.4
  123.0 15.3 %fusion.2 = bf16[64,14336]{1,0:T(8,128)(2,1)} fusion(f32[14336,256]{1,0:T(8,128)S(1)} %fusion.3, f32[64,256]{1,0:T(8,128)S(1)} %copy-done.4), kind=kOutput, calls=%fused_computation.5 | convolution fusion | flops 2819489792 | bytes 16580608 | tf_op jit(solution)/shard_map/rd,fd->rf/dot_general | solution.py:29
  138.3 0.0 all-reduce.2.cloned.1.call-update
  138.3 0.2 reduce-scatter.2.cloned.1.call-start
  138.5 68.8 %all-gather.3.cloned.1.call-done = bf16[14336,256]{1,0:T(8,128)(2,1)} async-done(((bf16[896,256]{1,0:T(8,128)(2,1)}), bf16[14336,256]{1,0:T(8,128)(2,1)}) %all-gather.3.cloned.1.call-update) | async-done | bytes 7340048 | tf_op jit(solution)/shard_map/all_gather | solution.py:11
  207.4 8.1 %convolution_convert_fusion = bf16[256,14336]{1,0:T(8,128)(2,1)} fusion(bf16[14336,256]{1,0:T(8,128)(2,1)} %all-gather.3.cloned.1.call-done, bf16[1,256,256]{2,1,0:T(8,128)(2,1)S(1)} %copy-done), kind=kOutput, calls=%fused_computation.2 | convolution fusion | flops 1882718208 | bytes 14811136 | tf_op jit(solution)/shard_map/td,fd->tf/dot_general | solution.py:14
  215.5 0.0 reduce-scatter.2.cloned.1.call-update
  215.5 157.9 %all-reduce.2.cloned.1.call-done = bf16[64,14336]{1,0:T(8,128)(2,1)} async-done(((bf16[64,14336]{1,0:T(8,128)(2,1)}), bf16[64,14336]{1,0:T(8,128)(2,1)}) %all-reduce.2.cloned.1.call-update) | async-done | bytes 1835024 | tf_op jit(solution)/shard_map/psum | solution.py:30
  373.4 5.5 %fusion.6 = f32[64,64]{1,0:T(8,128)S(1)} fusion(bf16[64,14336]{1,0:T(8,128)(2,1)} %all-reduce.2.cloned.1.call-done), kind=kOutput, calls=%fused_computation.10 | convolution fusion | flops 706478080 | bytes 1851392 | tf_op jit(solution)/shard_map/rf,sf->rs/dot_general | solution.py:31
  379.0 0.1 copy.7
  379.1 5.8 %cholesky.16 = f32[64,64]{1,0:T(8,128)S(1)} custom-call(f32[64,64]{1,0:T(8,128)S(1)} %fusion.13), custom_call_target="Cholesky" | custom-call | tf_op jit(solution)/shard_map/jit(cholesky)/cholesky | solution.py:32
  384.9 0.6 compare_reduce_fusion
  385.6 0.7 fusion.11
  386.3 4.9 custom-call.6
  391.2 4.9 fusion.5
  396.1 1.9 copy-done.2
  398.0 11.5 %convolution_convert_fusion.2 = bf16[64,256]{1,0:T(8,128)(2,1)S(1)} fusion(f32[64,14336]{1,0:T(8,128)S(1)} %fusion.5, f32[14336,256]{1,0:T(8,128)} %copy-done.1), kind=kOutput, calls=%fused_computation.13 | convolution fusion | flops 2818588672 | bytes 18382848 | tf_op jit(solution)/shard_map/rf,fd->rd/dot_general | solution.py:34
  409.4 88.1 %psum.15 = bf16[64,256]{1,0:T(8,128)(2,1)S(1)} all-reduce(bf16[64,256]{1,0:T(8,128)(2,1)S(1)} %convolution_convert_fusion.2), channel_id=1, replica_groups=mesh['dp'=16,'tensor'=16] {'dp'}, use_global_device_ids=true, to_apply=%region_4.5 | all-reduce | flops 16384 | bytes 65536 | tf_op jit(solution)/shard_map/psum | solution.py:35
  497.5 0.0 copy-start.3
  497.5 17.5 %fusion.1 = bf16[1,14336,256]{2,1,0:T(8,128)(2,1)} fusion(f32[14336,256]{1,0:T(8,128)} %copy-done.1, f32[64,14336]{1,0:T(8,128)} %copy-done.2, f32[64,256]{1,0:T(8,128)S(1)} %convert_multiply_fusion.3), kind=kOutput, calls=%fused_computation.3 | convolution fusion | flops 2825912320 | bytes 25755648 | tf_op jit(solution)/shard_map/rf,rd->fd/dot_general | solution.py:36
  (6 shorter events, 0.1 us)
Async XLA Ops:
  7.2 105.4 %copy-start = (bf16[1,256,256]{2,1,0:T(8,128)(2,1)S(1)}, bf16[1,256,256]{2,1,0:T(8,128)(2,1)}, u32[]{:S(2)}) copy-start(bf16[1,256,256]{2,1,0:T(8,128)(2,1)} %param.5) | copy-start | bytes 393220
  7.2 105.4 %all-gather.5.cloned.1.call-start = ((), (), s32[]{:S(2)}) async-start(), calls=%async_computation.3 | async-start | bytes 7798784 | tf_op jit(solution)/shard_map/all_gather | solution.py:25
  7.9 199.4 %all-gather.3.cloned.1.call-start = ((), (), s32[]{:S(2)}) async-start(), calls=%async_computation.1 | async-start | bytes 7798784 | tf_op jit(solution)/shard_map/all_gather | solution.py:11
  8.7 114.3 %copy-start.4 = (f32[64,256]{1,0:T(8,128)S(1)}, f32[64,256]{1,0:T(8,128)}, u32[]{:S(2)}) copy-start(f32[64,256]{1,0:T(8,128)} %param.7) | copy-start | bytes 196612
  8.7 364.8 %all-reduce.2.cloned.1.call-start = ((), (), s32[]{:S(2)}) async-start(), calls=%async_computation.4 | async-start | bytes 3670016 | tf_op jit(solution)/shard_map/psum | solution.py:30
  117.8 5.2 copy-start.1
  138.3 376.7 %reduce-scatter.2.cloned.1.call-start = ((), (), s32[]{:S(2)}) async-start(), calls=%async_computation.2 | async-start | bytes 7798784 | tf_op jit(solution)/shard_map/reduce_scatter | solution.py:13
  396.1 1.9 copy-start.2
  497.5 17.5 %copy-start.3 = (f32[64,256]{1,0:T(8,128)}, f32[64,256]{1,0:T(8,128)S(1)}, u32[]{:S(2)}) copy-start(f32[64,256]{1,0:T(8,128)S(1)} %convert_multiply_fusion.3) | copy-start | bytes 196612
Sparse Core Ops, SparseCore 0:
  10.7 101.8 all-gather.4
  114.4 92.9 all-gather.2
  210.6 162.7 all-reduce.1
  379.0 126.3 reduce-scatter.1
where the time goes:
time: 522 us
  waiting for transfers between devices  332 us (64%)
  blocking collectives  88.1 us (17%)
  matrix products  68 us (13%)
  between operations  13.9 us (3%)
  other arithmetic  12.1 us (2%)
  local copies, waits for them, and re-layouts  7.14 us (1%)
    psum x1, waiting for transfers between devices, on_device(): lax.psum(local_left.astype(jnp.bfloat16), 'dp').astype(jnp.float32) / groups  158 us
    all_gather x1, waiting for transfers between devices, on_device(): lax.all_gather(hidden_rows, 'tensor', axis=1, tiled=True)[0]  104 us
    psum x1, blocking collectives, on_device(): lax.psum(local_right.astype(jnp.bfloat16), 'dp').astype(jnp.float32)  88.1 us
    all_gather x1, waiting for transfers between devices, on_device(): full_weight = lax.all_gather(down_weight, 'dp', axis=0, tiled=True)  68.8 us
    dot_general x1, matrix products, on_device(): approx = jnp.einsum('rf,rd->fd', ortho, right, precision=highest)  17.5 us
    dot_general x1, matrix products, on_device(): local_left = jnp.einsum('rd,fd->rf', query_init, merged, precision=highest)  15.3 us
    dot_general x1, matrix products, on_device(): local_right = jnp.einsum('rf,fd->rd', ortho, merged, precision=highest)  11.5 us
  transfers between devices with their start and end apart: 4, of which 3 were waited for; matrix products, arithmetic and copies ran while one was open for 15% of the time, Pallas kernels for 0%

commit v1 on v0

v1 whole, which is shorter than its diff:
```python
import functools

import jax
import jax.numpy as jnp
from jax import lax
from jax.experimental import pallas as pl
from jax.experimental.pallas import tpu as pltpu
from jax.sharding import Mesh
from jax.sharding import PartitionSpec as P

AXES = ("zl", "x", "y", "zh", "c")
SIZES = (4, 4, 4, 2, 2)
F = 14336
BLOCK = 896
RANK = 64
TOKENS = 256
COLS = 256
STEP = 2048
PART = 128
BF = jnp.bfloat16
F32 = jnp.float32
HIGH = lax.Precision.HIGHEST
SWAP = ((0, 1), (1, 0))
VMEM = pl.BlockSpec(memory_space=pltpu.VMEM)
SMEM = pl.BlockSpec(memory_space=pltpu.SMEM)
LIMIT = pltpu.CompilerParams(vmem_limit_bytes=24 * 2**20)


def shift(s):
    return tuple((i, (i + s) % 4) for i in range(4))


def flip(s):
    return tuple((i, i ^ s) for i in range(4))


def ring3(value, axis):
    return [lax.ppermute(value, axis, shift(-s)) for s in (1, 2, 3)]


def flip3(value):
    return [lax.ppermute(value, "zl", flip(s)) for s in (1, 2, 3)]


def after(value, *others):
    return lax.optimization_barrier((value, *others))[0]


def dot(a, b, ca, cb):
    return lax.dot_general(a, b, (((ca,), (cb,)), ((), ())), preferred_element_type=F32)


def thirds(value):
    parts = []
    for _ in range(3):
        parts.append(value.astype(BF))
        value = value - parts[-1].astype(F32)
    return parts


def call(kernel, shapes, tables, arrays, flops, name):
    nbytes = sum(a.size * a.dtype.itemsize for a in arrays)
    return pl.pallas_call(
        kernel,
        out_shape=[jax.ShapeDtypeStruct(s, d) for s, d in shapes],
        in_specs=[SMEM] * len(tables) + [VMEM] * len(arrays),
        out_specs=[VMEM] * len(shapes),
        compiler_params=LIMIT,
        cost_estimate=pl.CostEstimate(flops=flops, bytes_accessed=nbytes, transcendentals=0),
        name=name,
    )(*tables, *arrays)


def prepare_kernel(order, grad, query, rows_ref, a_ref):
    for i in range(16):
        rows_ref[16 * i : 16 * i + 16, :] = grad[order[i]]
    rows = rows_ref[...]
    a = sum(dot(q, rows, 1, 1) for q in reversed(thirds(query[...])))
    high = a.astype(BF)
    a_ref[:RANK, :] = high
    a_ref[RANK:, :] = (a - high.astype(F32)).astype(BF)


def lay_kernel(blocks, out_ref):
    for j in range(16):
        out_ref[:, BLOCK * j : BLOCK * (j + 1)] = blocks[j]


def left_kernel(table, a_ref, *refs):
    hidden, outs = refs[:4], refs[4:]
    a = a_ref[...]
    for r in range(4):
        for p in range(4):
            here = pl.ds(pl.multiple_of(table[4 * r + p] * BLOCK, 128), BLOCK)
            both = dot(a, jnp.concatenate([h[:, here] for h in hidden], axis=0), 1, 0)
            outs[r][p] = (both[:RANK] + both[RANK:]).astype(BF)


def sum_kernel(a, b, c, d, own, *outs):
    for p in range(4):
        total = (a[p].astype(F32) + b[p].astype(F32)) + (c[p].astype(F32) + d[p].astype(F32))
        if p == 0:
            own[...] = total
        else:
            outs[p - 1][...] = total.astype(BF)


def stats_kernel(table, *refs):
    lefts, hidden, grad = refs[:4], refs[4:8], refs[8]
    left_ref, local_ref, gram_ref = refs[9:]
    total = jnp.zeros((TOKENS + RANK, RANK), F32)
    for r in range(4):
        for p in range(4):
            here = pl.ds(pl.multiple_of(table[4 * r + p] * BLOCK, 128), BLOCK)
            block = lefts[r][p]
            total += dot(jnp.concatenate([h[:, here] for h in hidden] + [block], axis=0), block, 1, 1)
            left_ref[:, here] = block
    gram_ref[...] = total[TOKENS:]
    local_ref[...] = sum(dot(t, grad[...], 0, 0) for t in reversed(thirds(total[:TOKENS])))


def inverse_kernel(gram, out_ref):
    row_of = lax.broadcasted_iota(jnp.int32, (RANK, 1), 0)
    eye = lax.broadcasted_iota(jnp.int32, (RANK, RANK), 0) == lax.broadcasted_iota(jnp.int32, (RANK, RANK), 1)
    both = jnp.concatenate([gram[...], eye.astype(F32)], axis=1)
    for k in range(RANK):
        pivot = both[k : k + 1, k : k + 1]
        factor = jnp.where(row_of > k, both[:, k : k + 1] / pivot, 0.0)
        scale = jnp.where(row_of == k, lax.rsqrt(pivot), 1.0)
        both = both * scale - factor * both[k : k + 1, :]
    out_ref[...] = both[:, RANK:]


def error_kernel(inverse, s0, s1, s2, s3, grad, left, h0, h1, h2, h3, right_ref, out_ref, weights):
    @pl.when(pl.program_id(0) == 0)
    def _():
        summed = (s0[...] + s1[...]) + (s2[...] + s3[...])
        inv = inverse[...]
        right = lax.dot_general(
            inv, summed, (((1,), (0,)), ((), ())), precision=HIGH, preferred_element_type=F32
        ) * (1.0 / 16)
        right_ref[...] = right
        m = -lax.dot_general(inv, right, (((0,), (0,)), ((), ())), precision=HIGH, preferred_element_type=F32)
        high = m.astype(BF)
        weights[:TOKENS, :] = grad[...]
        weights[TOKENS : TOKENS + RANK, :] = high
        weights[TOKENS + RANK :, :] = (m - high.astype(F32)).astype(BF)

    block = left[...]
    rows = jnp.concatenate([h0[...], h1[...], h2[...], h3[...], block, block], axis=0)
    out_ref[...] = dot(rows, weights[...], 0, 0).astype(BF)


def error_of(inverse, sums, grad, left, hidden):
    def whole(a):
        return pl.BlockSpec(a.shape, lambda i: (0, 0))

    def some(a):
        return pl.BlockSpec((a.shape[0], STEP), lambda i: (0, i))

    return pl.pallas_call(
        error_kernel,
        out_shape=(jax.ShapeDtypeStruct((RANK, COLS), F32), jax.ShapeDtypeStruct((F, COLS), BF)),
        grid=(F // STEP,),
        in_specs=[whole(inverse)] + [whole(s) for s in sums] + [whole(grad), some(left)] + [some(h) for h in hidden],
        out_specs=(
            pl.BlockSpec((RANK, COLS), lambda i: (0, 0)),
            pl.BlockSpec((STEP, COLS), lambda i: (i, 0)),
        ),
        scratch_shapes=[pltpu.VMEM((TOKENS + 2 * RANK, COLS), BF)],
        compiler_params=LIMIT,
        cost_estimate=pl.CostEstimate(
            flops=2 * (TOKENS + 2 * RANK) * F * COLS,
            bytes_accessed=2 * (TOKENS + RANK + COLS) * F,
            transcendentals=0,
        ),
        name="error_new",
    )(inverse, *sums, grad, left, *hidden)


def input_kernel(group, t0, t1, t2, t3, weight, out_ref):
    total = jnp.zeros((TOKENS, PART), F32)
    for d in range(16):
        rows = jnp.concatenate([t[:, d].reshape(64, COLS) for t in (t0, t1, t2, t3)], axis=0)
        total += dot(rows, weight[d], 1, 1)
    total = total.astype(BF).reshape(16, 16, PART)
    for i in range(16):
        out_ref[group[i]] = total[i]


def input_of(group, tokens, weight):
    return pl.pallas_call(
        input_kernel,
        out_shape=jax.ShapeDtypeStruct((16, 16, BLOCK), BF),
        grid=(BLOCK // PART,),
        in_specs=[SMEM]
        + [pl.BlockSpec(t.shape, lambda i: (0, 0, 0, 0)) for t in tokens]
        + [pl.BlockSpec((16, PART, COLS), lambda i: (0, i, 0))],
        out_specs=pl.BlockSpec((16, 16, PART), lambda i: (0, 0, i)),
        compiler_params=LIMIT,
        cost_estimate=pl.CostEstimate(
            flops=2 * TOKENS * 16 * COLS * BLOCK, bytes_accessed=10 * 2**20, transcendentals=0
        ),
        name="input_grad",
    )(group, *tokens, weight)


def on_device(hidden_rows, out_grad, down_weight, query_init):
    zl, x, y, zh, c = (lax.axis_index(a) for a in AXES)
    four = jnp.arange(4)
    ahead = (y + four) % 4
    grad = out_grad[0]
    mine = hidden_rows[0]

    with jax.named_scope("prepare"):
        order = jnp.concatenate([ahead * 4 + h * 2 + k for k in (c, 1 - c) for h in (zh, 1 - zh)]).astype(jnp.int32)
        grad_rows, a = call(
            prepare_kernel,
            [((TOKENS, COLS), BF), ((2 * RANK, TOKENS), BF)],
            [order],
            [grad.reshape(16, 16, COLS), query_init],
            2 * 3 * RANK * TOKENS * COLS,
            "prepare",
        )

    with jax.named_scope("hidden_gather"):
        other = lax.ppermute(mine, "zh", SWAP)
        rest = ring3(mine, "y")
        near = jnp.concatenate([mine] + rest, axis=0)
        far = jnp.concatenate([other] + ring3(after(other, near, a), "y"), axis=0)
        hidden = [near, far, lax.ppermute(near, "c", SWAP)]

    with jax.named_scope("weight_gather"):
        weight = lax.all_gather(down_weight, ("y", "zh", "c"))

    with jax.named_scope("grad_gather"):
        tokens = lax.all_to_all(grad.reshape(16, 16, COLS), ("y", "zh", "c"), 0, 0)
        tokens = jnp.stack([tokens] + flip3(tokens))
        far, tokens = lax.optimization_barrier((far, tokens))
        hidden = [near, far, hidden[2], lax.ppermute(far, "c", SWAP)]

    table = (((x + four) % 4)[:, None] * 4 + (zl ^ four)[None, :]).reshape(16).astype(jnp.int32)
    with jax.named_scope("left_reduce"):
        parts = call(
            left_kernel,
            [((4, RANK, BLOCK), BF)] * 4,
            [table],
            [a, *hidden],
            2 * 2 * RANK * TOKENS * F,
            "left",
        )
        parts = [parts[0]] + [lax.ppermute(parts[r], "x", shift(r)) for r in (1, 2, 3)]
        block, *sends = call(
            sum_kernel,
            [((RANK, BLOCK), F32)] + [((RANK, BLOCK), BF)] * 3,
            [],
            parts,
            16 * RANK * BLOCK,
            "sum",
        )
        ready = after(tokens, sends[0])
        token1, token3 = (lax.ppermute(ready, "x", shift(-s)) for s in (1, 3))
        for s in (1, 2, 3):
            block = block + lax.ppermute(sends[s - 1], "zl", flip(s)).astype(F32)
        block, token1, token3 = lax.optimization_barrier(((block * (1.0 / 16)).astype(BF), token1, token3))
    with jax.named_scope("left_gather"):
        token2 = lax.ppermute(after(tokens, block), "x", shift(-2))
        column = jnp.stack([block] + flip3(block))
        column, token2 = lax.optimization_barrier((column, token2))
        lefts = [column] + ring3(column, "x")

    with jax.named_scope("input_grad"):
        group = ((zl ^ four)[None, :] * 4 + ((x + four) % 4)[:, None]).reshape(16).astype(jnp.int32)
        partial = input_of(group, [after(tokens, column), token1, token2, token3], weight)
        lefts, _ = lax.optimization_barrier((lefts, partial))

    with jax.named_scope("stats"):
        left, local, gram = call(
            stats_kernel,
            [((RANK, F), BF), ((RANK, COLS), F32), ((RANK, RANK), F32)],
            [table],
            [*lefts, *hidden, grad_rows],
            2 * RANK * (TOKENS + RANK) * F,
            "stats",
        )
    with jax.named_scope("right"):
        for v in ring3(local, "x"):
            local = local + v
        sums = [local] + flip3(local)
        inverse = call(inverse_kernel, [((RANK, RANK), F32)], [], [after(gram, local)], 64 * 64 * 128 * 2, "inverse")[0]
    with jax.named_scope("error_new"):
        right, error_new = error_of(inverse, sums, grad_rows, left, hidden)

    with jax.named_scope("input_grad"):
        summed = lax.all_to_all(partial, ("zl", "x"), 0, 0)
        input_grad = call(lay_kernel, [((16, F), BF)], [], [summed], 16 * F, "lay")[0][None]
    return input_grad, right, error_new[None]


def solution(mesh):
    fine = Mesh(mesh.devices.reshape(SIZES), AXES)
    dp, tensor = ("zl", "x"), ("y", "zh", "c")
    return jax.shard_map(
        on_device,
        mesh=fine,
        in_specs=(P(dp, tensor, None), P(dp, None, tensor), P(dp, tensor), P(None, tensor)),
        out_specs=(P(dp, tensor, None), P(None, tensor), P(dp, None, tensor)),
        check_vma=False,
    )
```

time: 522 us -> 215 us (0.41)
  waiting for transfers between devices: 332 us -> 65.9 us
  blocking collectives: 88.1 us -> 0 us
  starting transfers between devices: 0.34 us -> 87.3 us
  matrix products: 68 us -> 0 us
  Pallas kernels: 0 us -> 33.9 us
  other arithmetic: 12.1 us -> 4.62 us
    all_gather x2 -> x1, waiting for transfers between devices: 173 us -> 0.01 us  [on_device(): weight = lax.all_gather(down_weight, ('y', 'zh', 'c'))]
    psum x1 -> x0, waiting for transfers between devices: 158 us -> none  [on_device(): lax.psum(local_left.astype(jnp.bfloat16), 'dp').astype(jnp.float32) / groups]
    psum x1 -> x0, blocking collectives: 88.1 us -> none  [on_device(): lax.psum(local_right.astype(jnp.bfloat16), 'dp').astype(jnp.float32)]
    ppermute x0 -> x33, starting transfers between devices: none -> 76.1 us  [the longest x9 28.6 us: flip3(): return [lax.ppermute(value, 'zl', flip(s)) for s in (1, 2, 3)]]
    ppermute x0 -> x33, waiting for transfers between devices: none -> 65.2 us  [the longest x12 19.2 us: ring3(): return [lax.ppermute(value, axis, shift(-s)) for s in (1, 2, 3)]]
    dot_general x6 -> x0, matrix products: 63.1 us -> none  [the longest x1 17.5 us: on_device(): approx = jnp.einsum('rf,rd->fd', ortho, right, precision=highest)]
    pallas_call x0 -> x8, Pallas kernels: none -> 33.9 us  [the longest x6 17.1 us: call(): pl.pallas_call(kernel, out_shape=[jax.ShapeDtypeStruct(s, d) for s, d in...]
    another operation x5 -> x2, other arithmetic: 12.1 us -> 0.14 us  [the longest x1 0.07 us: on_device(): column = jnp.stack([block] + flip3(block))]
  transfers between devices with their start and end apart: 4 -> 36, of which waited for: 3 -> 17; matrix products, arithmetic and copies ran while one was open for 15% -> 2% of each run, Pallas kernels for 0% -> 15%
where the time goes in v1:
time: 215 us
  starting transfers between devices  87.3 us (41%)
  waiting for transfers between devices  65.9 us (31%)
  Pallas kernels  33.9 us (16%)
  between operations  14.2 us (7%)
  local copies, waits for them, and re-layouts  8.67 us (4%)
  other arithmetic  4.62 us (2%)
    ppermute x9, starting transfers between devices, flip3(): return [lax.ppermute(value, 'zl', flip(s)) for s in (1, 2, 3)]  28.6 us
    ppermute x12, waiting for transfers between devices, ring3(): return [lax.ppermute(value, axis, shift(-s)) for s in (1, 2, 3)]  19.2 us
    ppermute x3, waiting for transfers between devices, on_device(): lax.ppermute(parts[r], 'x', shift(r))  19.2 us
    pallas_call x6, Pallas kernels, call(): pl.pallas_call(kernel, out_shape=[jax.ShapeDtypeStruct(s, d) for s, d in...  17.1 us
    ppermute x12, starting transfers between devices, ring3(): return [lax.ppermute(value, axis, shift(-s)) for s in (1, 2, 3)]  16.6 us
    ppermute x9, waiting for transfers between devices, flip3(): return [lax.ppermute(value, 'zl', flip(s)) for s in (1, 2, 3)]  13 us
    ppermute x3, starting transfers between devices, on_device(): block = block + lax.ppermute(sends[s - 1], 'zl', flip(s)).astype(F32)  12.5 us
    ppermute x3, waiting for transfers between devices, on_device(): block = block + lax.ppermute(sends[s - 1], 'zl', flip(s)).astype(F32)  10.3 us
  transfers between devices with their start and end apart: 36, of which 17 were waited for; matrix products, arithmetic and copies ran while one was open for 2% of the time, Pallas kernels for 15%

profile of v1, /device:TPU:16, one launch (start us, length us, event | category | flops | bytes accessed | tf_op | source)
XLA Modules:
  0.0 214.6 jit_solution(5287327935725081376)
XLA Ops:
  10.1 2.5 %collective-permute-start.1 = (bf16[16,14336]{1,0:T(8,128)(2,1)}, bf16[16,14336]{1,0:T(8,128)(2,1)}, u32[]{:S(2)}, u32[]{:S(2)}) collective-permute-start(bf16[16,14336]{1,0:T(8,128)(2,1)} %bitcast.19), channel_id=1, source_target_pairs={{0,12},{4,0},{8,4},{12,8},{1,13},{5,1},{9,5},{13,9},{2,14},{6,2},{... | collective-permute-start | bytes 1376264 | tf_op jit(solution)/shard_map/hidden_gather/ppermute | solution.py:38
  12.7 5.5 %collective-permute-start = (bf16[16,14336]{1,0:T(8,128)(2,1)}, bf16[16,14336]{1,0:T(8,128)(2,1)S(1)}, u32[]{:S(2)}, u32[]{:S(2)}) collective-permute-start(bf16[16,14336]{1,0:T(8,128)(2,1)} %bitcast.20), channel_id=1, source_target_pairs={{0,2},{2,0},{1,3},{3,1},{4,6},{6,4},{5,7},{7,5},{8,10},{10,8},{9,1... | collective-permute-start | bytes 1376264 | tf_op jit(solution)/shard_map/hidden_gather/ppermute | solution.py:227
  18.1 6.5 %all-to-all-start = ((bf16[16,16,256]{2,1,0:T(8,128)(2,1)}), bf16[16,16,256]{2,1,0:T(8,128)(2,1)S(1)}, u32[]{:S(2)}, u32[]{:S(2)}) async-start(bf16[16,16,256]{2,1,0:T(8,128)(2,1)} %bitcast.14), calls=%async_computation | async-start | bytes 262144 | tf_op jit(solution)/shard_map/grad_gather/all_to_all | solution.py:237
  27.8 5.6 %collective-permute-done.2 = bf16[16,14336]{1,0:T(8,128)(2,1)S(1)} collective-permute-done((bf16[16,14336]{1,0:T(8,128)(2,1)}, bf16[16,14336]{1,0:T(8,128)(2,1)S(1)}, u32[]{:S(2)}, u32[]{:S(2)}) %collective-permute-start.2) | collective-permute-done | bytes 458784 | tf_op jit(solution)/shard_map/hidden_gather/ppermute | solution.py:38
  34.2 2.1 collective-permute-done.1
  42.3 8.5 %collective-permute-start.9 = (bf16[16,16,256]{2,1,0:T(8,128)(2,1)S(1)}, bf16[16,16,256]{2,1,0:T(8,128)(2,1)S(1)}, u32[]{:S(2)}, u32[]{:S(2)}) collective-permute-start(bf16[16,16,256]{2,1,0:T(8,128)(2,1)S(1)} %all-to-all-done), channel_id=1, source_target_pairs={{0,192},{64,128},{128,64},{192,0},{1,193},{65,129},{129,65},{193,1... | collective-permute-start | bytes 393224 | tf_op jit(solution)/shard_map/grad_gather/ppermute | solution.py:42
  50.8 7.4 %collective-permute-start.8 = (bf16[16,16,256]{2,1,0:T(8,128)(2,1)S(1)}, bf16[16,16,256]{2,1,0:T(8,128)(2,1)S(1)}, u32[]{:S(2)}, u32[]{:S(2)}) collective-permute-start(bf16[16,16,256]{2,1,0:T(8,128)(2,1)S(1)} %all-to-all-done), channel_id=1, source_target_pairs={{0,128},{64,192},{128,0},{192,64},{1,129},{65,193},{129,1},{193,65... | collective-permute-start | bytes 393224 | tf_op jit(solution)/shard_map/grad_gather/ppermute | solution.py:42
  58.3 3.8 %collective-permute-start.7 = (bf16[16,16,256]{2,1,0:T(8,128)(2,1)S(1)}, bf16[16,16,256]{2,1,0:T(8,128)(2,1)S(1)}, u32[]{:S(2)}, u32[]{:S(2)}) collective-permute-start(bf16[16,16,256]{2,1,0:T(8,128)(2,1)S(1)} %all-to-all-done), channel_id=1, source_target_pairs={{0,64},{64,0},{128,192},{192,128},{1,65},{65,1},{129,193},{193,129... | collective-permute-start | bytes 393224 | tf_op jit(solution)/shard_map/grad_gather/ppermute | solution.py:42
  62.1 2.3 %collective-permute-done.8 = bf16[16,16,256]{2,1,0:T(8,128)(2,1)S(1)} collective-permute-done((bf16[16,16,256]{2,1,0:T(8,128)(2,1)S(1)}, bf16[16,16,256]{2,1,0:T(8,128)(2,1)S(1)}, u32[]{:S(2)}, u32[]{:S(2)}) %collective-permute-start.8) | collective-permute-done | bytes 131104 | tf_op jit(solution)/shard_map/grad_gather/ppermute | solution.py:42
  65.8 2.7 %pad_maximum_fusion.1.refs_1_.refs_5_.h1 = bf16[64,14336]{1,0:T(8,128)(2,1)} fusion(bf16[16,14336]{1,0:T(8,128)(2,1)} %collective-permute-done.6, bf16[16,14336]{1,0:T(8,128)(2,1)} %collective-permute-done.5, bf16[16,14336]{1,0:T(8,128)(2,1)} %collective-permute-done.4, bf16[16,14336]{1,0:T(8,128)(2,1)S(1)} %collective-permute-done), kind=kLoop, calls=%fused_computation.1 | loop fusion | flops 7340032 | bytes 3670016 | tf_op jit(solution)/shard_map/hidden_gather/concatenate | solution.py:230
  69.7 3.1 %collective-permute-done.11.refs_3_.refs_7_.h3 = bf16[64,14336]{1,0:T(8,128)(2,1)} collective-permute-done((bf16[64,14336]{1,0:T(8,128)(2,1)}, bf16[64,14336]{1,0:T(8,128)(2,1)}, u32[]{:S(2)}, u32[]{:S(2)}) %collective-permute-start.11) | collective-permute-done | bytes 1835040 | tf_op jit(solution)/shard_map/grad_gather/ppermute | solution.py:240
  72.8 3.9 %left.1 = (bf16[4,64,896]{2,1,0:T(8,128)(2,1)S(1)}, bf16[4,64,896]{2,1,0:T(8,128)(2,1)S(1)}, bf16[4,64,896]{2,1,0:T(8,128)(2,1)S(1)}, bf16[4,64,896]{2,1,0:T(8,128)(2,1)S(1)}) custom-call(s32[16]{0:T(128)S(1)} %add.151.table, bf16[128,256]{1,0:T(8,128)(2,1)S(1)} %get-tuple-element.34.a_ref, bf16[64,14336]{1,0:T(8,128)(2,1)S(1)} %pad_maximum_fusion.refs_0_.refs_4_.h0, ...), custom_call_target="tpu_custom_call" | custom-call | flops 939524096 | bytes 7405568 | tf_op jit(solution)/shard_map/left_reduce/left/pallas_call | solution.py:63
  78.2 2.7 %collective-permute-start.13 = (bf16[4,64,896]{2,1,0:T(8,128)(2,1)S(1)}, bf16[4,64,896]{2,1,0:T(8,128)(2,1)S(1)}, u32[]{:S(2)}, u32[]{:S(2)}) collective-permute-start(bf16[4,64,896]{2,1,0:T(8,128)(2,1)S(1)} %get-tuple-element.40), channel_id=1, source_target_pairs={{0,32},{16,48},{32,0},{48,16},{1,33},{17,49},{33,1},{49,17},{2,34}... | collective-permute-start | bytes 1376264 | tf_op jit(solution)/shard_map/left_reduce/ppermute | solution.py:252
  82.4 8.3 %collective-permute-done.12.b = bf16[4,64,896]{2,1,0:T(8,128)(2,1)S(1)} collective-permute-done((bf16[4,64,896]{2,1,0:T(8,128)(2,1)S(1)}, bf16[4,64,896]{2,1,0:T(8,128)(2,1)S(1)}, u32[]{:S(2)}, u32[]{:S(2)}) %collective-permute-start.12) | collective-permute-done | bytes 458784 | tf_op jit(solution)/shard_map/left_reduce/ppermute | solution.py:252
  90.8 10.8 %collective-permute-done.13.c = bf16[4,64,896]{2,1,0:T(8,128)(2,1)S(1)} collective-permute-done((bf16[4,64,896]{2,1,0:T(8,128)(2,1)S(1)}, bf16[4,64,896]{2,1,0:T(8,128)(2,1)S(1)}, u32[]{:S(2)}, u32[]{:S(2)}) %collective-permute-start.13) | collective-permute-done | bytes 458784 | tf_op jit(solution)/shard_map/left_reduce/ppermute | solution.py:252
  105.3 12.0 %collective-permute-start.16 = (bf16[64,896]{1,0:T(8,128)(2,1)S(1)}, bf16[64,896]{1,0:T(8,128)(2,1)S(1)}, u32[]{:S(2)}, u32[]{:S(2)}) collective-permute-start(bf16[64,896]{1,0:T(8,128)(2,1)S(1)} %get-tuple-element.44), channel_id=1, source_target_pairs={{0,128},{64,192},{128,0},{192,64},{1,129},{65,193},{129,1},{193,65... | collective-permute-start | bytes 344072 | tf_op jit(solution)/shard_map/left_reduce/ppermute | solution.py:264
  117.8 10.3 %collective-permute-done.16 = bf16[64,896]{1,0:T(8,128)(2,1)S(1)} collective-permute-done((bf16[64,896]{1,0:T(8,128)(2,1)S(1)}, bf16[64,896]{1,0:T(8,128)(2,1)S(1)}, u32[]{:S(2)}, u32[]{:S(2)}) %collective-permute-start.16) | collective-permute-done | bytes 114720 | tf_op jit(solution)/shard_map/left_reduce/ppermute | solution.py:264
  128.2 3.1 %collective-permute-start.23 = (bf16[4,16,16,256]{3,2,1,0:T(8,128)(2,1)S(1)}, bf16[4,16,16,256]{3,2,1,0:T(8,128)(2,1)S(1)}, u32[]{:S(2)}, u32[]{:S(2)}) collective-permute-start(bf16[4,16,16,256]{3,2,1,0:T(8,128)(2,1)S(1)} %pad_maximum_fusion.2.t0), channel_id=1, source_target_pairs={{0,32},{16,48},{32,0},{48,16},{1,33},{17,49},{33,1},{49,17},{2,34}... | collective-permute-start | bytes 1572872 | tf_op jit(solution)/shard_map/left_gather/ppermute | solution.py:267
  131.3 2.3 %collective-permute-start.22 = (bf16[64,896]{1,0:T(8,128)(2,1)S(1)}, bf16[64,896]{1,0:T(8,128)(2,1)S(1)}, u32[]{:S(2)}, u32[]{:S(2)}) collective-permute-start(bf16[64,896]{1,0:T(8,128)(2,1)S(1)} %multiply_convert_fusion), channel_id=1, source_target_pairs={{0,192},{64,128},{128,64},{192,0},{1,193},{65,129},{129,65},{193,1... | collective-permute-start | bytes 344072 | tf_op jit(solution)/shard_map/left_gather/ppermute | solution.py:42
  135.7 3.2 %collective-permute-done.22 = bf16[64,896]{1,0:T(8,128)(2,1)S(1)} collective-permute-done((bf16[64,896]{1,0:T(8,128)(2,1)S(1)}, bf16[64,896]{1,0:T(8,128)(2,1)S(1)}, u32[]{:S(2)}, u32[]{:S(2)}) %collective-permute-start.22) | collective-permute-done | bytes 114720 | tf_op jit(solution)/shard_map/left_gather/ppermute | solution.py:42
  138.9 6.3 %collective-permute-done.21 = bf16[64,896]{1,0:T(8,128)(2,1)S(1)} collective-permute-done((bf16[64,896]{1,0:T(8,128)(2,1)S(1)}, bf16[64,896]{1,0:T(8,128)(2,1)S(1)}, u32[]{:S(2)}, u32[]{:S(2)}) %collective-permute-start.21) | collective-permute-done | bytes 114720 | tf_op jit(solution)/shard_map/left_gather/ppermute | solution.py:42
  150.1 3.1 %copy-done = bf16[14336,256]{1,0:T(8,128)(2,1)S(1)} copy-done((bf16[14336,256]{1,0:T(8,128)(2,1)S(1)}, bf16[14336,256]{1,0:T(8,128)(2,1)}, u32[]{:S(2)}) %copy-start) | copy-done | bytes 7340056
  155.3 6.6 %input_grad.1 = bf16[16,16,896]{2,1,0:T(8,128)(2,1)} custom-call(s32[16]{0:T(128)S(1)} %add.134.group, bf16[4,16,16,256]{3,2,1,0:T(8,128)(2,1)S(1)} %pad_maximum_fusion.2.t0, bf16[4,16,16,256]{3,2,1,0:T(8,128)(2,1)S(1)} %copy-done.2, bf16[4,16,16,256]{3,2,1,0:T(8,128)(2,1)S(1)} %copy-done.4, bf16[4,16,16,256]{3,2,1,0:T(8,128)(2,1)S(1)} %collective-permute-done.19.t3, ...), custom_call_target="tpu_custom_call" | custom-call | flops 1879048192 | bytes 10485760 | tf_op jit(solution)/shard_map/input_grad/input_grad/pallas_call | solution.py:192
  161.9 4.6 %all-to-all-start.1 = ((bf16[16,16,896]{2,1,0:T(8,128)(2,1)}), bf16[16,16,896]{2,1,0:T(8,128)(2,1)S(1)}, u32[]{:S(2)}, u32[]{:S(2)}) async-start(bf16[16,16,896]{2,1,0:T(8,128)(2,1)} %input_grad.1), calls=%async_computation.1 | async-start | bytes 917504 | tf_op jit(solution)/shard_map/input_grad/all_to_all | solution.py:295
  166.5 4.3 %collective-permute-done.26.refs_3_ = bf16[4,64,896]{2,1,0:T(8,128)(2,1)} collective-permute-done((bf16[4,64,896]{2,1,0:T(8,128)(2,1)S(1)}, bf16[4,64,896]{2,1,0:T(8,128)(2,1)}, u32[]{:S(2)}, u32[]{:S(2)}) %collective-permute-start.26) | collective-permute-done | bytes 458784 | tf_op jit(solution)/shard_map/left_gather/ppermute | solution.py:38
  170.8 2.5 %collective-permute-done.24.refs_1_ = bf16[4,64,896]{2,1,0:T(8,128)(2,1)} collective-permute-done((bf16[4,64,896]{2,1,0:T(8,128)(2,1)S(1)}, bf16[4,64,896]{2,1,0:T(8,128)(2,1)}, u32[]{:S(2)}, u32[]{:S(2)}) %collective-permute-start.24) | collective-permute-done | bytes 458784 | tf_op jit(solution)/shard_map/left_gather/ppermute | solution.py:38
  173.3 5.9 %stats.1 = (bf16[64,14336]{1,0:T(8,128)(2,1)S(1)}, f32[64,256]{1,0:T(8,128)S(1)}, f32[64,64]{1,0:T(8,128)S(1)}) custom-call(s32[16]{0:T(128)S(1)} %add.151.table, bf16[4,64,896]{2,1,0:T(8,128)(2,1)S(1)} %pad_maximum_fusion.3.refs_0_, bf16[4,64,896]{2,1,0:T(8,128)(2,1)} %collective-permute-done.24.refs_1_, ...), custom_call_target="tpu_custom_call" | custom-call | flops 587202560 | bytes 9306112 | tf_op jit(solution)/shard_map/stats/stats/pallas_call | solution.py:63
  179.3 3.3 %collective-permute-start.28 = (f32[64,256]{1,0:T(8,128)S(1)}, f32[64,256]{1,0:T(8,128)S(1)}, u32[]{:S(2)}, u32[]{:S(2)}) collective-permute-start(f32[64,256]{1,0:T(8,128)S(1)} %get-tuple-element.60), channel_id=1, source_target_pairs={{0,32},{16,48},{32,0},{48,16},{1,33},{17,49},{33,1},{49,17},{2,34}... | collective-permute-start | bytes 196616 | tf_op jit(solution)/shard_map/right/ppermute | solution.py:38
  182.5 2.2 %collective-permute-done.29 = f32[64,256]{1,0:T(8,128)S(1)} collective-permute-done((f32[64,256]{1,0:T(8,128)S(1)}, f32[64,256]{1,0:T(8,128)S(1)}, u32[]{:S(2)}, u32[]{:S(2)}) %collective-permute-start.29) | collective-permute-done | bytes 65568 | tf_op jit(solution)/shard_map/right/ppermute | solution.py:38
  188.7 2.7 %collective-permute-start.30 = (f32[64,256]{1,0:T(8,128)S(1)}, f32[64,256]{1,0:T(8,128)S(1)}, u32[]{:S(2)}, u32[]{:S(2)}) collective-permute-start(f32[64,256]{1,0:T(8,128)S(1)} %add_add_fusion.s0), channel_id=1, source_target_pairs={{0,64},{64,0},{128,192},{192,128},{1,65},{65,1},{129,193},{193,129... | collective-permute-start | bytes 196616 | tf_op jit(solution)/shard_map/right/ppermute | solution.py:42
  191.3 5.5 %inverse.1 = f32[64,64]{1,0:T(8,128)S(1)} custom-call(f32[64,64]{1,0:T(8,128)S(1)} %get-tuple-element.61.gram), custom_call_target="tpu_custom_call" | custom-call | flops 1048576 | bytes 16384 | tf_op jit(solution)/shard_map/right/inverse/pallas_call | solution.py:63
  196.8 10.1 %error_new.1 = (f32[64,256]{1,0:T(8,128)}, bf16[14336,256]{1,0:T(8,128)(2,1)}) custom-call(f32[64,64]{1,0:T(8,128)S(1)} %inverse.1, f32[64,256]{1,0:T(8,128)S(1)} %add_add_fusion.s0, f32[64,256]{1,0:T(8,128)S(1)} %collective-permute-done.30.s1, f32[64,256]{1,0:T(8,128)S(1)} %collective-permute-done.31.s2, f32[64,256]{1,0:T(8,128)S(1)} %collective-permute-done.32.s3, ...), custom_call_target="tpu_custom_call" | custom-call | flops 2818572288 | bytes 16515072 | tf_op jit(solution)/shard_map/error_new/error_new/pallas_call | solution.py:161
  (80 shorter events, 36.6 us)
Async XLA Ops:
  7.2 143.0 %all-gather.3.cloned.1.call-start = ((), (), s32[]{:S(2)}) async-start(), calls=%async_computation.2 | async-start | bytes 7798784 | tf_op jit(solution)/shard_map/weight_gather/all_gather | solution.py:234
  7.9 19.9 %collective-permute-start.3 = (bf16[16,14336]{1,0:T(8,128)(2,1)}, bf16[16,14336]{1,0:T(8,128)(2,1)S(1)}, u32[]{:S(2)}, u32[]{:S(2)}) collective-permute-start(bf16[16,14336]{1,0:T(8,128)(2,1)} %bitcast.17), channel_id=1, source_target_pairs={{0,4},{4,8},{8,12},{12,0},{1,5},{5,9},{9,13},{13,1},{2,6},{6,10},{... | collective-permute-start | bytes 1376264 | tf_op jit(solution)/shard_map/hidden_gather/ppermute | solution.py:38
  9.3 24.2 %collective-permute-start.2 = (bf16[16,14336]{1,0:T(8,128)(2,1)}, bf16[16,14336]{1,0:T(8,128)(2,1)S(1)}, u32[]{:S(2)}, u32[]{:S(2)}) collective-permute-start(bf16[16,14336]{1,0:T(8,128)(2,1)} %bitcast.18), channel_id=1, source_target_pairs={{0,8},{4,12},{8,0},{12,4},{1,9},{5,13},{9,1},{13,5},{2,10},{6,14},... | collective-permute-start | bytes 1376264 | tf_op jit(solution)/shard_map/hidden_gather/ppermute | solution.py:38
  10.1 26.2 %collective-permute-start.1 = (bf16[16,14336]{1,0:T(8,128)(2,1)}, bf16[16,14336]{1,0:T(8,128)(2,1)}, u32[]{:S(2)}, u32[]{:S(2)}) collective-permute-start(bf16[16,14336]{1,0:T(8,128)(2,1)} %bitcast.19), channel_id=1, source_target_pairs={{0,12},{4,0},{8,4},{12,8},{1,13},{5,1},{9,5},{13,9},{2,14},{6,2},{... | collective-permute-start | bytes 1376264 | tf_op jit(solution)/shard_map/hidden_gather/ppermute | solution.py:38
  12.7 25.1 %collective-permute-start = (bf16[16,14336]{1,0:T(8,128)(2,1)}, bf16[16,14336]{1,0:T(8,128)(2,1)S(1)}, u32[]{:S(2)}, u32[]{:S(2)}) collective-permute-start(bf16[16,14336]{1,0:T(8,128)(2,1)} %bitcast.20), channel_id=1, source_target_pairs={{0,2},{2,0},{1,3},{3,1},{4,6},{6,4},{5,7},{7,5},{8,10},{10,8},{9,1... | collective-permute-start | bytes 1376264 | tf_op jit(solution)/shard_map/hidden_gather/ppermute | solution.py:227
  18.1 24.2 %all-to-all-start = ((bf16[16,16,256]{2,1,0:T(8,128)(2,1)}), bf16[16,16,256]{2,1,0:T(8,128)(2,1)S(1)}, u32[]{:S(2)}, u32[]{:S(2)}) async-start(bf16[16,16,256]{2,1,0:T(8,128)(2,1)} %bitcast.14), calls=%async_computation | async-start | bytes 262144 | tf_op jit(solution)/shard_map/grad_gather/all_to_all | solution.py:237
  37.8 28.0 %collective-permute-start.6 = (bf16[16,14336]{1,0:T(8,128)(2,1)S(1)}, bf16[16,14336]{1,0:T(8,128)(2,1)}, u32[]{:S(2)}, u32[]{:S(2)}) collective-permute-start(bf16[16,14336]{1,0:T(8,128)(2,1)S(1)} %collective-permute-done), channel_id=1, source_target_pairs={{0,4},{4,8},{8,12},{12,0},{1,5},{5,9},{9,13},{13,1},{2,6},{6,10},{... | collective-permute-start | bytes 1376264 | tf_op jit(solution)/shard_map/hidden_gather/ppermute | solution.py:38
  38.8 26.9 %collective-permute-start.5 = (bf16[16,14336]{1,0:T(8,128)(2,1)S(1)}, bf16[16,14336]{1,0:T(8,128)(2,1)}, u32[]{:S(2)}, u32[]{:S(2)}) collective-permute-start(bf16[16,14336]{1,0:T(8,128)(2,1)S(1)} %collective-permute-done), channel_id=1, source_target_pairs={{0,8},{4,12},{8,0},{12,4},{1,9},{5,13},{9,1},{13,5},{2,10},{6,14},... | collective-permute-start | bytes 1376264 | tf_op jit(solution)/shard_map/hidden_gather/ppermute | solution.py:38
  40.4 25.4 %collective-permute-start.4 = (bf16[16,14336]{1,0:T(8,128)(2,1)S(1)}, bf16[16,14336]{1,0:T(8,128)(2,1)}, u32[]{:S(2)}, u32[]{:S(2)}) collective-permute-start(bf16[16,14336]{1,0:T(8,128)(2,1)S(1)} %collective-permute-done), channel_id=1, source_target_pairs={{0,12},{4,0},{8,4},{12,8},{1,13},{5,1},{9,5},{13,9},{2,14},{6,2},{... | collective-permute-start | bytes 1376264 | tf_op jit(solution)/shard_map/hidden_gather/ppermute | solution.py:38
  42.3 16.0 %collective-permute-start.9 = (bf16[16,16,256]{2,1,0:T(8,128)(2,1)S(1)}, bf16[16,16,256]{2,1,0:T(8,128)(2,1)S(1)}, u32[]{:S(2)}, u32[]{:S(2)}) collective-permute-start(bf16[16,16,256]{2,1,0:T(8,128)(2,1)S(1)} %all-to-all-done), channel_id=1, source_target_pairs={{0,192},{64,128},{128,64},{192,0},{1,193},{65,129},{129,65},{193,1... | collective-permute-start | bytes 393224 | tf_op jit(solution)/shard_map/grad_gather/ppermute | solution.py:42
  50.8 13.6 %collective-permute-start.8 = (bf16[16,16,256]{2,1,0:T(8,128)(2,1)S(1)}, bf16[16,16,256]{2,1,0:T(8,128)(2,1)S(1)}, u32[]{:S(2)}, u32[]{:S(2)}) collective-permute-start(bf16[16,16,256]{2,1,0:T(8,128)(2,1)S(1)} %all-to-all-done), channel_id=1, source_target_pairs={{0,128},{64,192},{128,0},{192,64},{1,129},{65,193},{129,1},{193,65... | collective-permute-start | bytes 393224 | tf_op jit(solution)/shard_map/grad_gather/ppermute | solution.py:42
  58.3 7.3 %collective-permute-start.7 = (bf16[16,16,256]{2,1,0:T(8,128)(2,1)S(1)}, bf16[16,16,256]{2,1,0:T(8,128)(2,1)S(1)}, u32[]{:S(2)}, u32[]{:S(2)}) collective-permute-start(bf16[16,16,256]{2,1,0:T(8,128)(2,1)S(1)} %all-to-all-done), channel_id=1, source_target_pairs={{0,64},{64,0},{128,192},{192,128},{1,65},{65,1},{129,193},{193,129... | collective-permute-start | bytes 393224 | tf_op jit(solution)/shard_map/grad_gather/ppermute | solution.py:42
  76.7 14.1 %collective-permute-start.12 = (bf16[4,64,896]{2,1,0:T(8,128)(2,1)S(1)}, bf16[4,64,896]{2,1,0:T(8,128)(2,1)S(1)}, u32[]{:S(2)}, u32[]{:S(2)}) collective-permute-start(bf16[4,64,896]{2,1,0:T(8,128)(2,1)S(1)} %get-tuple-element.39), channel_id=1, source_target_pairs={{0,16},{16,32},{32,48},{48,0},{1,17},{17,33},{33,49},{49,1},{2,18}... | collective-permute-start | bytes 1376264 | tf_op jit(solution)/shard_map/left_reduce/ppermute | solution.py:252
  78.2 23.3 %collective-permute-start.13 = (bf16[4,64,896]{2,1,0:T(8,128)(2,1)S(1)}, bf16[4,64,896]{2,1,0:T(8,128)(2,1)S(1)}, u32[]{:S(2)}, u32[]{:S(2)}) collective-permute-start(bf16[4,64,896]{2,1,0:T(8,128)(2,1)S(1)} %get-tuple-element.40), channel_id=1, source_target_pairs={{0,32},{16,48},{32,0},{48,16},{1,33},{17,49},{33,1},{49,17},{2,34}... | collective-permute-start | bytes 1376264 | tf_op jit(solution)/shard_map/left_reduce/ppermute | solution.py:252
  81.0 20.6 %collective-permute-start.14 = (bf16[4,64,896]{2,1,0:T(8,128)(2,1)S(1)}, bf16[4,64,896]{2,1,0:T(8,128)(2,1)S(1)}, u32[]{:S(2)}, u32[]{:S(2)}) collective-permute-start(bf16[4,64,896]{2,1,0:T(8,128)(2,1)S(1)} %get-tuple-element.41), channel_id=1, source_target_pairs={{0,48},{16,0},{32,16},{48,32},{1,49},{17,1},{33,17},{49,33},{2,50}... | collective-permute-start | bytes 1376264 | tf_op jit(solution)/shard_map/left_reduce/ppermute | solution.py:252
  101.8 26.4 %collective-permute-start.19 = (bf16[4,16,16,256]{3,2,1,0:T(8,128)(2,1)S(1)}, bf16[4,16,16,256]{3,2,1,0:T(8,128)(2,1)S(1)}, u32[]{:S(2)}, u32[]{:S(2)}) collective-permute-start(bf16[4,16,16,256]{3,2,1,0:T(8,128)(2,1)S(1)} %pad_maximum_fusion.2.t0), channel_id=1, source_target_pairs={{0,16},{16,32},{32,48},{48,0},{1,17},{17,33},{33,49},{49,1},{2,18}... | collective-permute-start | bytes 1572872 | tf_op jit(solution)/shard_map/left_reduce/ppermute | solution.py:262
  103.4 24.8 %collective-permute-start.18 = (bf16[4,16,16,256]{3,2,1,0:T(8,128)(2,1)S(1)}, bf16[4,16,16,256]{3,2,1,0:T(8,128)(2,1)S(1)}, u32[]{:S(2)}, u32[]{:S(2)}) collective-permute-start(bf16[4,16,16,256]{3,2,1,0:T(8,128)(2,1)S(1)} %pad_maximum_fusion.2.t0), channel_id=1, source_target_pairs={{0,48},{16,0},{32,16},{48,32},{1,49},{17,1},{33,17},{49,33},{2,50}... | collective-permute-start | bytes 1572872 | tf_op jit(solution)/shard_map/left_reduce/ppermute | solution.py:262
  105.3 22.8 %collective-permute-start.16 = (bf16[64,896]{1,0:T(8,128)(2,1)S(1)}, bf16[64,896]{1,0:T(8,128)(2,1)S(1)}, u32[]{:S(2)}, u32[]{:S(2)}) collective-permute-start(bf16[64,896]{1,0:T(8,128)(2,1)S(1)} %get-tuple-element.44), channel_id=1, source_target_pairs={{0,128},{64,192},{128,0},{192,64},{1,129},{65,193},{129,1},{193,65... | collective-permute-start | bytes 344072 | tf_op jit(solution)/shard_map/left_reduce/ppermute | solution.py:264
  117.3 10.8 %collective-permute-start.17 = (bf16[64,896]{1,0:T(8,128)(2,1)S(1)}, bf16[64,896]{1,0:T(8,128)(2,1)S(1)}, u32[]{:S(2)}, u32[]{:S(2)}) collective-permute-start(bf16[64,896]{1,0:T(8,128)(2,1)S(1)} %get-tuple-element.45), channel_id=1, source_target_pairs={{0,192},{64,128},{128,64},{192,0},{1,193},{65,129},{129,65},{193,1... | collective-permute-start | bytes 344072 | tf_op jit(solution)/shard_map/left_reduce/ppermute | solution.py:264
  117.3 10.8 %collective-permute-start.15 = (bf16[64,896]{1,0:T(8,128)(2,1)S(1)}, bf16[64,896]{1,0:T(8,128)(2,1)S(1)}, u32[]{:S(2)}, u32[]{:S(2)}) collective-permute-start(bf16[64,896]{1,0:T(8,128)(2,1)S(1)} %get-tuple-element.43), channel_id=1, source_target_pairs={{0,64},{64,0},{128,192},{192,128},{1,65},{65,1},{129,193},{193,129... | collective-permute-start | bytes 344072 | tf_op jit(solution)/shard_map/left_reduce/ppermute | solution.py:264
  128.2 17.0 %collective-permute-start.23 = (bf16[4,16,16,256]{3,2,1,0:T(8,128)(2,1)S(1)}, bf16[4,16,16,256]{3,2,1,0:T(8,128)(2,1)S(1)}, u32[]{:S(2)}, u32[]{:S(2)}) collective-permute-start(bf16[4,16,16,256]{3,2,1,0:T(8,128)(2,1)S(1)} %pad_maximum_fusion.2.t0), channel_id=1, source_target_pairs={{0,32},{16,48},{32,0},{48,16},{1,33},{17,49},{33,1},{49,17},{2,34}... | collective-permute-start | bytes 1572872 | tf_op jit(solution)/shard_map/left_gather/ppermute | solution.py:267
  131.3 7.6 %collective-permute-start.22 = (bf16[64,896]{1,0:T(8,128)(2,1)S(1)}, bf16[64,896]{1,0:T(8,128)(2,1)S(1)}, u32[]{:S(2)}, u32[]{:S(2)}) collective-permute-start(bf16[64,896]{1,0:T(8,128)(2,1)S(1)} %multiply_convert_fusion), channel_id=1, source_target_pairs={{0,192},{64,128},{128,64},{192,0},{1,193},{65,129},{129,65},{193,1... | collective-permute-start | bytes 344072 | tf_op jit(solution)/shard_map/left_gather/ppermute | solution.py:42
  133.6 11.5 %collective-permute-start.21 = (bf16[64,896]{1,0:T(8,128)(2,1)S(1)}, bf16[64,896]{1,0:T(8,128)(2,1)S(1)}, u32[]{:S(2)}, u32[]{:S(2)}) collective-permute-start(bf16[64,896]{1,0:T(8,128)(2,1)S(1)} %multiply_convert_fusion), channel_id=1, source_target_pairs={{0,128},{64,192},{128,0},{192,64},{1,129},{65,193},{129,1},{193,65... | collective-permute-start | bytes 344072 | tf_op jit(solution)/shard_map/left_gather/ppermute | solution.py:42
  135.7 9.5 %collective-permute-start.20 = (bf16[64,896]{1,0:T(8,128)(2,1)S(1)}, bf16[64,896]{1,0:T(8,128)(2,1)S(1)}, u32[]{:S(2)}, u32[]{:S(2)}) collective-permute-start(bf16[64,896]{1,0:T(8,128)(2,1)S(1)} %multiply_convert_fusion), channel_id=1, source_target_pairs={{0,64},{64,0},{128,192},{192,128},{1,65},{65,1},{129,193},{193,129... | collective-permute-start | bytes 344072 | tf_op jit(solution)/shard_map/left_gather/ppermute | solution.py:42
  146.0 24.8 %collective-permute-start.26 = (bf16[4,64,896]{2,1,0:T(8,128)(2,1)S(1)}, bf16[4,64,896]{2,1,0:T(8,128)(2,1)}, u32[]{:S(2)}, u32[]{:S(2)}) collective-permute-start(bf16[4,64,896]{2,1,0:T(8,128)(2,1)S(1)} %pad_maximum_fusion.3.refs_0_), channel_id=1, source_target_pairs={{0,16},{16,32},{32,48},{48,0},{1,17},{17,33},{33,49},{49,1},{2,18}... | collective-permute-start | bytes 1376264 | tf_op jit(solution)/shard_map/left_gather/ppermute | solution.py:38
  146.6 24.2 %collective-permute-start.25 = (bf16[4,64,896]{2,1,0:T(8,128)(2,1)S(1)}, bf16[4,64,896]{2,1,0:T(8,128)(2,1)}, u32[]{:S(2)}, u32[]{:S(2)}) collective-permute-start(bf16[4,64,896]{2,1,0:T(8,128)(2,1)S(1)} %pad_maximum_fusion.3.refs_0_), channel_id=1, source_target_pairs={{0,32},{16,48},{32,0},{48,16},{1,33},{17,49},{33,1},{49,17},{2,34}... | collective-permute-start | bytes 1376264 | tf_op jit(solution)/shard_map/left_gather/ppermute | solution.py:38
  148.7 24.6 %collective-permute-start.24 = (bf16[4,64,896]{2,1,0:T(8,128)(2,1)S(1)}, bf16[4,64,896]{2,1,0:T(8,128)(2,1)}, u32[]{:S(2)}, u32[]{:S(2)}) collective-permute-start(bf16[4,64,896]{2,1,0:T(8,128)(2,1)S(1)} %pad_maximum_fusion.3.refs_0_), channel_id=1, source_target_pairs={{0,48},{16,0},{32,16},{48,32},{1,49},{17,1},{33,17},{49,33},{2,50}... | collective-permute-start | bytes 1376264 | tf_op jit(solution)/shard_map/left_gather/ppermute | solution.py:38
  161.9 45.0 %all-to-all-start.1 = ((bf16[16,16,896]{2,1,0:T(8,128)(2,1)}), bf16[16,16,896]{2,1,0:T(8,128)(2,1)S(1)}, u32[]{:S(2)}, u32[]{:S(2)}) async-start(bf16[16,16,896]{2,1,0:T(8,128)(2,1)} %input_grad.1), calls=%async_computation.1 | async-start | bytes 917504 | tf_op jit(solution)/shard_map/input_grad/all_to_all | solution.py:295
  179.3 6.2 %collective-permute-start.28 = (f32[64,256]{1,0:T(8,128)S(1)}, f32[64,256]{1,0:T(8,128)S(1)}, u32[]{:S(2)}, u32[]{:S(2)}) collective-permute-start(f32[64,256]{1,0:T(8,128)S(1)} %get-tuple-element.60), channel_id=1, source_target_pairs={{0,32},{16,48},{32,0},{48,16},{1,33},{17,49},{33,1},{49,17},{2,34}... | collective-permute-start | bytes 196616 | tf_op jit(solution)/shard_map/right/ppermute | solution.py:38
  186.8 9.9 %collective-permute-start.32 = (f32[64,256]{1,0:T(8,128)S(1)}, f32[64,256]{1,0:T(8,128)S(1)}, u32[]{:S(2)}, u32[]{:S(2)}) collective-permute-start(f32[64,256]{1,0:T(8,128)S(1)} %add_add_fusion.s0), channel_id=1, source_target_pairs={{0,192},{64,128},{128,64},{192,0},{1,193},{65,129},{129,65},{193,1... | collective-permute-start | bytes 196616 | tf_op jit(solution)/shard_map/right/ppermute | solution.py:42
  186.9 9.8 %collective-permute-start.31 = (f32[64,256]{1,0:T(8,128)S(1)}, f32[64,256]{1,0:T(8,128)S(1)}, u32[]{:S(2)}, u32[]{:S(2)}) collective-permute-start(f32[64,256]{1,0:T(8,128)S(1)} %add_add_fusion.s0), channel_id=1, source_target_pairs={{0,128},{64,192},{128,0},{192,64},{1,129},{65,193},{129,1},{193,65... | collective-permute-start | bytes 196616 | tf_op jit(solution)/shard_map/right/ppermute | solution.py:42
  188.7 8.1 %collective-permute-start.30 = (f32[64,256]{1,0:T(8,128)S(1)}, f32[64,256]{1,0:T(8,128)S(1)}, u32[]{:S(2)}, u32[]{:S(2)}) collective-permute-start(f32[64,256]{1,0:T(8,128)S(1)} %add_add_fusion.s0), channel_id=1, source_target_pairs={{0,64},{64,0},{128,192},{192,128},{1,65},{65,1},{129,193},{193,129... | collective-permute-start | bytes 196616 | tf_op jit(solution)/shard_map/right/ppermute | solution.py:42
  (12 other events, 45.0 us)
Sparse Core Ops, SparseCore 0:
  10.7 122.4 all-gather.2

commit v2 on v1

--- a/solution.py
+++ b/solution.py
@@ -15,7 +15,7 @@
 RANK = 64
 TOKENS = 256
 COLS = 256
-STEP = 2048
+STEP = 3584
 PART = 128
 BF = jnp.bfloat16
 F32 = jnp.float32
@@ -119,16 +119,23 @@
     local_ref[...] = sum(dot(t, grad[...], 0, 0) for t in reversed(thirds(total[:TOKENS])))
 
 
-def inverse_kernel(gram, out_ref):
+def eliminate(both, first, last):
     row_of = lax.broadcasted_iota(jnp.int32, (RANK, 1), 0)
-    eye = lax.broadcasted_iota(jnp.int32, (RANK, RANK), 0) == lax.broadcasted_iota(jnp.int32, (RANK, RANK), 1)
-    both = jnp.concatenate([gram[...], eye.astype(F32)], axis=1)
-    for k in range(RANK):
+    for k in range(first, last):
         pivot = both[k : k + 1, k : k + 1]
         factor = jnp.where(row_of > k, both[:, k : k + 1] / pivot, 0.0)
         scale = jnp.where(row_of == k, lax.rsqrt(pivot), 1.0)
         both = both * scale - factor * both[k : k + 1, :]
-    out_ref[...] = both[:, RANK:]
+    return both
+
+
+def upper_kernel(gram, out_ref):
+    eye = lax.broadcasted_iota(jnp.int32, (RANK, RANK), 0) == lax.broadcasted_iota(jnp.int32, (RANK, RANK), 1)
+    out_ref[...] = eliminate(jnp.concatenate([gram[...], eye.astype(F32)], axis=1), 0, RANK // 2)
+
+
+def lower_kernel(both, out_ref):
+    out_ref[...] = eliminate(both[...], RANK // 2, RANK)[:, RANK:]
 
 
 def error_kernel(inverse, s0, s1, s2, s3, grad, left, h0, h1, h2, h3, right_ref, out_ref, weights):
@@ -178,31 +185,31 @@
     )(inverse, *sums, grad, left, *hidden)
 
 
-def input_kernel(group, t0, t1, t2, t3, weight, out_ref):
+def input_kernel(group, shard, t0, t1, t2, t3, near, far, out_ref):
     total = jnp.zeros((TOKENS, PART), F32)
     for d in range(16):
-        rows = jnp.concatenate([t[:, d].reshape(64, COLS) for t in (t0, t1, t2, t3)], axis=0)
-        total += dot(rows, weight[d], 1, 1)
+        rows = jnp.concatenate([t[:, shard[d]].reshape(64, COLS) for t in (t0, t1, t2, t3)], axis=0)
+        total += dot(rows, near[d] if d < 8 else far[d - 8], 1, 1)
     total = total.astype(BF).reshape(16, 16, PART)
     for i in range(16):
         out_ref[group[i]] = total[i]
 
 
-def input_of(group, tokens, weight):
+def input_of(group, shard, tokens, near, far):
     return pl.pallas_call(
         input_kernel,
         out_shape=jax.ShapeDtypeStruct((16, 16, BLOCK), BF),
         grid=(BLOCK // PART,),
-        in_specs=[SMEM]
+        in_specs=[SMEM, SMEM]
         + [pl.BlockSpec(t.shape, lambda i: (0, 0, 0, 0)) for t in tokens]
-        + [pl.BlockSpec((16, PART, COLS), lambda i: (0, i, 0))],
+        + [pl.BlockSpec((8, PART, COLS), lambda i: (0, i, 0))] * 2,
         out_specs=pl.BlockSpec((16, 16, PART), lambda i: (0, 0, i)),
-        compiler_params=LIMIT,
+        compiler_params=pltpu.CompilerParams(vmem_limit_bytes=56 * 2**20),
         cost_estimate=pl.CostEstimate(
             flops=2 * TOKENS * 16 * COLS * BLOCK, bytes_accessed=10 * 2**20, transcendentals=0
         ),
         name="input_grad",
-    )(group, *tokens, weight)
+    )(group, shard, *tokens, near, far)
 
 
 def on_device(hidden_rows, out_grad, down_weight, query_init):
@@ -225,19 +232,20 @@
 
     with jax.named_scope("hidden_gather"):
         other = lax.ppermute(mine, "zh", SWAP)
-        rest = ring3(mine, "y")
-        near = jnp.concatenate([mine] + rest, axis=0)
-        far = jnp.concatenate([other] + ring3(after(other, near, a), "y"), axis=0)
-        hidden = [near, far, lax.ppermute(near, "c", SWAP)]
-
-    with jax.named_scope("weight_gather"):
-        weight = lax.all_gather(down_weight, ("y", "zh", "c"))
-
+        near = jnp.concatenate([mine] + ring3(mine, "y"), axis=0)
     with jax.named_scope("grad_gather"):
         tokens = lax.all_to_all(grad.reshape(16, 16, COLS), ("y", "zh", "c"), 0, 0)
-        tokens = jnp.stack([tokens] + flip3(tokens))
-        far, tokens = lax.optimization_barrier((far, tokens))
-        hidden = [near, far, hidden[2], lax.ppermute(far, "c", SWAP)]
+    near, other, tokens, a = lax.optimization_barrier((near, other, tokens, a))
+    with jax.named_scope("weight_gather"):
+        weight = lax.all_gather(down_weight, ("y", "c"))
+        far_weight = lax.ppermute(after(down_weight, near), "zh", SWAP)
+    with jax.named_scope("hidden_gather"):
+        far = jnp.concatenate([other] + ring3(other, "y"), axis=0)
+        cross = lax.ppermute(near, "c", SWAP)
+        far, far_weight, cross = lax.optimization_barrier((far, far_weight, cross))
+        hidden = [near, far, cross, lax.ppermute(far, "c", SWAP)]
+    with jax.named_scope("weight_gather"):
+        far_weight = lax.all_gather(far_weight, ("y", "c"))
 
     table = (((x + four) % 4)[:, None] * 4 + (zl ^ four)[None, :]).reshape(16).astype(jnp.int32)
     with jax.named_scope("left_reduce"):
@@ -250,6 +258,8 @@
             "left",
         )
         parts = [parts[0]] + [lax.ppermute(parts[r], "x", shift(r)) for r in (1, 2, 3)]
+        tokens = jnp.stack([tokens] + flip3(after(tokens, parts[0])))
+        parts, tokens = lax.optimization_barrier((parts, tokens))
         block, *sends = call(
             sum_kernel,
             [((RANK, BLOCK), F32)] + [((RANK, BLOCK), BF)] * 3,
@@ -271,7 +281,10 @@
 
     with jax.named_scope("input_grad"):
         group = ((zl ^ four)[None, :] * 4 + ((x + four) % 4)[:, None]).reshape(16).astype(jnp.int32)
-        partial = input_of(group, [after(tokens, column), token1, token2, token3], weight)
+        both = jnp.arange(8)
+        shard = [(both // 2) * 4 + h * 2 + both % 2 for h in (zh, 1 - zh)]
+        shard = jnp.concatenate(shard).astype(jnp.int32)
+        partial = input_of(group, shard, [after(tokens, column), token1, token2, token3], weight, far_weight)
         lefts, _ = lax.optimization_barrier((lefts, partial))
 
     with jax.named_scope("stats"):
@@ -284,10 +297,12 @@
             "stats",
         )
     with jax.named_scope("right"):
+        half = call(upper_kernel, [((RANK, 2 * RANK), F32)], [], [gram], 64 * 64 * 128, "inverse_upper")[0]
         for v in ring3(local, "x"):
             local = local + v
+        local, half = lax.optimization_barrier((local, half))
         sums = [local] + flip3(local)
-        inverse = call(inverse_kernel, [((RANK, RANK), F32)], [], [after(gram, local)], 64 * 64 * 128 * 2, "inverse")[0]
+        inverse = call(lower_kernel, [((RANK, RANK), F32)], [], [half], 64 * 64 * 128, "inverse_lower")[0]
     with jax.named_scope("error_new"):
         right, error_new = error_of(inverse, sums, grad_rows, left, hidden)
 

time: 215 us -> 206 us (0.958); the launches traced: 215 us -> 202 us
  waiting for transfers between devices: 65.9 us -> 60.2 us
  starting transfers between devices: 87.3 us -> 83.6 us
  local copies, waits for them, and re-layouts: 8.67 us -> 6.2 us
    ppermute x3, waiting for transfers between devices: 19.2 us -> 0.01 us  [on_device(): lax.ppermute(parts[r], 'x', shift(r))]
    ppermute x12, waiting for transfers between devices: 19.2 us -> 33.5 us  [ring3(): return [lax.ppermute(value, axis, shift(-s)) for s in (1, 2, 3)]]
    ppermute x2 -> x3, starting transfers between devices: 0.57 us -> 6.92 us  [the longest x1 6.82 us: on_device(): far_weight = lax.ppermute(after(down_weight, near), 'zh', SWAP)]
    ppermute x3, starting transfers between devices: 12.5 us -> 6.84 us  [on_device(): block = block + lax.ppermute(sends[s - 1], 'zl', flip(s)).astype(F32)]
    ppermute x9, starting transfers between devices: 28.6 us -> 23.1 us  [flip3(): return [lax.ppermute(value, 'zl', flip(s)) for s in (1, 2, 3)]]
    ppermute x3, waiting for transfers between devices: 10.3 us -> 7.03 us  [on_device(): block = block + lax.ppermute(sends[s - 1], 'zl', flip(s)).astype(F32)]
    unnamed x16 -> x10, local copies, waits for them, and re-layouts: 8.5 us -> 5.52 us
    all_to_all x1, starting transfers between devices: 4.58 us -> 7.1 us  [on_device(): summed = lax.all_to_all(partial, ('zl', 'x'), 0, 0)]
  transfers between devices with their start and end apart: 36 -> 38, of which waited for: 17 -> 19; matrix products, arithmetic and copies ran while one was open for 2% -> 3% of each run, Pallas kernels for 15% -> 16%
where the time goes in v2:
time: 206 us; the launch traced here: 202 us
  starting transfers between devices  83.6 us (41%)
  waiting for transfers between devices  60.2 us (29%)
  Pallas kernels  33.4 us (16%)
  between operations  14.2 us (7%)
  local copies, waits for them, and re-layouts  6.2 us (3%)
  other arithmetic  4.57 us (2%)
    ppermute x12, waiting for transfers between devices, ring3(): return [lax.ppermute(value, axis, shift(-s)) for s in (1, 2, 3)]  33.5 us
    ppermute x9, starting transfers between devices, flip3(): return [lax.ppermute(value, 'zl', flip(s)) for s in (1, 2, 3)]  23.1 us
    ppermute x12, starting transfers between devices, ring3(): return [lax.ppermute(value, axis, shift(-s)) for s in (1, 2, 3)]  17 us
    pallas_call x7, Pallas kernels, call(): pl.pallas_call(kernel, out_shape=[jax.ShapeDtypeStruct(s, d) for s, d in...  15.8 us
    ppermute x9, waiting for transfers between devices, flip3(): return [lax.ppermute(value, 'zl', flip(s)) for s in (1, 2, 3)]  15 us
    pallas_call x1, Pallas kernels, input_of(): pl.pallas_call(input_kernel, out_shape=jax.ShapeDtypeStruct((16, 16, BLOC...  9.13 us
    pallas_call x1, Pallas kernels, error_of(): pl.pallas_call(error_kernel, out_shape=(jax.ShapeDtypeStruct((RANK, COLS)...  8.44 us
    all_to_all x1, starting transfers between devices, on_device(): summed = lax.all_to_all(partial, ('zl', 'x'), 0, 0)  7.1 us
  transfers between devices with their start and end apart: 38, of which 19 were waited for; matrix products, arithmetic and copies ran while one was open for 3% of the time, Pallas kernels for 16%

profile of v2, /device:TPU:16, one launch (start us, length us, event | category | flops | bytes accessed | tf_op | source)
XLA Modules:
  0.0 202.2 jit_solution(7293759118400206622)
XLA Ops:
  10.1 2.5 %collective-permute-start = (bf16[16,14336]{1,0:T(8,128)(2,1)}, bf16[16,14336]{1,0:T(8,128)(2,1)}, u32[]{:S(2)}, u32[]{:S(2)}) collective-permute-start(bf16[16,14336]{1,0:T(8,128)(2,1)} %bitcast.21), channel_id=1, source_target_pairs={{0,12},{4,0},{8,4},{12,8},{1,13},{5,1},{9,5},{13,9},{2,14},{6,2},{... | collective-permute-start | bytes 1376264 | tf_op jit(solution)/shard_map/hidden_gather/ppermute | solution.py:38
  12.7 5.5 %collective-permute-start.3 = (bf16[16,14336]{1,0:T(8,128)(2,1)}, bf16[16,14336]{1,0:T(8,128)(2,1)S(1)}, u32[]{:S(2)}, u32[]{:S(2)}) collective-permute-start(bf16[16,14336]{1,0:T(8,128)(2,1)} %bitcast.22), channel_id=1, source_target_pairs={{0,2},{2,0},{1,3},{3,1},{4,6},{6,4},{5,7},{7,5},{8,10},{10,8},{9,1... | collective-permute-start | bytes 1376264 | tf_op jit(solution)/shard_map/hidden_gather/ppermute | solution.py:234
  18.1 6.5 %all-to-all-start = ((bf16[16,16,256]{2,1,0:T(8,128)(2,1)}), bf16[16,16,256]{2,1,0:T(8,128)(2,1)S(1)}, u32[]{:S(2)}, u32[]{:S(2)}) async-start(bf16[16,16,256]{2,1,0:T(8,128)(2,1)} %bitcast.14), calls=%async_computation | async-start | bytes 262144 | tf_op jit(solution)/shard_map/grad_gather/all_to_all | solution.py:237
  27.4 8.8 %collective-permute-done.1 = bf16[16,14336]{1,0:T(8,128)(2,1)S(1)} collective-permute-done((bf16[16,14336]{1,0:T(8,128)(2,1)}, bf16[16,14336]{1,0:T(8,128)(2,1)S(1)}, u32[]{:S(2)}, u32[]{:S(2)}) %collective-permute-start.1) | collective-permute-done | bytes 458784 | tf_op jit(solution)/shard_map/hidden_gather/ppermute | solution.py:38
  36.2 3.0 %collective-permute-done = bf16[16,14336]{1,0:T(8,128)(2,1)} collective-permute-done((bf16[16,14336]{1,0:T(8,128)(2,1)}, bf16[16,14336]{1,0:T(8,128)(2,1)}, u32[]{:S(2)}, u32[]{:S(2)}) %collective-permute-start) | collective-permute-done | bytes 458784 | tf_op jit(solution)/shard_map/hidden_gather/ppermute | solution.py:38
  42.5 2.5 %collective-permute-start.4 = (bf16[16,14336]{1,0:T(8,128)(2,1)S(1)}, bf16[16,14336]{1,0:T(8,128)(2,1)S(1)}, u32[]{:S(2)}, u32[]{:S(2)}) collective-permute-start(bf16[16,14336]{1,0:T(8,128)(2,1)S(1)} %collective-permute-done.3), channel_id=1, source_target_pairs={{0,12},{4,0},{8,4},{12,8},{1,13},{5,1},{9,5},{13,9},{2,14},{6,2},{... | collective-permute-start | bytes 1376264 | tf_op jit(solution)/shard_map/hidden_gather/ppermute | solution.py:38
  45.1 6.8 %collective-permute-start.7 = (bf16[896,256]{1,0:T(8,128)(2,1)}, bf16[896,256]{1,0:T(8,128)(2,1)S(1)}, u32[]{:S(2)}, u32[]{:S(2)}) collective-permute-start(bf16[896,256]{1,0:T(8,128)(2,1)} %param.6), channel_id=1, source_target_pairs={{0,2},{2,0},{1,3},{3,1},{4,6},{6,4},{5,7},{7,5},{8,10},{10,8},{9,1... | collective-permute-start | bytes 1376264 | tf_op jit(solution)/shard_map/weight_gather/ppermute | solution.py:241
  51.9 4.3 %collective-permute-done.6 = bf16[16,14336]{1,0:T(8,128)(2,1)S(1)} collective-permute-done((bf16[16,14336]{1,0:T(8,128)(2,1)S(1)}, bf16[16,14336]{1,0:T(8,128)(2,1)S(1)}, u32[]{:S(2)}, u32[]{:S(2)}) %collective-permute-start.6) | collective-permute-done | bytes 458784 | tf_op jit(solution)/shard_map/hidden_gather/ppermute | solution.py:38
  56.3 10.2 %collective-permute-done.5 = bf16[16,14336]{1,0:T(8,128)(2,1)S(1)} collective-permute-done((bf16[16,14336]{1,0:T(8,128)(2,1)S(1)}, bf16[16,14336]{1,0:T(8,128)(2,1)S(1)}, u32[]{:S(2)}, u32[]{:S(2)}) %collective-permute-start.5) | collective-permute-done | bytes 458784 | tf_op jit(solution)/shard_map/hidden_gather/ppermute | solution.py:38
  70.4 3.9 %collective-permute-done.9.refs_3_.refs_7_.h3 = bf16[64,14336]{1,0:T(8,128)(2,1)} collective-permute-done((bf16[64,14336]{1,0:T(8,128)(2,1)}, bf16[64,14336]{1,0:T(8,128)(2,1)}, u32[]{:S(2)}, u32[]{:S(2)}) %collective-permute-start.9) | collective-permute-done | bytes 1835040 | tf_op jit(solution)/shard_map/hidden_gather/ppermute | solution.py:246
  75.8 3.4 %left.1 = (bf16[4,64,896]{2,1,0:T(8,128)(2,1)S(1)}, bf16[4,64,896]{2,1,0:T(8,128)(2,1)S(1)}, bf16[4,64,896]{2,1,0:T(8,128)(2,1)S(1)}, bf16[4,64,896]{2,1,0:T(8,128)(2,1)S(1)}) custom-call(s32[16]{0:T(128)S(1)} %add.174.table, bf16[128,256]{1,0:T(8,128)(2,1)S(1)} %get-tuple-element.47.a_ref, bf16[64,14336]{1,0:T(8,128)(2,1)S(1)} %pad_maximum_fusion.refs_0_.refs_4_.h0, ...), custom_call_target="tpu_custom_call" | custom-call | flops 939524096 | bytes 7405568 | tf_op jit(solution)/shard_map/left_reduce/left/pallas_call | solution.py:63
  80.7 2.7 %collective-permute-start.11 = (bf16[4,64,896]{2,1,0:T(8,128)(2,1)S(1)}, bf16[4,64,896]{2,1,0:T(8,128)(2,1)S(1)}, u32[]{:S(2)}, u32[]{:S(2)}) collective-permute-start(bf16[4,64,896]{2,1,0:T(8,128)(2,1)S(1)} %get-tuple-element.55), channel_id=1, source_target_pairs={{0,32},{16,48},{32,0},{48,16},{1,33},{17,49},{33,1},{49,17},{2,34}... | collective-permute-start | bytes 1376264 | tf_op jit(solution)/shard_map/left_reduce/ppermute | solution.py:260
  84.9 4.6 %collective-permute-start.15 = (bf16[16,16,256]{2,1,0:T(8,128)(2,1)S(1)}, bf16[16,16,256]{2,1,0:T(8,128)(2,1)S(1)}, u32[]{:S(2)}, u32[]{:S(2)}) collective-permute-start(bf16[16,16,256]{2,1,0:T(8,128)(2,1)S(1)} %all-to-all-done), channel_id=1, source_target_pairs={{0,192},{64,128},{128,64},{192,0},{1,193},{65,129},{129,65},{193,1... | collective-permute-start | bytes 393224 | tf_op jit(solution)/shard_map/left_reduce/ppermute | solution.py:42
  89.5 2.1 %collective-permute-start.14 = (bf16[16,16,256]{2,1,0:T(8,128)(2,1)S(1)}, bf16[16,16,256]{2,1,0:T(8,128)(2,1)S(1)}, u32[]{:S(2)}, u32[]{:S(2)}) collective-permute-start(bf16[16,16,256]{2,1,0:T(8,128)(2,1)S(1)} %all-to-all-done), channel_id=1, source_target_pairs={{0,128},{64,192},{128,0},{192,64},{1,129},{65,193},{129,1},{193,65... | collective-permute-start | bytes 393224 | tf_op jit(solution)/shard_map/left_reduce/ppermute | solution.py:42
  93.3 6.1 %collective-permute-start.13 = (bf16[16,16,256]{2,1,0:T(8,128)(2,1)S(1)}, bf16[16,16,256]{2,1,0:T(8,128)(2,1)S(1)}, u32[]{:S(2)}, u32[]{:S(2)}) collective-permute-start(bf16[16,16,256]{2,1,0:T(8,128)(2,1)S(1)} %all-to-all-done), channel_id=1, source_target_pairs={{0,64},{64,0},{128,192},{192,128},{1,65},{65,1},{129,193},{193,129... | collective-permute-start | bytes 393224 | tf_op jit(solution)/shard_map/left_reduce/ppermute | solution.py:42
  101.0 2.7 %collective-permute-done.13 = bf16[16,16,256]{2,1,0:T(8,128)(2,1)S(1)} collective-permute-done((bf16[16,16,256]{2,1,0:T(8,128)(2,1)S(1)}, bf16[16,16,256]{2,1,0:T(8,128)(2,1)S(1)}, u32[]{:S(2)}, u32[]{:S(2)}) %collective-permute-start.13) | collective-permute-done | bytes 131104 | tf_op jit(solution)/shard_map/left_reduce/ppermute | solution.py:42
  105.5 2.6 %collective-permute-start.19 = (bf16[4,16,16,256]{3,2,1,0:T(8,128)(2,1)}, bf16[4,16,16,256]{3,2,1,0:T(8,128)(2,1)}, u32[]{:S(2)}, u32[]{:S(2)}) collective-permute-start(bf16[4,16,16,256]{3,2,1,0:T(8,128)(2,1)} %pad_maximum_fusion.2.t0), channel_id=1, source_target_pairs={{0,48},{16,0},{32,16},{48,32},{1,49},{17,1},{33,17},{49,33},{2,50}... | collective-permute-start | bytes 1572872 | tf_op jit(solution)/shard_map/left_reduce/ppermute | solution.py:272
  108.1 5.2 %collective-permute-start.17 = (bf16[64,896]{1,0:T(8,128)(2,1)S(1)}, bf16[64,896]{1,0:T(8,128)(2,1)S(1)}, u32[]{:S(2)}, u32[]{:S(2)}) collective-permute-start(bf16[64,896]{1,0:T(8,128)(2,1)S(1)} %get-tuple-element.66), channel_id=1, source_target_pairs={{0,128},{64,192},{128,0},{192,64},{1,129},{65,193},{129,1},{193,65... | collective-permute-start | bytes 344072 | tf_op jit(solution)/shard_map/left_reduce/ppermute | solution.py:274
  115.0 6.7 %collective-permute-done.17 = bf16[64,896]{1,0:T(8,128)(2,1)S(1)} collective-permute-done((bf16[64,896]{1,0:T(8,128)(2,1)S(1)}, bf16[64,896]{1,0:T(8,128)(2,1)S(1)}, u32[]{:S(2)}, u32[]{:S(2)}) %collective-permute-start.17) | collective-permute-done | bytes 114720 | tf_op jit(solution)/shard_map/left_reduce/ppermute | solution.py:274
  123.6 2.8 %collective-permute-start.23 = (bf16[64,896]{1,0:T(8,128)(2,1)S(1)}, bf16[64,896]{1,0:T(8,128)(2,1)S(1)}, u32[]{:S(2)}, u32[]{:S(2)}) collective-permute-start(bf16[64,896]{1,0:T(8,128)(2,1)S(1)} %multiply_convert_fusion), channel_id=1, source_target_pairs={{0,192},{64,128},{128,64},{192,0},{1,193},{65,129},{129,65},{193,1... | collective-permute-start | bytes 344072 | tf_op jit(solution)/shard_map/left_gather/ppermute | solution.py:42
  126.4 2.1 %collective-permute-start.22 = (bf16[64,896]{1,0:T(8,128)(2,1)S(1)}, bf16[64,896]{1,0:T(8,128)(2,1)S(1)}, u32[]{:S(2)}, u32[]{:S(2)}) collective-permute-start(bf16[64,896]{1,0:T(8,128)(2,1)S(1)} %multiply_convert_fusion), channel_id=1, source_target_pairs={{0,128},{64,192},{128,0},{192,64},{1,129},{65,193},{129,1},{193,65... | collective-permute-start | bytes 344072 | tf_op jit(solution)/shard_map/left_gather/ppermute | solution.py:42
  131.0 5.2 %collective-permute-done.22 = bf16[64,896]{1,0:T(8,128)(2,1)S(1)} collective-permute-done((bf16[64,896]{1,0:T(8,128)(2,1)S(1)}, bf16[64,896]{1,0:T(8,128)(2,1)S(1)}, u32[]{:S(2)}, u32[]{:S(2)}) %collective-permute-start.22) | collective-permute-done | bytes 114720 | tf_op jit(solution)/shard_map/left_gather/ppermute | solution.py:42
  137.3 2.1 %collective-permute-start.26 = (bf16[4,64,896]{2,1,0:T(8,128)(2,1)S(1)}, bf16[4,64,896]{2,1,0:T(8,128)(2,1)}, u32[]{:S(2)}, u32[]{:S(2)}) collective-permute-start(bf16[4,64,896]{2,1,0:T(8,128)(2,1)S(1)} %pad_maximum_fusion.3.refs_0_), channel_id=1, source_target_pairs={{0,32},{16,48},{32,0},{48,16},{1,33},{17,49},{33,1},{49,17},{2,34}... | collective-permute-start | bytes 1376264 | tf_op jit(solution)/shard_map/left_gather/ppermute | solution.py:38
  140.7 9.1 %input_grad.1 = bf16[16,16,896]{2,1,0:T(8,128)(2,1)} custom-call(s32[16]{0:T(128)} %add.163.group, s32[16]{0:T(128)} %pad_add_fusion.shard, bf16[4,16,16,256]{3,2,1,0:T(8,128)(2,1)} %pad_maximum_fusion.2.t0, bf16[4,16,16,256]{3,2,1,0:T(8,128)(2,1)} %collective-permute-done.19.t1, bf16[4,16,16,256]{3,2,1,0:T(8,128)(2,1)} %collective-permute-done.24.t2, ...), custom_call_target="tpu_custom_call" | custom-call | flops 1879048192 | bytes 10485760 | tf_op jit(solution)/shard_map/input_grad/input_grad/pallas_call | solution.py:199
  149.8 7.1 %all-to-all-start.1 = ((bf16[16,16,896]{2,1,0:T(8,128)(2,1)}), bf16[16,16,896]{2,1,0:T(8,128)(2,1)S(1)}, u32[]{:S(2)}, u32[]{:S(2)}) async-start(bf16[16,16,896]{2,1,0:T(8,128)(2,1)} %input_grad.1), calls=%async_computation.1 | async-start | bytes 917504 | tf_op jit(solution)/shard_map/input_grad/all_to_all | solution.py:310
  156.9 2.1 %collective-permute-done.27.refs_3_ = bf16[4,64,896]{2,1,0:T(8,128)(2,1)S(1)} collective-permute-done((bf16[4,64,896]{2,1,0:T(8,128)(2,1)S(1)}, bf16[4,64,896]{2,1,0:T(8,128)(2,1)S(1)}, u32[]{:S(2)}, u32[]{:S(2)}) %collective-permute-start.27) | collective-permute-done | bytes 458784 | tf_op jit(solution)/shard_map/left_gather/ppermute | solution.py:38
  162.6 5.2 %stats.1 = (bf16[64,14336]{1,0:T(8,128)(2,1)S(1)}, f32[64,256]{1,0:T(8,128)S(1)}, f32[64,64]{1,0:T(8,128)S(1)}) custom-call(s32[16]{0:T(128)S(1)} %add.174.table, bf16[4,64,896]{2,1,0:T(8,128)(2,1)S(1)} %pad_maximum_fusion.3.refs_0_, bf16[4,64,896]{2,1,0:T(8,128)(2,1)} %collective-permute-done.25.refs_1_, ...), custom_call_target="tpu_custom_call" | custom-call | flops 587202560 | bytes 9306112 | tf_op jit(solution)/shard_map/stats/stats/pallas_call | solution.py:63
  167.9 3.9 %collective-permute-start.29 = (f32[64,256]{1,0:T(8,128)S(1)}, f32[64,256]{1,0:T(8,128)S(1)}, u32[]{:S(2)}, u32[]{:S(2)}) collective-permute-start(f32[64,256]{1,0:T(8,128)S(1)} %get-tuple-element.82), channel_id=1, source_target_pairs={{0,32},{16,48},{32,0},{48,16},{1,33},{17,49},{33,1},{49,17},{2,34}... | collective-permute-start | bytes 196616 | tf_op jit(solution)/shard_map/right/ppermute | solution.py:38
  171.8 2.7 %inverse_upper.1.both = f32[64,128]{1,0:T(8,128)S(1)} custom-call(f32[64,64]{1,0:T(8,128)S(1)} %get-tuple-element.83.gram), custom_call_target="tpu_custom_call" | custom-call | flops 524288 | bytes 16384 | tf_op jit(solution)/shard_map/right/inverse_upper/pallas_call | solution.py:63
  176.1 4.7 %collective-permute-start.33 = (f32[64,256]{1,0:T(8,128)S(1)}, f32[64,256]{1,0:T(8,128)S(1)}, u32[]{:S(2)}, u32[]{:S(2)}) collective-permute-start(f32[64,256]{1,0:T(8,128)S(1)} %add_add_fusion.s0), channel_id=1, source_target_pairs={{0,192},{64,128},{128,64},{192,0},{1,193},{65,129},{129,65},{193,1... | collective-permute-start | bytes 196616 | tf_op jit(solution)/shard_map/right/ppermute | solution.py:42
  181.4 2.7 %inverse_lower.1.inverse = f32[64,64]{1,0:T(8,128)S(1)} custom-call(f32[64,128]{1,0:T(8,128)S(1)} %inverse_upper.1.both), custom_call_target="tpu_custom_call" | custom-call | flops 524288 | bytes 32768 | tf_op jit(solution)/shard_map/right/inverse_lower/pallas_call | solution.py:63
  186.1 8.4 %error_new.1 = (f32[64,256]{1,0:T(8,128)}, bf16[14336,256]{1,0:T(8,128)(2,1)}) custom-call(f32[64,64]{1,0:T(8,128)S(1)} %inverse_lower.1.inverse, f32[64,256]{1,0:T(8,128)S(1)} %add_add_fusion.s0, f32[64,256]{1,0:T(8,128)S(1)} %collective-permute-done.31.s1, f32[64,256]{1,0:T(8,128)S(1)} %collective-permute-done.32.s2, ...), custom_call_target="tpu_custom_call" | custom-call | flops 2818572288 | bytes 16515072 | tf_op jit(solution)/shard_map/error_new/error_new/pallas_call | solution.py:168
  (82 shorter events, 39.4 us)
Async XLA Ops:
  7.2 133.5 %all-gather.5.cloned.1.call-start = ((), (), s32[]{:S(2)}) async-start(), calls=%async_computation.2 | async-start | bytes 4128768 | tf_op jit(solution)/shard_map/weight_gather/all_gather | solution.py:240
  7.9 19.5 %collective-permute-start.2 = (bf16[16,14336]{1,0:T(8,128)(2,1)}, bf16[16,14336]{1,0:T(8,128)(2,1)S(1)}, u32[]{:S(2)}, u32[]{:S(2)}) collective-permute-start(bf16[16,14336]{1,0:T(8,128)(2,1)} %bitcast.19), channel_id=1, source_target_pairs={{0,4},{4,8},{8,12},{12,0},{1,5},{5,9},{9,13},{13,1},{2,6},{6,10},{... | collective-permute-start | bytes 1376264 | tf_op jit(solution)/shard_map/hidden_gather/ppermute | solution.py:38
  9.3 27.0 %collective-permute-start.1 = (bf16[16,14336]{1,0:T(8,128)(2,1)}, bf16[16,14336]{1,0:T(8,128)(2,1)S(1)}, u32[]{:S(2)}, u32[]{:S(2)}) collective-permute-start(bf16[16,14336]{1,0:T(8,128)(2,1)} %bitcast.20), channel_id=1, source_target_pairs={{0,8},{4,12},{8,0},{12,4},{1,9},{5,13},{9,1},{13,5},{2,10},{6,14},... | collective-permute-start | bytes 1376264 | tf_op jit(solution)/shard_map/hidden_gather/ppermute | solution.py:38
  10.1 29.1 %collective-permute-start = (bf16[16,14336]{1,0:T(8,128)(2,1)}, bf16[16,14336]{1,0:T(8,128)(2,1)}, u32[]{:S(2)}, u32[]{:S(2)}) collective-permute-start(bf16[16,14336]{1,0:T(8,128)(2,1)} %bitcast.21), channel_id=1, source_target_pairs={{0,12},{4,0},{8,4},{12,8},{1,13},{5,1},{9,5},{13,9},{2,14},{6,2},{... | collective-permute-start | bytes 1376264 | tf_op jit(solution)/shard_map/hidden_gather/ppermute | solution.py:38
  12.7 27.8 %collective-permute-start.3 = (bf16[16,14336]{1,0:T(8,128)(2,1)}, bf16[16,14336]{1,0:T(8,128)(2,1)S(1)}, u32[]{:S(2)}, u32[]{:S(2)}) collective-permute-start(bf16[16,14336]{1,0:T(8,128)(2,1)} %bitcast.22), channel_id=1, source_target_pairs={{0,2},{2,0},{1,3},{3,1},{4,6},{6,4},{5,7},{7,5},{8,10},{10,8},{9,1... | collective-permute-start | bytes 1376264 | tf_op jit(solution)/shard_map/hidden_gather/ppermute | solution.py:234
  18.1 22.4 %all-to-all-start = ((bf16[16,16,256]{2,1,0:T(8,128)(2,1)}), bf16[16,16,256]{2,1,0:T(8,128)(2,1)S(1)}, u32[]{:S(2)}, u32[]{:S(2)}) async-start(bf16[16,16,256]{2,1,0:T(8,128)(2,1)} %bitcast.14), calls=%async_computation | async-start | bytes 262144 | tf_op jit(solution)/shard_map/grad_gather/all_to_all | solution.py:237
  24.7 116.0 %all-gather.7.cloned.1.call-start = ((), (), s32[]{:S(2)}) async-start(), calls=%async_computation.3 | async-start | bytes 4128768 | tf_op jit(solution)/shard_map/weight_gather/all_gather | solution.py:248
  40.5 15.8 %collective-permute-start.6 = (bf16[16,14336]{1,0:T(8,128)(2,1)S(1)}, bf16[16,14336]{1,0:T(8,128)(2,1)S(1)}, u32[]{:S(2)}, u32[]{:S(2)}) collective-permute-start(bf16[16,14336]{1,0:T(8,128)(2,1)S(1)} %collective-permute-done.3), channel_id=1, source_target_pairs={{0,4},{4,8},{8,12},{12,0},{1,5},{5,9},{9,13},{13,1},{2,6},{6,10},{... | collective-permute-start | bytes 1376264 | tf_op jit(solution)/shard_map/hidden_gather/ppermute | solution.py:38
  41.8 24.7 %collective-permute-start.5 = (bf16[16,14336]{1,0:T(8,128)(2,1)S(1)}, bf16[16,14336]{1,0:T(8,128)(2,1)S(1)}, u32[]{:S(2)}, u32[]{:S(2)}) collective-permute-start(bf16[16,14336]{1,0:T(8,128)(2,1)S(1)} %collective-permute-done.3), channel_id=1, source_target_pairs={{0,8},{4,12},{8,0},{12,4},{1,9},{5,13},{9,1},{13,5},{2,10},{6,14},... | collective-permute-start | bytes 1376264 | tf_op jit(solution)/shard_map/hidden_gather/ppermute | solution.py:38
  42.5 25.4 %collective-permute-start.4 = (bf16[16,14336]{1,0:T(8,128)(2,1)S(1)}, bf16[16,14336]{1,0:T(8,128)(2,1)S(1)}, u32[]{:S(2)}, u32[]{:S(2)}) collective-permute-start(bf16[16,14336]{1,0:T(8,128)(2,1)S(1)} %collective-permute-done.3), channel_id=1, source_target_pairs={{0,12},{4,0},{8,4},{12,8},{1,13},{5,1},{9,5},{13,9},{2,14},{6,2},{... | collective-permute-start | bytes 1376264 | tf_op jit(solution)/shard_map/hidden_gather/ppermute | solution.py:38
  45.1 24.2 %collective-permute-start.8 = (bf16[64,14336]{1,0:T(8,128)(2,1)S(1)}, bf16[64,14336]{1,0:T(8,128)(2,1)}, u32[]{:S(2)}, u32[]{:S(2)}) collective-permute-start(bf16[64,14336]{1,0:T(8,128)(2,1)S(1)} %pad_maximum_fusion.refs_0_.refs_4_.h0), channel_id=1, source_target_pairs={{0,1},{1,0},{2,3},{3,2},{4,5},{5,4},{6,7},{7,6},{8,9},{9,8},{10,11... | collective-permute-start | bytes 5505032 | tf_op jit(solution)/shard_map/hidden_gather/ppermute | solution.py:244
  45.1 24.2 %collective-permute-start.7 = (bf16[896,256]{1,0:T(8,128)(2,1)}, bf16[896,256]{1,0:T(8,128)(2,1)S(1)}, u32[]{:S(2)}, u32[]{:S(2)}) collective-permute-start(bf16[896,256]{1,0:T(8,128)(2,1)} %param.6), channel_id=1, source_target_pairs={{0,2},{2,0},{1,3},{3,1},{4,6},{6,4},{5,7},{7,5},{8,10},{10,8},{9,1... | collective-permute-start | bytes 1376264 | tf_op jit(solution)/shard_map/weight_gather/ppermute | solution.py:241
  79.2 25.4 %collective-permute-start.10 = (bf16[4,64,896]{2,1,0:T(8,128)(2,1)S(1)}, bf16[4,64,896]{2,1,0:T(8,128)(2,1)S(1)}, u32[]{:S(2)}, u32[]{:S(2)}) collective-permute-start(bf16[4,64,896]{2,1,0:T(8,128)(2,1)S(1)} %get-tuple-element.54), channel_id=1, source_target_pairs={{0,16},{16,32},{32,48},{48,0},{1,17},{17,33},{33,49},{49,1},{2,18}... | collective-permute-start | bytes 1376264 | tf_op jit(solution)/shard_map/left_reduce/ppermute | solution.py:260
  80.7 23.8 %collective-permute-start.11 = (bf16[4,64,896]{2,1,0:T(8,128)(2,1)S(1)}, bf16[4,64,896]{2,1,0:T(8,128)(2,1)S(1)}, u32[]{:S(2)}, u32[]{:S(2)}) collective-permute-start(bf16[4,64,896]{2,1,0:T(8,128)(2,1)S(1)} %get-tuple-element.55), channel_id=1, source_target_pairs={{0,32},{16,48},{32,0},{48,16},{1,33},{17,49},{33,1},{49,17},{2,34}... | collective-permute-start | bytes 1376264 | tf_op jit(solution)/shard_map/left_reduce/ppermute | solution.py:260
  83.5 21.1 %collective-permute-start.12 = (bf16[4,64,896]{2,1,0:T(8,128)(2,1)S(1)}, bf16[4,64,896]{2,1,0:T(8,128)(2,1)S(1)}, u32[]{:S(2)}, u32[]{:S(2)}) collective-permute-start(bf16[4,64,896]{2,1,0:T(8,128)(2,1)S(1)} %get-tuple-element.56), channel_id=1, source_target_pairs={{0,48},{16,0},{32,16},{48,32},{1,49},{17,1},{33,17},{49,33},{2,50}... | collective-permute-start | bytes 1376264 | tf_op jit(solution)/shard_map/left_reduce/ppermute | solution.py:260
  84.9 8.4 %collective-permute-start.15 = (bf16[16,16,256]{2,1,0:T(8,128)(2,1)S(1)}, bf16[16,16,256]{2,1,0:T(8,128)(2,1)S(1)}, u32[]{:S(2)}, u32[]{:S(2)}) collective-permute-start(bf16[16,16,256]{2,1,0:T(8,128)(2,1)S(1)} %all-to-all-done), channel_id=1, source_target_pairs={{0,192},{64,128},{128,64},{192,0},{1,193},{65,129},{129,65},{193,1... | collective-permute-start | bytes 393224 | tf_op jit(solution)/shard_map/left_reduce/ppermute | solution.py:42
  89.5 11.5 %collective-permute-start.14 = (bf16[16,16,256]{2,1,0:T(8,128)(2,1)S(1)}, bf16[16,16,256]{2,1,0:T(8,128)(2,1)S(1)}, u32[]{:S(2)}, u32[]{:S(2)}) collective-permute-start(bf16[16,16,256]{2,1,0:T(8,128)(2,1)S(1)} %all-to-all-done), channel_id=1, source_target_pairs={{0,128},{64,192},{128,0},{192,64},{1,129},{65,193},{129,1},{193,65... | collective-permute-start | bytes 393224 | tf_op jit(solution)/shard_map/left_reduce/ppermute | solution.py:42
  93.3 10.5 %collective-permute-start.13 = (bf16[16,16,256]{2,1,0:T(8,128)(2,1)S(1)}, bf16[16,16,256]{2,1,0:T(8,128)(2,1)S(1)}, u32[]{:S(2)}, u32[]{:S(2)}) collective-permute-start(bf16[16,16,256]{2,1,0:T(8,128)(2,1)S(1)} %all-to-all-done), channel_id=1, source_target_pairs={{0,64},{64,0},{128,192},{192,128},{1,65},{65,1},{129,193},{193,129... | collective-permute-start | bytes 393224 | tf_op jit(solution)/shard_map/left_reduce/ppermute | solution.py:42
  104.8 17.3 %collective-permute-start.20 = (bf16[4,16,16,256]{3,2,1,0:T(8,128)(2,1)}, bf16[4,16,16,256]{3,2,1,0:T(8,128)(2,1)}, u32[]{:S(2)}, u32[]{:S(2)}) collective-permute-start(bf16[4,16,16,256]{3,2,1,0:T(8,128)(2,1)} %pad_maximum_fusion.2.t0), channel_id=1, source_target_pairs={{0,16},{16,32},{32,48},{48,0},{1,17},{17,33},{33,49},{49,1},{2,18}... | collective-permute-start | bytes 1572872 | tf_op jit(solution)/shard_map/left_reduce/ppermute | solution.py:272
  105.5 16.6 %collective-permute-start.19 = (bf16[4,16,16,256]{3,2,1,0:T(8,128)(2,1)}, bf16[4,16,16,256]{3,2,1,0:T(8,128)(2,1)}, u32[]{:S(2)}, u32[]{:S(2)}) collective-permute-start(bf16[4,16,16,256]{3,2,1,0:T(8,128)(2,1)} %pad_maximum_fusion.2.t0), channel_id=1, source_target_pairs={{0,48},{16,0},{32,16},{48,32},{1,49},{17,1},{33,17},{49,33},{2,50}... | collective-permute-start | bytes 1572872 | tf_op jit(solution)/shard_map/left_reduce/ppermute | solution.py:272
  108.1 13.6 %collective-permute-start.17 = (bf16[64,896]{1,0:T(8,128)(2,1)S(1)}, bf16[64,896]{1,0:T(8,128)(2,1)S(1)}, u32[]{:S(2)}, u32[]{:S(2)}) collective-permute-start(bf16[64,896]{1,0:T(8,128)(2,1)S(1)} %get-tuple-element.66), channel_id=1, source_target_pairs={{0,128},{64,192},{128,0},{192,64},{1,129},{65,193},{129,1},{193,65... | collective-permute-start | bytes 344072 | tf_op jit(solution)/shard_map/left_reduce/ppermute | solution.py:274
  113.3 8.3 %collective-permute-start.18 = (bf16[64,896]{1,0:T(8,128)(2,1)S(1)}, bf16[64,896]{1,0:T(8,128)(2,1)S(1)}, u32[]{:S(2)}, u32[]{:S(2)}) collective-permute-start(bf16[64,896]{1,0:T(8,128)(2,1)S(1)} %get-tuple-element.67), channel_id=1, source_target_pairs={{0,192},{64,128},{128,64},{192,0},{1,193},{65,129},{129,65},{193,1... | collective-permute-start | bytes 344072 | tf_op jit(solution)/shard_map/left_reduce/ppermute | solution.py:274
  115.0 7.0 %collective-permute-start.16 = (bf16[64,896]{1,0:T(8,128)(2,1)S(1)}, bf16[64,896]{1,0:T(8,128)(2,1)S(1)}, u32[]{:S(2)}, u32[]{:S(2)}) collective-permute-start(bf16[64,896]{1,0:T(8,128)(2,1)S(1)} %get-tuple-element.65), channel_id=1, source_target_pairs={{0,64},{64,0},{128,192},{192,128},{1,65},{65,1},{129,193},{193,129... | collective-permute-start | bytes 344072 | tf_op jit(solution)/shard_map/left_reduce/ppermute | solution.py:274
  122.1 14.2 %collective-permute-start.24 = (bf16[4,16,16,256]{3,2,1,0:T(8,128)(2,1)}, bf16[4,16,16,256]{3,2,1,0:T(8,128)(2,1)}, u32[]{:S(2)}, u32[]{:S(2)}) collective-permute-start(bf16[4,16,16,256]{3,2,1,0:T(8,128)(2,1)} %pad_maximum_fusion.2.t0), channel_id=1, source_target_pairs={{0,32},{16,48},{32,0},{48,16},{1,33},{17,49},{33,1},{49,17},{2,34}... | collective-permute-start | bytes 1572872 | tf_op jit(solution)/shard_map/left_gather/ppermute | solution.py:277
  123.6 7.4 %collective-permute-start.23 = (bf16[64,896]{1,0:T(8,128)(2,1)S(1)}, bf16[64,896]{1,0:T(8,128)(2,1)S(1)}, u32[]{:S(2)}, u32[]{:S(2)}) collective-permute-start(bf16[64,896]{1,0:T(8,128)(2,1)S(1)} %multiply_convert_fusion), channel_id=1, source_target_pairs={{0,192},{64,128},{128,64},{192,0},{1,193},{65,129},{129,65},{193,1... | collective-permute-start | bytes 344072 | tf_op jit(solution)/shard_map/left_gather/ppermute | solution.py:42
  126.4 9.8 %collective-permute-start.22 = (bf16[64,896]{1,0:T(8,128)(2,1)S(1)}, bf16[64,896]{1,0:T(8,128)(2,1)S(1)}, u32[]{:S(2)}, u32[]{:S(2)}) collective-permute-start(bf16[64,896]{1,0:T(8,128)(2,1)S(1)} %multiply_convert_fusion), channel_id=1, source_target_pairs={{0,128},{64,192},{128,0},{192,64},{1,129},{65,193},{129,1},{193,65... | collective-permute-start | bytes 344072 | tf_op jit(solution)/shard_map/left_gather/ppermute | solution.py:42
  128.5 7.7 %collective-permute-start.21 = (bf16[64,896]{1,0:T(8,128)(2,1)S(1)}, bf16[64,896]{1,0:T(8,128)(2,1)S(1)}, u32[]{:S(2)}, u32[]{:S(2)}) collective-permute-start(bf16[64,896]{1,0:T(8,128)(2,1)S(1)} %multiply_convert_fusion), channel_id=1, source_target_pairs={{0,64},{64,0},{128,192},{192,128},{1,65},{65,1},{129,193},{193,129... | collective-permute-start | bytes 344072 | tf_op jit(solution)/shard_map/left_gather/ppermute | solution.py:42
  136.3 22.8 %collective-permute-start.27 = (bf16[4,64,896]{2,1,0:T(8,128)(2,1)S(1)}, bf16[4,64,896]{2,1,0:T(8,128)(2,1)S(1)}, u32[]{:S(2)}, u32[]{:S(2)}) collective-permute-start(bf16[4,64,896]{2,1,0:T(8,128)(2,1)S(1)} %pad_maximum_fusion.3.refs_0_), channel_id=1, source_target_pairs={{0,16},{16,32},{32,48},{48,0},{1,17},{17,33},{33,49},{49,1},{2,18}... | collective-permute-start | bytes 1376264 | tf_op jit(solution)/shard_map/left_gather/ppermute | solution.py:38
  137.3 21.8 %collective-permute-start.26 = (bf16[4,64,896]{2,1,0:T(8,128)(2,1)S(1)}, bf16[4,64,896]{2,1,0:T(8,128)(2,1)}, u32[]{:S(2)}, u32[]{:S(2)}) collective-permute-start(bf16[4,64,896]{2,1,0:T(8,128)(2,1)S(1)} %pad_maximum_fusion.3.refs_0_), channel_id=1, source_target_pairs={{0,32},{16,48},{32,0},{48,16},{1,33},{17,49},{33,1},{49,17},{2,34}... | collective-permute-start | bytes 1376264 | tf_op jit(solution)/shard_map/left_gather/ppermute | solution.py:38
  139.4 21.7 %collective-permute-start.25 = (bf16[4,64,896]{2,1,0:T(8,128)(2,1)S(1)}, bf16[4,64,896]{2,1,0:T(8,128)(2,1)}, u32[]{:S(2)}, u32[]{:S(2)}) collective-permute-start(bf16[4,64,896]{2,1,0:T(8,128)(2,1)S(1)} %pad_maximum_fusion.3.refs_0_), channel_id=1, source_target_pairs={{0,48},{16,0},{32,16},{48,32},{1,49},{17,1},{33,17},{49,33},{2,50}... | collective-permute-start | bytes 1376264 | tf_op jit(solution)/shard_map/left_gather/ppermute | solution.py:38
  149.8 44.8 %all-to-all-start.1 = ((bf16[16,16,896]{2,1,0:T(8,128)(2,1)}), bf16[16,16,896]{2,1,0:T(8,128)(2,1)S(1)}, u32[]{:S(2)}, u32[]{:S(2)}) async-start(bf16[16,16,896]{2,1,0:T(8,128)(2,1)} %input_grad.1), calls=%async_computation.1 | async-start | bytes 917504 | tf_op jit(solution)/shard_map/input_grad/all_to_all | solution.py:310
  176.1 8.0 %collective-permute-start.33 = (f32[64,256]{1,0:T(8,128)S(1)}, f32[64,256]{1,0:T(8,128)S(1)}, u32[]{:S(2)}, u32[]{:S(2)}) collective-permute-start(f32[64,256]{1,0:T(8,128)S(1)} %add_add_fusion.s0), channel_id=1, source_target_pairs={{0,192},{64,128},{128,64},{192,0},{1,193},{65,129},{129,65},{193,1... | collective-permute-start | bytes 196616 | tf_op jit(solution)/shard_map/right/ppermute | solution.py:42
  (11 other events, 38.1 us)
Sparse Core Ops, SparseCore 0:
  9.8 48.6 all-gather.4
  70.2 36.6 all-gather.6

commit v3 on v2

--- a/solution.py
+++ b/solution.py
@@ -235,16 +235,17 @@
         near = jnp.concatenate([mine] + ring3(mine, "y"), axis=0)
     with jax.named_scope("grad_gather"):
         tokens = lax.all_to_all(grad.reshape(16, 16, COLS), ("y", "zh", "c"), 0, 0)
-    near, other, tokens, a = lax.optimization_barrier((near, other, tokens, a))
+    near, other, a = lax.optimization_barrier((near, other, a))
     with jax.named_scope("weight_gather"):
-        weight = lax.all_gather(down_weight, ("y", "c"))
         far_weight = lax.ppermute(after(down_weight, near), "zh", SWAP)
     with jax.named_scope("hidden_gather"):
         far = jnp.concatenate([other] + ring3(other, "y"), axis=0)
-        cross = lax.ppermute(near, "c", SWAP)
+        shared, tokens = lax.optimization_barrier((near, tokens))
+        cross = lax.ppermute(shared, "c", SWAP)
         far, far_weight, cross = lax.optimization_barrier((far, far_weight, cross))
         hidden = [near, far, cross, lax.ppermute(far, "c", SWAP)]
     with jax.named_scope("weight_gather"):
+        weight = lax.all_gather(after(down_weight, far), ("y", "c"))
         far_weight = lax.all_gather(far_weight, ("y", "c"))
 
     table = (((x + four) % 4)[:, None] * 4 + (zl ^ four)[None, :]).reshape(16).astype(jnp.int32)

time: 206 us -> 198 us (0.961)
  waiting for transfers between devices: 60.2 us -> 54.5 us
    ppermute x12, waiting for transfers between devices: 33.5 us -> 22.9 us  [ring3(): return [lax.ppermute(value, axis, shift(-s)) for s in (1, 2, 3)]]
    ppermute x1, waiting for transfers between devices: 0.01 us -> 7.69 us  [on_device(): far_weight = lax.ppermute(after(down_weight, near), 'zh', SWAP)]
    unnamed x10 -> x8, local copies, waits for them, and re-layouts: 5.52 us -> 4.74 us
  transfers between devices with their start and end apart: 38 -> 38, of which waited for: 19 -> 20; matrix products, arithmetic and copies ran while one was open for 3% -> 3% of each run, Pallas kernels for 16% -> 17%
where the time goes in v3:
time: 198 us; the launch traced here: 195 us
  starting transfers between devices  82 us (41%)
  waiting for transfers between devices  54.5 us (28%)
  Pallas kernels  33.4 us (17%)
  between operations  14.2 us (7%)
  other arithmetic  5.49 us (3%)
  local copies, waits for them, and re-layouts  5.43 us (3%)
    ppermute x12, waiting for transfers between devices, ring3(): return [lax.ppermute(value, axis, shift(-s)) for s in (1, 2, 3)]  22.9 us
    ppermute x9, starting transfers between devices, flip3(): return [lax.ppermute(value, 'zl', flip(s)) for s in (1, 2, 3)]  22.2 us
    pallas_call x7, Pallas kernels, call(): pl.pallas_call(kernel, out_shape=[jax.ShapeDtypeStruct(s, d) for s, d in...  15.8 us
    ppermute x12, starting transfers between devices, ring3(): return [lax.ppermute(value, axis, shift(-s)) for s in (1, 2, 3)]  15.3 us
    ppermute x9, waiting for transfers between devices, flip3(): return [lax.ppermute(value, 'zl', flip(s)) for s in (1, 2, 3)]  13.2 us
    pallas_call x1, Pallas kernels, input_of(): pl.pallas_call(input_kernel, out_shape=jax.ShapeDtypeStruct((16, 16, BLOC...  9.13 us
    ppermute x1, starting transfers between devices, on_device(): far_weight = lax.ppermute(after(down_weight, near), 'zh', SWAP)  8.75 us
    pallas_call x1, Pallas kernels, error_of(): pl.pallas_call(error_kernel, out_shape=(jax.ShapeDtypeStruct((RANK, COLS)...  8.46 us
  transfers between devices with their start and end apart: 38, of which 20 were waited for; matrix products, arithmetic and copies ran while one was open for 3% of the time, Pallas kernels for 17%

profile of v3, /device:TPU:16, one launch (start us, length us, event | category | flops | bytes accessed | tf_op | source)
XLA Modules:
  0.0 195.1 jit_solution(7185097858930067965)
XLA Ops:
  9.4 2.5 %collective-permute-start = (bf16[16,14336]{1,0:T(8,128)(2,1)}, bf16[16,14336]{1,0:T(8,128)(2,1)}, u32[]{:S(2)}, u32[]{:S(2)}) collective-permute-start(bf16[16,14336]{1,0:T(8,128)(2,1)} %bitcast.21), channel_id=1, source_target_pairs={{0,12},{4,0},{8,4},{12,8},{1,13},{5,1},{9,5},{13,9},{2,14},{6,2},{... | collective-permute-start | bytes 1376264 | tf_op jit(solution)/shard_map/hidden_gather/ppermute | solution.py:38
  11.9 5.5 %collective-permute-start.3 = (bf16[16,14336]{1,0:T(8,128)(2,1)}, bf16[16,14336]{1,0:T(8,128)(2,1)S(1)}, u32[]{:S(2)}, u32[]{:S(2)}) collective-permute-start(bf16[16,14336]{1,0:T(8,128)(2,1)} %bitcast.22), channel_id=1, source_target_pairs={{0,2},{2,0},{1,3},{3,1},{4,6},{6,4},{5,7},{7,5},{8,10},{10,8},{9,1... | collective-permute-start | bytes 1376264 | tf_op jit(solution)/shard_map/hidden_gather/ppermute | solution.py:234
  17.4 6.5 %all-to-all-start = ((bf16[16,16,256]{2,1,0:T(8,128)(2,1)}), bf16[16,16,256]{2,1,0:T(8,128)(2,1)S(1)}, u32[]{:S(2)}, u32[]{:S(2)}) async-start(bf16[16,16,256]{2,1,0:T(8,128)(2,1)} %bitcast.14), calls=%async_computation | async-start | bytes 262144 | tf_op jit(solution)/shard_map/grad_gather/all_to_all | solution.py:237
  29.9 2.5 %collective-permute-done = bf16[16,14336]{1,0:T(8,128)(2,1)} collective-permute-done((bf16[16,14336]{1,0:T(8,128)(2,1)}, bf16[16,14336]{1,0:T(8,128)(2,1)}, u32[]{:S(2)}, u32[]{:S(2)}) %collective-permute-start) | collective-permute-done | bytes 458784 | tf_op jit(solution)/shard_map/hidden_gather/ppermute | solution.py:38
  36.8 8.8 %collective-permute-start.7 = (bf16[896,256]{1,0:T(8,128)(2,1)}, bf16[896,256]{1,0:T(8,128)(2,1)}, u32[]{:S(2)}, u32[]{:S(2)}) collective-permute-start(bf16[896,256]{1,0:T(8,128)(2,1)} %param.6), channel_id=1, source_target_pairs={{0,2},{2,0},{1,3},{3,1},{4,6},{6,4},{5,7},{7,5},{8,10},{10,8},{9,1... | collective-permute-start | bytes 1376264 | tf_op jit(solution)/shard_map/weight_gather/ppermute | solution.py:240
  45.5 9.0 %collective-permute-done.5 = bf16[16,14336]{1,0:T(8,128)(2,1)S(1)} collective-permute-done((bf16[16,14336]{1,0:T(8,128)(2,1)S(1)}, bf16[16,14336]{1,0:T(8,128)(2,1)S(1)}, u32[]{:S(2)}, u32[]{:S(2)}) %collective-permute-start.5) | collective-permute-done | bytes 458784 | tf_op jit(solution)/shard_map/hidden_gather/ppermute | solution.py:38
  55.7 2.4 %pad_maximum_fusion.1.refs_1_.refs_5_.h1 = bf16[64,14336]{1,0:T(8,128)(2,1)} fusion(bf16[16,14336]{1,0:T(8,128)(2,1)S(1)} %collective-permute-done.6, bf16[16,14336]{1,0:T(8,128)(2,1)S(1)} %collective-permute-done.5, bf16[16,14336]{1,0:T(8,128)(2,1)} %collective-permute-done.4, bf16[16,14336]{1,0:T(8,128)(2,1)S(1)} %collective-permute-done.3), kind=kLoop, calls=%fused_computation.1 | loop fusion | flops 7340032 | bytes 3670016 | tf_op jit(solution)/shard_map/hidden_gather/concatenate | solution.py:242
  58.1 7.7 %collective-permute-done.7 = bf16[896,256]{1,0:T(8,128)(2,1)} collective-permute-done((bf16[896,256]{1,0:T(8,128)(2,1)}, bf16[896,256]{1,0:T(8,128)(2,1)}, u32[]{:S(2)}, u32[]{:S(2)}) %collective-permute-start.7) | collective-permute-done | bytes 458784 | tf_op jit(solution)/shard_map/weight_gather/ppermute | solution.py:240
  66.9 3.9 %collective-permute-done.9.refs_3_.refs_7_.h3 = bf16[64,14336]{1,0:T(8,128)(2,1)} collective-permute-done((bf16[64,14336]{1,0:T(8,128)(2,1)}, bf16[64,14336]{1,0:T(8,128)(2,1)}, u32[]{:S(2)}, u32[]{:S(2)}) %collective-permute-start.9) | collective-permute-done | bytes 1835040 | tf_op jit(solution)/shard_map/hidden_gather/ppermute | solution.py:246
  72.3 3.4 %left.1 = (bf16[4,64,896]{2,1,0:T(8,128)(2,1)S(1)}, bf16[4,64,896]{2,1,0:T(8,128)(2,1)S(1)}, bf16[4,64,896]{2,1,0:T(8,128)(2,1)S(1)}, bf16[4,64,896]{2,1,0:T(8,128)(2,1)S(1)}) custom-call(s32[16]{0:T(128)S(1)} %add.174.table, bf16[128,256]{1,0:T(8,128)(2,1)S(1)} %get-tuple-element.49.a_ref, bf16[64,14336]{1,0:T(8,128)(2,1)S(1)} %pad_maximum_fusion.refs_0_.refs_4_.h0, ...), custom_call_target="tpu_custom_call" | custom-call | flops 939524096 | bytes 7405568 | tf_op jit(solution)/shard_map/left_reduce/left/pallas_call | solution.py:63
  77.2 2.7 %collective-permute-start.11 = (bf16[4,64,896]{2,1,0:T(8,128)(2,1)S(1)}, bf16[4,64,896]{2,1,0:T(8,128)(2,1)S(1)}, u32[]{:S(2)}, u32[]{:S(2)}) collective-permute-start(bf16[4,64,896]{2,1,0:T(8,128)(2,1)S(1)} %get-tuple-element.58), channel_id=1, source_target_pairs={{0,32},{16,48},{32,0},{48,16},{1,33},{17,49},{33,1},{49,17},{2,34}... | collective-permute-start | bytes 1376264 | tf_op jit(solution)/shard_map/left_reduce/ppermute | solution.py:261
  81.4 5.8 %collective-permute-start.14 = (bf16[16,16,256]{2,1,0:T(8,128)(2,1)S(1)}, bf16[16,16,256]{2,1,0:T(8,128)(2,1)S(1)}, u32[]{:S(2)}, u32[]{:S(2)}) collective-permute-start(bf16[16,16,256]{2,1,0:T(8,128)(2,1)S(1)} %all-to-all-done), channel_id=1, source_target_pairs={{0,128},{64,192},{128,0},{192,64},{1,129},{65,193},{129,1},{193,65... | collective-permute-start | bytes 393224 | tf_op jit(solution)/shard_map/left_reduce/ppermute | solution.py:42
  88.4 6.1 %collective-permute-start.13 = (bf16[16,16,256]{2,1,0:T(8,128)(2,1)S(1)}, bf16[16,16,256]{2,1,0:T(8,128)(2,1)S(1)}, u32[]{:S(2)}, u32[]{:S(2)}) collective-permute-start(bf16[16,16,256]{2,1,0:T(8,128)(2,1)S(1)} %all-to-all-done), channel_id=1, source_target_pairs={{0,64},{64,0},{128,192},{192,128},{1,65},{65,1},{129,193},{193,129... | collective-permute-start | bytes 393224 | tf_op jit(solution)/shard_map/left_reduce/ppermute | solution.py:42
  94.4 2.3 %collective-permute-done.14 = bf16[16,16,256]{2,1,0:T(8,128)(2,1)S(1)} collective-permute-done((bf16[16,16,256]{2,1,0:T(8,128)(2,1)S(1)}, bf16[16,16,256]{2,1,0:T(8,128)(2,1)S(1)}, u32[]{:S(2)}, u32[]{:S(2)}) %collective-permute-start.14) | collective-permute-done | bytes 131104 | tf_op jit(solution)/shard_map/left_reduce/ppermute | solution.py:42
  96.7 2.7 %collective-permute-done.13 = bf16[16,16,256]{2,1,0:T(8,128)(2,1)S(1)} collective-permute-done((bf16[16,16,256]{2,1,0:T(8,128)(2,1)S(1)}, bf16[16,16,256]{2,1,0:T(8,128)(2,1)S(1)}, u32[]{:S(2)}, u32[]{:S(2)}) %collective-permute-start.13) | collective-permute-done | bytes 131104 | tf_op jit(solution)/shard_map/left_reduce/ppermute | solution.py:42
  103.9 3.2 %collective-permute-start.17 = (bf16[64,896]{1,0:T(8,128)(2,1)S(1)}, bf16[64,896]{1,0:T(8,128)(2,1)S(1)}, u32[]{:S(2)}, u32[]{:S(2)}) collective-permute-start(bf16[64,896]{1,0:T(8,128)(2,1)S(1)} %get-tuple-element.69), channel_id=1, source_target_pairs={{0,128},{64,192},{128,0},{192,64},{1,129},{65,193},{129,1},{193,65... | collective-permute-start | bytes 344072 | tf_op jit(solution)/shard_map/left_reduce/ppermute | solution.py:275
  107.0 3.6 %collective-permute-start.18 = (bf16[64,896]{1,0:T(8,128)(2,1)S(1)}, bf16[64,896]{1,0:T(8,128)(2,1)S(1)}, u32[]{:S(2)}, u32[]{:S(2)}) collective-permute-start(bf16[64,896]{1,0:T(8,128)(2,1)S(1)} %get-tuple-element.70), channel_id=1, source_target_pairs={{0,192},{64,128},{128,64},{192,0},{1,193},{65,129},{129,65},{193,1... | collective-permute-start | bytes 344072 | tf_op jit(solution)/shard_map/left_reduce/ppermute | solution.py:275
  110.6 3.2 %collective-permute-done.17 = bf16[64,896]{1,0:T(8,128)(2,1)S(1)} collective-permute-done((bf16[64,896]{1,0:T(8,128)(2,1)S(1)}, bf16[64,896]{1,0:T(8,128)(2,1)S(1)}, u32[]{:S(2)}, u32[]{:S(2)}) %collective-permute-start.17) | collective-permute-done | bytes 114720 | tf_op jit(solution)/shard_map/left_reduce/ppermute | solution.py:275
  113.8 2.5 %collective-permute-done.18 = bf16[64,896]{1,0:T(8,128)(2,1)S(1)} collective-permute-done((bf16[64,896]{1,0:T(8,128)(2,1)S(1)}, bf16[64,896]{1,0:T(8,128)(2,1)S(1)}, u32[]{:S(2)}, u32[]{:S(2)}) %collective-permute-start.18) | collective-permute-done | bytes 114720 | tf_op jit(solution)/shard_map/left_reduce/ppermute | solution.py:275
  118.2 2.2 %collective-permute-start.23 = (bf16[64,896]{1,0:T(8,128)(2,1)S(1)}, bf16[64,896]{1,0:T(8,128)(2,1)S(1)}, u32[]{:S(2)}, u32[]{:S(2)}) collective-permute-start(bf16[64,896]{1,0:T(8,128)(2,1)S(1)} %multiply_convert_fusion), channel_id=1, source_target_pairs={{0,192},{64,128},{128,64},{192,0},{1,193},{65,129},{129,65},{193,1... | collective-permute-start | bytes 344072 | tf_op jit(solution)/shard_map/left_gather/ppermute | solution.py:42
  120.4 3.6 %collective-permute-start.22 = (bf16[64,896]{1,0:T(8,128)(2,1)S(1)}, bf16[64,896]{1,0:T(8,128)(2,1)S(1)}, u32[]{:S(2)}, u32[]{:S(2)}) collective-permute-start(bf16[64,896]{1,0:T(8,128)(2,1)S(1)} %multiply_convert_fusion), channel_id=1, source_target_pairs={{0,128},{64,192},{128,0},{192,64},{1,129},{65,193},{129,1},{193,65... | collective-permute-start | bytes 344072 | tf_op jit(solution)/shard_map/left_gather/ppermute | solution.py:42
  125.7 6.1 %collective-permute-done.22 = bf16[64,896]{1,0:T(8,128)(2,1)S(1)} collective-permute-done((bf16[64,896]{1,0:T(8,128)(2,1)S(1)}, bf16[64,896]{1,0:T(8,128)(2,1)S(1)}, u32[]{:S(2)}, u32[]{:S(2)}) %collective-permute-start.22) | collective-permute-done | bytes 114720 | tf_op jit(solution)/shard_map/left_gather/ppermute | solution.py:42
  136.3 9.1 %input_grad.1 = bf16[16,16,896]{2,1,0:T(8,128)(2,1)} custom-call(s32[16]{0:T(128)} %add.163.group, s32[16]{0:T(128)} %pad_add_fusion.shard, bf16[4,16,16,256]{3,2,1,0:T(8,128)(2,1)} %pad_maximum_fusion.2.t0, bf16[4,16,16,256]{3,2,1,0:T(8,128)(2,1)} %collective-permute-done.19.t1, bf16[4,16,16,256]{3,2,1,0:T(8,128)(2,1)} %collective-permute-done.24.t2, ...), custom_call_target="tpu_custom_call" | custom-call | flops 1879048192 | bytes 10485760 | tf_op jit(solution)/shard_map/input_grad/input_grad/pallas_call | solution.py:199
  145.4 6.3 %all-to-all-start.1 = ((bf16[16,16,896]{2,1,0:T(8,128)(2,1)}), bf16[16,16,896]{2,1,0:T(8,128)(2,1)S(1)}, u32[]{:S(2)}, u32[]{:S(2)}) async-start(bf16[16,16,896]{2,1,0:T(8,128)(2,1)} %input_grad.1), calls=%async_computation.1 | async-start | bytes 917504 | tf_op jit(solution)/shard_map/input_grad/all_to_all | solution.py:311
  151.7 3.2 %collective-permute-done.27.refs_3_ = bf16[4,64,896]{2,1,0:T(8,128)(2,1)S(1)} collective-permute-done((bf16[4,64,896]{2,1,0:T(8,128)(2,1)S(1)}, bf16[4,64,896]{2,1,0:T(8,128)(2,1)S(1)}, u32[]{:S(2)}, u32[]{:S(2)}) %collective-permute-start.27) | collective-permute-done | bytes 458784 | tf_op jit(solution)/shard_map/left_gather/ppermute | solution.py:38
  155.0 2.3 %collective-permute-done.25.refs_1_ = bf16[4,64,896]{2,1,0:T(8,128)(2,1)} collective-permute-done((bf16[4,64,896]{2,1,0:T(8,128)(2,1)S(1)}, bf16[4,64,896]{2,1,0:T(8,128)(2,1)}, u32[]{:S(2)}, u32[]{:S(2)}) %collective-permute-start.25) | collective-permute-done | bytes 458784 | tf_op jit(solution)/shard_map/left_gather/ppermute | solution.py:38
  158.8 5.2 %stats.1 = (bf16[64,14336]{1,0:T(8,128)(2,1)S(1)}, f32[64,256]{1,0:T(8,128)S(1)}, f32[64,64]{1,0:T(8,128)S(1)}) custom-call(s32[16]{0:T(128)S(1)} %add.174.table, bf16[4,64,896]{2,1,0:T(8,128)(2,1)S(1)} %pad_maximum_fusion.3.refs_0_, bf16[4,64,896]{2,1,0:T(8,128)(2,1)} %collective-permute-done.25.refs_1_, ...), custom_call_target="tpu_custom_call" | custom-call | flops 587202560 | bytes 9306112 | tf_op jit(solution)/shard_map/stats/stats/pallas_call | solution.py:63
  164.1 3.5 %collective-permute-start.29 = (f32[64,256]{1,0:T(8,128)S(1)}, f32[64,256]{1,0:T(8,128)S(1)}, u32[]{:S(2)}, u32[]{:S(2)}) collective-permute-start(f32[64,256]{1,0:T(8,128)S(1)} %get-tuple-element.86), channel_id=1, source_target_pairs={{0,32},{16,48},{32,0},{48,16},{1,33},{17,49},{33,1},{49,17},{2,34}... | collective-permute-start | bytes 196616 | tf_op jit(solution)/shard_map/right/ppermute | solution.py:38
  167.5 2.7 %inverse_upper.1.both = f32[64,128]{1,0:T(8,128)S(1)} custom-call(f32[64,64]{1,0:T(8,128)S(1)} %get-tuple-element.87.gram), custom_call_target="tpu_custom_call" | custom-call | flops 524288 | bytes 16384 | tf_op jit(solution)/shard_map/right/inverse_upper/pallas_call | solution.py:63
  173.5 2.7 %collective-permute-start.31 = (f32[64,256]{1,0:T(8,128)S(1)}, f32[64,256]{1,0:T(8,128)S(1)}, u32[]{:S(2)}, u32[]{:S(2)}) collective-permute-start(f32[64,256]{1,0:T(8,128)S(1)} %add_add_fusion.s0), channel_id=1, source_target_pairs={{0,64},{64,0},{128,192},{192,128},{1,65},{65,1},{129,193},{193,129... | collective-permute-start | bytes 196616 | tf_op jit(solution)/shard_map/right/ppermute | solution.py:42
  176.3 2.7 %inverse_lower.1.inverse = f32[64,64]{1,0:T(8,128)S(1)} custom-call(f32[64,128]{1,0:T(8,128)S(1)} %inverse_upper.1.both), custom_call_target="tpu_custom_call" | custom-call | flops 524288 | bytes 32768 | tf_op jit(solution)/shard_map/right/inverse_lower/pallas_call | solution.py:63
  179.0 8.5 %error_new.1 = (f32[64,256]{1,0:T(8,128)}, bf16[14336,256]{1,0:T(8,128)(2,1)}) custom-call(f32[64,64]{1,0:T(8,128)S(1)} %inverse_lower.1.inverse, f32[64,256]{1,0:T(8,128)S(1)} %add_add_fusion.s0, f32[64,256]{1,0:T(8,128)S(1)} %collective-permute-done.31.s1, f32[64,256]{1,0:T(8,128)S(1)} %collective-permute-done.32.s2, ...), custom_call_target="tpu_custom_call" | custom-call | flops 2818572288 | bytes 16515072 | tf_op jit(solution)/shard_map/error_new/error_new/pallas_call | solution.py:168
  (80 shorter events, 38.6 us)
Async XLA Ops:
  7.2 21.1 %collective-permute-start.2 = (bf16[16,14336]{1,0:T(8,128)(2,1)}, bf16[16,14336]{1,0:T(8,128)(2,1)S(1)}, u32[]{:S(2)}, u32[]{:S(2)}) collective-permute-start(bf16[16,14336]{1,0:T(8,128)(2,1)} %bitcast.19), channel_id=1, source_target_pairs={{0,4},{4,8},{8,12},{12,0},{1,5},{5,9},{9,13},{13,1},{2,6},{6,10},{... | collective-permute-start | bytes 1376264 | tf_op jit(solution)/shard_map/hidden_gather/ppermute | solution.py:38
  8.5 21.4 %collective-permute-start.1 = (bf16[16,14336]{1,0:T(8,128)(2,1)}, bf16[16,14336]{1,0:T(8,128)(2,1)S(1)}, u32[]{:S(2)}, u32[]{:S(2)}) collective-permute-start(bf16[16,14336]{1,0:T(8,128)(2,1)} %bitcast.20), channel_id=1, source_target_pairs={{0,8},{4,12},{8,0},{12,4},{1,9},{5,13},{9,1},{13,5},{2,10},{6,14},... | collective-permute-start | bytes 1376264 | tf_op jit(solution)/shard_map/hidden_gather/ppermute | solution.py:38
  9.4 22.9 %collective-permute-start = (bf16[16,14336]{1,0:T(8,128)(2,1)}, bf16[16,14336]{1,0:T(8,128)(2,1)}, u32[]{:S(2)}, u32[]{:S(2)}) collective-permute-start(bf16[16,14336]{1,0:T(8,128)(2,1)} %bitcast.21), channel_id=1, source_target_pairs={{0,12},{4,0},{8,4},{12,8},{1,13},{5,1},{9,5},{13,9},{2,14},{6,2},{... | collective-permute-start | bytes 1376264 | tf_op jit(solution)/shard_map/hidden_gather/ppermute | solution.py:38
  11.9 21.7 %collective-permute-start.3 = (bf16[16,14336]{1,0:T(8,128)(2,1)}, bf16[16,14336]{1,0:T(8,128)(2,1)S(1)}, u32[]{:S(2)}, u32[]{:S(2)}) collective-permute-start(bf16[16,14336]{1,0:T(8,128)(2,1)} %bitcast.22), channel_id=1, source_target_pairs={{0,2},{2,0},{1,3},{3,1},{4,6},{6,4},{5,7},{7,5},{8,10},{10,8},{9,1... | collective-permute-start | bytes 1376264 | tf_op jit(solution)/shard_map/hidden_gather/ppermute | solution.py:234
  17.4 19.4 %all-to-all-start = ((bf16[16,16,256]{2,1,0:T(8,128)(2,1)}), bf16[16,16,256]{2,1,0:T(8,128)(2,1)S(1)}, u32[]{:S(2)}, u32[]{:S(2)}) async-start(bf16[16,16,256]{2,1,0:T(8,128)(2,1)} %bitcast.14), calls=%async_computation | async-start | bytes 262144 | tf_op jit(solution)/shard_map/grad_gather/all_to_all | solution.py:237
  23.9 112.3 %all-gather.5.cloned.1.call-start = ((), (), s32[]{:S(2)}) async-start(), calls=%async_computation.2 | async-start | bytes 4128768 | tf_op jit(solution)/shard_map/weight_gather/all_gather | solution.py:248
  33.6 11.9 %collective-permute-start.6 = (bf16[16,14336]{1,0:T(8,128)(2,1)S(1)}, bf16[16,14336]{1,0:T(8,128)(2,1)S(1)}, u32[]{:S(2)}, u32[]{:S(2)}) collective-permute-start(bf16[16,14336]{1,0:T(8,128)(2,1)S(1)} %collective-permute-done.3), channel_id=1, source_target_pairs={{0,4},{4,8},{8,12},{12,0},{1,5},{5,9},{9,13},{13,1},{2,6},{6,10},{... | collective-permute-start | bytes 1376264 | tf_op jit(solution)/shard_map/hidden_gather/ppermute | solution.py:38
  34.3 20.3 %collective-permute-start.5 = (bf16[16,14336]{1,0:T(8,128)(2,1)S(1)}, bf16[16,14336]{1,0:T(8,128)(2,1)S(1)}, u32[]{:S(2)}, u32[]{:S(2)}) collective-permute-start(bf16[16,14336]{1,0:T(8,128)(2,1)S(1)} %collective-permute-done.3), channel_id=1, source_target_pairs={{0,8},{4,12},{8,0},{12,4},{1,9},{5,13},{9,1},{13,5},{2,10},{6,14},... | collective-permute-start | bytes 1376264 | tf_op jit(solution)/shard_map/hidden_gather/ppermute | solution.py:38
  35.6 20.1 %collective-permute-start.4 = (bf16[16,14336]{1,0:T(8,128)(2,1)S(1)}, bf16[16,14336]{1,0:T(8,128)(2,1)}, u32[]{:S(2)}, u32[]{:S(2)}) collective-permute-start(bf16[16,14336]{1,0:T(8,128)(2,1)S(1)} %collective-permute-done.3), channel_id=1, source_target_pairs={{0,12},{4,0},{8,4},{12,8},{1,13},{5,1},{9,5},{13,9},{2,14},{6,2},{... | collective-permute-start | bytes 1376264 | tf_op jit(solution)/shard_map/hidden_gather/ppermute | solution.py:38
  36.8 29.0 %collective-permute-start.8 = (bf16[64,14336]{1,0:T(8,128)(2,1)S(1)}, bf16[64,14336]{1,0:T(8,128)(2,1)}, u32[]{:S(2)}, u32[]{:S(2)}) collective-permute-start(bf16[64,14336]{1,0:T(8,128)(2,1)S(1)} %pad_maximum_fusion.refs_0_.refs_4_.h0), channel_id=1, source_target_pairs={{0,1},{1,0},{2,3},{3,2},{4,5},{5,4},{6,7},{7,6},{8,9},{9,8},{10,11... | collective-permute-start | bytes 5505032 | tf_op jit(solution)/shard_map/hidden_gather/ppermute | solution.py:244
  36.8 29.0 %collective-permute-start.7 = (bf16[896,256]{1,0:T(8,128)(2,1)}, bf16[896,256]{1,0:T(8,128)(2,1)}, u32[]{:S(2)}, u32[]{:S(2)}) collective-permute-start(bf16[896,256]{1,0:T(8,128)(2,1)} %param.6), channel_id=1, source_target_pairs={{0,2},{2,0},{1,3},{3,1},{4,6},{6,4},{5,7},{7,5},{8,10},{10,8},{9,1... | collective-permute-start | bytes 1376264 | tf_op jit(solution)/shard_map/weight_gather/ppermute | solution.py:240
  65.8 70.5 %all-gather.7.cloned.1.call-start = ((), (), s32[]{:S(2)}) async-start(), calls=%async_computation.3 | async-start | bytes 4128768 | tf_op jit(solution)/shard_map/weight_gather/all_gather | solution.py:249
  75.7 24.6 %collective-permute-start.10 = (bf16[4,64,896]{2,1,0:T(8,128)(2,1)S(1)}, bf16[4,64,896]{2,1,0:T(8,128)(2,1)S(1)}, u32[]{:S(2)}, u32[]{:S(2)}) collective-permute-start(bf16[4,64,896]{2,1,0:T(8,128)(2,1)S(1)} %get-tuple-element.57), channel_id=1, source_target_pairs={{0,16},{16,32},{32,48},{48,0},{1,17},{17,33},{33,49},{49,1},{2,18}... | collective-permute-start | bytes 1376264 | tf_op jit(solution)/shard_map/left_reduce/ppermute | solution.py:261
  77.2 23.1 %collective-permute-start.11 = (bf16[4,64,896]{2,1,0:T(8,128)(2,1)S(1)}, bf16[4,64,896]{2,1,0:T(8,128)(2,1)S(1)}, u32[]{:S(2)}, u32[]{:S(2)}) collective-permute-start(bf16[4,64,896]{2,1,0:T(8,128)(2,1)S(1)} %get-tuple-element.58), channel_id=1, source_target_pairs={{0,32},{16,48},{32,0},{48,16},{1,33},{17,49},{33,1},{49,17},{2,34}... | collective-permute-start | bytes 1376264 | tf_op jit(solution)/shard_map/left_reduce/ppermute | solution.py:261
  79.9 20.4 %collective-permute-start.12 = (bf16[4,64,896]{2,1,0:T(8,128)(2,1)S(1)}, bf16[4,64,896]{2,1,0:T(8,128)(2,1)S(1)}, u32[]{:S(2)}, u32[]{:S(2)}) collective-permute-start(bf16[4,64,896]{2,1,0:T(8,128)(2,1)S(1)} %get-tuple-element.59), channel_id=1, source_target_pairs={{0,48},{16,0},{32,16},{48,32},{1,49},{17,1},{33,17},{49,33},{2,50}... | collective-permute-start | bytes 1376264 | tf_op jit(solution)/shard_map/left_reduce/ppermute | solution.py:261
  81.4 7.0 %collective-permute-start.15 = (bf16[16,16,256]{2,1,0:T(8,128)(2,1)S(1)}, bf16[16,16,256]{2,1,0:T(8,128)(2,1)S(1)}, u32[]{:S(2)}, u32[]{:S(2)}) collective-permute-start(bf16[16,16,256]{2,1,0:T(8,128)(2,1)S(1)} %all-to-all-done), channel_id=1, source_target_pairs={{0,192},{64,128},{128,64},{192,0},{1,193},{65,129},{129,65},{193,1... | collective-permute-start | bytes 393224 | tf_op jit(solution)/shard_map/left_reduce/ppermute | solution.py:42
  81.4 15.3 %collective-permute-start.14 = (bf16[16,16,256]{2,1,0:T(8,128)(2,1)S(1)}, bf16[16,16,256]{2,1,0:T(8,128)(2,1)S(1)}, u32[]{:S(2)}, u32[]{:S(2)}) collective-permute-start(bf16[16,16,256]{2,1,0:T(8,128)(2,1)S(1)} %all-to-all-done), channel_id=1, source_target_pairs={{0,128},{64,192},{128,0},{192,64},{1,129},{65,193},{129,1},{193,65... | collective-permute-start | bytes 393224 | tf_op jit(solution)/shard_map/left_reduce/ppermute | solution.py:42
  88.4 11.0 %collective-permute-start.13 = (bf16[16,16,256]{2,1,0:T(8,128)(2,1)S(1)}, bf16[16,16,256]{2,1,0:T(8,128)(2,1)S(1)}, u32[]{:S(2)}, u32[]{:S(2)}) collective-permute-start(bf16[16,16,256]{2,1,0:T(8,128)(2,1)S(1)} %all-to-all-done), channel_id=1, source_target_pairs={{0,64},{64,0},{128,192},{192,128},{1,65},{65,1},{129,193},{193,129... | collective-permute-start | bytes 393224 | tf_op jit(solution)/shard_map/left_reduce/ppermute | solution.py:42
  100.5 16.1 %collective-permute-start.20 = (bf16[4,16,16,256]{3,2,1,0:T(8,128)(2,1)}, bf16[4,16,16,256]{3,2,1,0:T(8,128)(2,1)}, u32[]{:S(2)}, u32[]{:S(2)}) collective-permute-start(bf16[4,16,16,256]{3,2,1,0:T(8,128)(2,1)} %pad_maximum_fusion.2.t0), channel_id=1, source_target_pairs={{0,16},{16,32},{32,48},{48,0},{1,17},{17,33},{33,49},{49,1},{2,18}... | collective-permute-start | bytes 1572872 | tf_op jit(solution)/shard_map/left_reduce/ppermute | solution.py:273
  102.0 14.7 %collective-permute-start.19 = (bf16[4,16,16,256]{3,2,1,0:T(8,128)(2,1)}, bf16[4,16,16,256]{3,2,1,0:T(8,128)(2,1)}, u32[]{:S(2)}, u32[]{:S(2)}) collective-permute-start(bf16[4,16,16,256]{3,2,1,0:T(8,128)(2,1)} %pad_maximum_fusion.2.t0), channel_id=1, source_target_pairs={{0,48},{16,0},{32,16},{48,32},{1,49},{17,1},{33,17},{49,33},{2,50}... | collective-permute-start | bytes 1572872 | tf_op jit(solution)/shard_map/left_reduce/ppermute | solution.py:273
  103.9 10.0 %collective-permute-start.17 = (bf16[64,896]{1,0:T(8,128)(2,1)S(1)}, bf16[64,896]{1,0:T(8,128)(2,1)S(1)}, u32[]{:S(2)}, u32[]{:S(2)}) collective-permute-start(bf16[64,896]{1,0:T(8,128)(2,1)S(1)} %get-tuple-element.69), channel_id=1, source_target_pairs={{0,128},{64,192},{128,0},{192,64},{1,129},{65,193},{129,1},{193,65... | collective-permute-start | bytes 344072 | tf_op jit(solution)/shard_map/left_reduce/ppermute | solution.py:275
  107.0 9.3 %collective-permute-start.18 = (bf16[64,896]{1,0:T(8,128)(2,1)S(1)}, bf16[64,896]{1,0:T(8,128)(2,1)S(1)}, u32[]{:S(2)}, u32[]{:S(2)}) collective-permute-start(bf16[64,896]{1,0:T(8,128)(2,1)S(1)} %get-tuple-element.70), channel_id=1, source_target_pairs={{0,192},{64,128},{128,64},{192,0},{1,193},{65,129},{129,65},{193,1... | collective-permute-start | bytes 344072 | tf_op jit(solution)/shard_map/left_reduce/ppermute | solution.py:275
  116.7 15.2 %collective-permute-start.24 = (bf16[4,16,16,256]{3,2,1,0:T(8,128)(2,1)}, bf16[4,16,16,256]{3,2,1,0:T(8,128)(2,1)}, u32[]{:S(2)}, u32[]{:S(2)}) collective-permute-start(bf16[4,16,16,256]{3,2,1,0:T(8,128)(2,1)} %pad_maximum_fusion.2.t0), channel_id=1, source_target_pairs={{0,32},{16,48},{32,0},{48,16},{1,33},{17,49},{33,1},{49,17},{2,34}... | collective-permute-start | bytes 1572872 | tf_op jit(solution)/shard_map/left_gather/ppermute | solution.py:278
  118.2 7.5 %collective-permute-start.23 = (bf16[64,896]{1,0:T(8,128)(2,1)S(1)}, bf16[64,896]{1,0:T(8,128)(2,1)S(1)}, u32[]{:S(2)}, u32[]{:S(2)}) collective-permute-start(bf16[64,896]{1,0:T(8,128)(2,1)S(1)} %multiply_convert_fusion), channel_id=1, source_target_pairs={{0,192},{64,128},{128,64},{192,0},{1,193},{65,129},{129,65},{193,1... | collective-permute-start | bytes 344072 | tf_op jit(solution)/shard_map/left_gather/ppermute | solution.py:42
  120.4 11.4 %collective-permute-start.22 = (bf16[64,896]{1,0:T(8,128)(2,1)S(1)}, bf16[64,896]{1,0:T(8,128)(2,1)S(1)}, u32[]{:S(2)}, u32[]{:S(2)}) collective-permute-start(bf16[64,896]{1,0:T(8,128)(2,1)S(1)} %multiply_convert_fusion), channel_id=1, source_target_pairs={{0,128},{64,192},{128,0},{192,64},{1,129},{65,193},{129,1},{193,65... | collective-permute-start | bytes 344072 | tf_op jit(solution)/shard_map/left_gather/ppermute | solution.py:42
  124.1 7.7 %collective-permute-start.21 = (bf16[64,896]{1,0:T(8,128)(2,1)S(1)}, bf16[64,896]{1,0:T(8,128)(2,1)S(1)}, u32[]{:S(2)}, u32[]{:S(2)}) collective-permute-start(bf16[64,896]{1,0:T(8,128)(2,1)S(1)} %multiply_convert_fusion), channel_id=1, source_target_pairs={{0,64},{64,0},{128,192},{192,128},{1,65},{65,1},{129,193},{193,129... | collective-permute-start | bytes 344072 | tf_op jit(solution)/shard_map/left_gather/ppermute | solution.py:42
  131.9 23.1 %collective-permute-start.27 = (bf16[4,64,896]{2,1,0:T(8,128)(2,1)S(1)}, bf16[4,64,896]{2,1,0:T(8,128)(2,1)S(1)}, u32[]{:S(2)}, u32[]{:S(2)}) collective-permute-start(bf16[4,64,896]{2,1,0:T(8,128)(2,1)S(1)} %pad_maximum_fusion.3.refs_0_), channel_id=1, source_target_pairs={{0,16},{16,32},{32,48},{48,0},{1,17},{17,33},{33,49},{49,1},{2,18}... | collective-permute-start | bytes 1376264 | tf_op jit(solution)/shard_map/left_gather/ppermute | solution.py:38
  132.9 22.1 %collective-permute-start.26 = (bf16[4,64,896]{2,1,0:T(8,128)(2,1)S(1)}, bf16[4,64,896]{2,1,0:T(8,128)(2,1)}, u32[]{:S(2)}, u32[]{:S(2)}) collective-permute-start(bf16[4,64,896]{2,1,0:T(8,128)(2,1)S(1)} %pad_maximum_fusion.3.refs_0_), channel_id=1, source_target_pairs={{0,32},{16,48},{32,0},{48,16},{1,33},{17,49},{33,1},{49,17},{2,34}... | collective-permute-start | bytes 1376264 | tf_op jit(solution)/shard_map/left_gather/ppermute | solution.py:38
  135.1 22.2 %collective-permute-start.25 = (bf16[4,64,896]{2,1,0:T(8,128)(2,1)S(1)}, bf16[4,64,896]{2,1,0:T(8,128)(2,1)}, u32[]{:S(2)}, u32[]{:S(2)}) collective-permute-start(bf16[4,64,896]{2,1,0:T(8,128)(2,1)S(1)} %pad_maximum_fusion.3.refs_0_), channel_id=1, source_target_pairs={{0,48},{16,0},{32,16},{48,32},{1,49},{17,1},{33,17},{49,33},{2,50}... | collective-permute-start | bytes 1376264 | tf_op jit(solution)/shard_map/left_gather/ppermute | solution.py:38
  145.4 42.0 %all-to-all-start.1 = ((bf16[16,16,896]{2,1,0:T(8,128)(2,1)}), bf16[16,16,896]{2,1,0:T(8,128)(2,1)S(1)}, u32[]{:S(2)}, u32[]{:S(2)}) async-start(bf16[16,16,896]{2,1,0:T(8,128)(2,1)} %input_grad.1), calls=%async_computation.1 | async-start | bytes 917504 | tf_op jit(solution)/shard_map/input_grad/all_to_all | solution.py:311
  171.8 7.2 %collective-permute-start.33 = (f32[64,256]{1,0:T(8,128)S(1)}, f32[64,256]{1,0:T(8,128)S(1)}, u32[]{:S(2)}, u32[]{:S(2)}) collective-permute-start(f32[64,256]{1,0:T(8,128)S(1)} %add_add_fusion.s0), channel_id=1, source_target_pairs={{0,192},{64,128},{128,64},{192,0},{1,193},{65,129},{129,65},{193,1... | collective-permute-start | bytes 196616 | tf_op jit(solution)/shard_map/right/ppermute | solution.py:42
  171.9 7.1 %collective-permute-start.32 = (f32[64,256]{1,0:T(8,128)S(1)}, f32[64,256]{1,0:T(8,128)S(1)}, u32[]{:S(2)}, u32[]{:S(2)}) collective-permute-start(f32[64,256]{1,0:T(8,128)S(1)} %add_add_fusion.s0), channel_id=1, source_target_pairs={{0,128},{64,192},{128,0},{192,64},{1,129},{65,193},{129,1},{193,65... | collective-permute-start | bytes 196616 | tf_op jit(solution)/shard_map/right/ppermute | solution.py:42
  (10 other events, 37.4 us)
Sparse Core Ops, SparseCore 0:
  65.9 35.0 all-gather.4
  102.8 32.4 all-gather.6

commit v4 on v3

--- a/solution.py
+++ b/solution.py
@@ -81,11 +81,6 @@
     a_ref[RANK:, :] = (a - high.astype(F32)).astype(BF)
 
 
-def lay_kernel(blocks, out_ref):
-    for j in range(16):
-        out_ref[:, BLOCK * j : BLOCK * (j + 1)] = blocks[j]
-
-
 def left_kernel(table, a_ref, *refs):
     hidden, outs = refs[:4], refs[4:]
     a = a_ref[...]
@@ -134,31 +129,39 @@
     out_ref[...] = eliminate(jnp.concatenate([gram[...], eye.astype(F32)], axis=1), 0, RANK // 2)
 
 
-def lower_kernel(both, out_ref):
-    out_ref[...] = eliminate(both[...], RANK // 2, RANK)[:, RANK:]
-
-
-def error_kernel(inverse, s0, s1, s2, s3, grad, left, h0, h1, h2, h3, right_ref, out_ref, weights):
+def lower_kernel(both, out_ref, square_ref):
+    inverse = eliminate(both[...], RANK // 2, RANK)[:, RANK:]
+    out_ref[...] = inverse
+    square_ref[...] = lax.dot_general(
+        inverse, inverse, (((0,), (0,)), ((), ())), precision=HIGH, preferred_element_type=F32
+    )
+
+
+def error_kernel(
+    inverse, square, s0, s1, s2, s3, grad, blocks, left, h0, h1, h2, h3, right_ref, out_ref, laid_ref, weights
+):
     @pl.when(pl.program_id(0) == 0)
     def _():
-        summed = (s0[...] + s1[...]) + (s2[...] + s3[...])
-        inv = inverse[...]
-        right = lax.dot_general(
-            inv, summed, (((1,), (0,)), ((), ())), precision=HIGH, preferred_element_type=F32
-        ) * (1.0 / 16)
-        right_ref[...] = right
-        m = -lax.dot_general(inv, right, (((0,), (0,)), ((), ())), precision=HIGH, preferred_element_type=F32)
+        summed = ((s0[...] + s1[...]) + (s2[...] + s3[...])) * (1.0 / 16)
+        right_ref[...] = lax.dot_general(
+            inverse[...], summed, (((1,), (0,)), ((), ())), precision=HIGH, preferred_element_type=F32
+        )
+        m = -lax.dot_general(
+            square[...], summed, (((1,), (0,)), ((), ())), precision=HIGH, preferred_element_type=F32
+        )
         high = m.astype(BF)
         weights[:TOKENS, :] = grad[...]
         weights[TOKENS : TOKENS + RANK, :] = high
         weights[TOKENS + RANK :, :] = (m - high.astype(F32)).astype(BF)
 
+    for j in range(STEP // BLOCK):
+        laid_ref[:, BLOCK * j : BLOCK * (j + 1)] = blocks[j]
     block = left[...]
     rows = jnp.concatenate([h0[...], h1[...], h2[...], h3[...], block, block], axis=0)
     out_ref[...] = dot(rows, weights[...], 0, 0).astype(BF)
 
 
-def error_of(inverse, sums, grad, left, hidden):
+def error_of(inverse, square, sums, grad, blocks, left, hidden):
     def whole(a):
         return pl.BlockSpec(a.shape, lambda i: (0, 0))
 
@@ -167,12 +170,20 @@
 
     return pl.pallas_call(
         error_kernel,
-        out_shape=(jax.ShapeDtypeStruct((RANK, COLS), F32), jax.ShapeDtypeStruct((F, COLS), BF)),
+        out_shape=(
+            jax.ShapeDtypeStruct((RANK, COLS), F32),
+            jax.ShapeDtypeStruct((F, COLS), BF),
+            jax.ShapeDtypeStruct((16, F), BF),
+        ),
         grid=(F // STEP,),
-        in_specs=[whole(inverse)] + [whole(s) for s in sums] + [whole(grad), some(left)] + [some(h) for h in hidden],
+        in_specs=[whole(inverse), whole(square)]
+        + [whole(s) for s in sums]
+        + [whole(grad), pl.BlockSpec((STEP // BLOCK, 16, BLOCK), lambda i: (i, 0, 0)), some(left)]
+        + [some(h) for h in hidden],
         out_specs=(
             pl.BlockSpec((RANK, COLS), lambda i: (0, 0)),
             pl.BlockSpec((STEP, COLS), lambda i: (i, 0)),
+            pl.BlockSpec((16, STEP), lambda i: (0, i)),
         ),
         scratch_shapes=[pltpu.VMEM((TOKENS + 2 * RANK, COLS), BF)],
         compiler_params=LIMIT,
@@ -182,7 +193,7 @@
             transcendentals=0,
         ),
         name="error_new",
-    )(inverse, *sums, grad, left, *hidden)
+    )(inverse, square, *sums, grad, blocks, left, *hidden)
 
 
 def input_kernel(group, shard, t0, t1, t2, t3, near, far, out_ref):
@@ -303,14 +314,12 @@
             local = local + v
         local, half = lax.optimization_barrier((local, half))
         sums = [local] + flip3(local)
-        inverse = call(lower_kernel, [((RANK, RANK), F32)], [], [half], 64 * 64 * 128, "inverse_lower")[0]
-    with jax.named_scope("error_new"):
-        right, error_new = error_of(inverse, sums, grad_rows, left, hidden)
-
+        inverse, square = call(lower_kernel, [((RANK, RANK), F32)] * 2, [], [half], 64 * 64 * 128, "inverse_lower")
     with jax.named_scope("input_grad"):
         summed = lax.all_to_all(partial, ("zl", "x"), 0, 0)
-        input_grad = call(lay_kernel, [((16, F), BF)], [], [summed], 16 * F, "lay")[0][None]
-    return input_grad, right, error_new[None]
+    with jax.named_scope("error_new"):
+        right, error_new, laid = error_of(inverse, square, sums, grad_rows, summed, left, hidden)
+    return laid[None], right, error_new[None]
 
 
 def solution(mesh):

time: 198 us -> 201 us (1.015)
  local copies, waits for them, and re-layouts: 5.43 us -> 9.68 us
    unnamed x8 -> x14, local copies, waits for them, and re-layouts: 4.74 us -> 9 us
    pallas_call x7 -> x6, Pallas kernels: 15.8 us -> 15.2 us  [call(): pl.pallas_call(kernel, out_shape=[jax.ShapeDtypeStruct(s, d) for s, d in...]
  transfers between devices with their start and end apart: 38 -> 38, of which waited for: 20 -> 20; matrix products, arithmetic and copies ran while one was open for 3% -> 3% of each run, Pallas kernels for 17% -> 12%
where the time goes in v4:
time: 201 us; the launch traced here: 199 us
  starting transfers between devices  82.5 us (41%)
  waiting for transfers between devices  54 us (27%)
  Pallas kernels  32.6 us (16%)
  between operations  14.3 us (7%)
  local copies, waits for them, and re-layouts  9.68 us (5%)
  other arithmetic  5.59 us (3%)
    ppermute x12, waiting for transfers between devices, ring3(): return [lax.ppermute(value, axis, shift(-s)) for s in (1, 2, 3)]  23 us
    ppermute x9, starting transfers between devices, flip3(): return [lax.ppermute(value, 'zl', flip(s)) for s in (1, 2, 3)]  22.2 us
    ppermute x12, starting transfers between devices, ring3(): return [lax.ppermute(value, axis, shift(-s)) for s in (1, 2, 3)]  15.2 us
    pallas_call x6, Pallas kernels, call(): pl.pallas_call(kernel, out_shape=[jax.ShapeDtypeStruct(s, d) for s, d in...  15.2 us
    ppermute x9, waiting for transfers between devices, flip3(): return [lax.ppermute(value, 'zl', flip(s)) for s in (1, 2, 3)]  12.6 us
    pallas_call x1, Pallas kernels, input_of(): pl.pallas_call(input_kernel, out_shape=jax.ShapeDtypeStruct((16, 16, BLOC...  9.13 us
    unnamed x14, local copies, waits for them, and re-layouts  9 us
    ppermute x1, starting transfers between devices, on_device(): far_weight = lax.ppermute(after(down_weight, near), 'zh', SWAP)  8.75 us
  transfers between devices with their start and end apart: 38, of which 20 were waited for; matrix products, arithmetic and copies ran while one was open for 3% of the time, Pallas kernels for 12%

profile of v4, /device:TPU:16, one launch (start us, length us, event | category | flops | bytes accessed | tf_op | source)
XLA Modules:
  0.0 198.6 jit_solution(4733911555804026960)
XLA Ops:
  9.4 2.5 %collective-permute-start = (bf16[16,14336]{1,0:T(8,128)(2,1)}, bf16[16,14336]{1,0:T(8,128)(2,1)}, u32[]{:S(2)}, u32[]{:S(2)}) collective-permute-start(bf16[16,14336]{1,0:T(8,128)(2,1)} %bitcast.21), channel_id=1, source_target_pairs={{0,12},{4,0},{8,4},{12,8},{1,13},{5,1},{9,5},{13,9},{2,14},{6,2},{... | collective-permute-start | bytes 1376264 | tf_op jit(solution)/shard_map/hidden_gather/ppermute | solution.py:38
  11.9 5.5 %collective-permute-start.3 = (bf16[16,14336]{1,0:T(8,128)(2,1)}, bf16[16,14336]{1,0:T(8,128)(2,1)S(1)}, u32[]{:S(2)}, u32[]{:S(2)}) collective-permute-start(bf16[16,14336]{1,0:T(8,128)(2,1)} %bitcast.22), channel_id=1, source_target_pairs={{0,2},{2,0},{1,3},{3,1},{4,6},{6,4},{5,7},{7,5},{8,10},{10,8},{9,1... | collective-permute-start | bytes 1376264 | tf_op jit(solution)/shard_map/hidden_gather/ppermute | solution.py:245
  17.4 6.5 %all-to-all-start = ((bf16[16,16,256]{2,1,0:T(8,128)(2,1)}), bf16[16,16,256]{2,1,0:T(8,128)(2,1)S(1)}, u32[]{:S(2)}, u32[]{:S(2)}) async-start(bf16[16,16,256]{2,1,0:T(8,128)(2,1)} %bitcast.14), calls=%async_computation | async-start | bytes 262144 | tf_op jit(solution)/shard_map/grad_gather/all_to_all | solution.py:248
  29.9 2.5 %collective-permute-done = bf16[16,14336]{1,0:T(8,128)(2,1)} collective-permute-done((bf16[16,14336]{1,0:T(8,128)(2,1)}, bf16[16,14336]{1,0:T(8,128)(2,1)}, u32[]{:S(2)}, u32[]{:S(2)}) %collective-permute-start) | collective-permute-done | bytes 458784 | tf_op jit(solution)/shard_map/hidden_gather/ppermute | solution.py:38
  36.8 8.8 %collective-permute-start.7 = (bf16[896,256]{1,0:T(8,128)(2,1)}, bf16[896,256]{1,0:T(8,128)(2,1)}, u32[]{:S(2)}, u32[]{:S(2)}) collective-permute-start(bf16[896,256]{1,0:T(8,128)(2,1)} %param.6), channel_id=1, source_target_pairs={{0,2},{2,0},{1,3},{3,1},{4,6},{6,4},{5,7},{7,5},{8,10},{10,8},{9,1... | collective-permute-start | bytes 1376264 | tf_op jit(solution)/shard_map/weight_gather/ppermute | solution.py:251
  45.5 9.0 %collective-permute-done.5 = bf16[16,14336]{1,0:T(8,128)(2,1)S(1)} collective-permute-done((bf16[16,14336]{1,0:T(8,128)(2,1)S(1)}, bf16[16,14336]{1,0:T(8,128)(2,1)S(1)}, u32[]{:S(2)}, u32[]{:S(2)}) %collective-permute-start.5) | collective-permute-done | bytes 458784 | tf_op jit(solution)/shard_map/hidden_gather/ppermute | solution.py:38
  55.7 2.4 %pad_maximum_fusion.1.refs_1_.refs_5_.h1 = bf16[64,14336]{1,0:T(8,128)(2,1)} fusion(bf16[16,14336]{1,0:T(8,128)(2,1)S(1)} %collective-permute-done.6, bf16[16,14336]{1,0:T(8,128)(2,1)S(1)} %collective-permute-done.5, bf16[16,14336]{1,0:T(8,128)(2,1)} %collective-permute-done.4, bf16[16,14336]{1,0:T(8,128)(2,1)S(1)} %collective-permute-done.3), kind=kLoop, calls=%fused_computation.1 | loop fusion | flops 7340032 | bytes 3670016 | tf_op jit(solution)/shard_map/hidden_gather/concatenate | solution.py:253
  58.1 7.7 %collective-permute-done.7 = bf16[896,256]{1,0:T(8,128)(2,1)} collective-permute-done((bf16[896,256]{1,0:T(8,128)(2,1)}, bf16[896,256]{1,0:T(8,128)(2,1)}, u32[]{:S(2)}, u32[]{:S(2)}) %collective-permute-start.7) | collective-permute-done | bytes 458784 | tf_op jit(solution)/shard_map/weight_gather/ppermute | solution.py:251
  66.9 3.9 %collective-permute-done.9.refs_3_.refs_7_.h3 = bf16[64,14336]{1,0:T(8,128)(2,1)} collective-permute-done((bf16[64,14336]{1,0:T(8,128)(2,1)}, bf16[64,14336]{1,0:T(8,128)(2,1)}, u32[]{:S(2)}, u32[]{:S(2)}) %collective-permute-start.9) | collective-permute-done | bytes 1835040 | tf_op jit(solution)/shard_map/hidden_gather/ppermute | solution.py:257
  72.3 3.4 %left.1 = (bf16[4,64,896]{2,1,0:T(8,128)(2,1)S(1)}, bf16[4,64,896]{2,1,0:T(8,128)(2,1)S(1)}, bf16[4,64,896]{2,1,0:T(8,128)(2,1)S(1)}, bf16[4,64,896]{2,1,0:T(8,128)(2,1)S(1)}) custom-call(s32[16]{0:T(128)S(1)} %add.163.table, bf16[128,256]{1,0:T(8,128)(2,1)S(1)} %get-tuple-element.52.a_ref, bf16[64,14336]{1,0:T(8,128)(2,1)S(1)} %pad_maximum_fusion.refs_0_.refs_4_.h0, ...), custom_call_target="tpu_custom_call" | custom-call | flops 939524096 | bytes 7405568 | tf_op jit(solution)/shard_map/left_reduce/left/pallas_call | solution.py:63
  77.2 2.7 %collective-permute-start.11 = (bf16[4,64,896]{2,1,0:T(8,128)(2,1)S(1)}, bf16[4,64,896]{2,1,0:T(8,128)(2,1)S(1)}, u32[]{:S(2)}, u32[]{:S(2)}) collective-permute-start(bf16[4,64,896]{2,1,0:T(8,128)(2,1)S(1)} %get-tuple-element.61), channel_id=1, source_target_pairs={{0,32},{16,48},{32,0},{48,16},{1,33},{17,49},{33,1},{49,17},{2,34}... | collective-permute-start | bytes 1376264 | tf_op jit(solution)/shard_map/left_reduce/ppermute | solution.py:272
  81.4 5.8 %collective-permute-start.14 = (bf16[16,16,256]{2,1,0:T(8,128)(2,1)S(1)}, bf16[16,16,256]{2,1,0:T(8,128)(2,1)S(1)}, u32[]{:S(2)}, u32[]{:S(2)}) collective-permute-start(bf16[16,16,256]{2,1,0:T(8,128)(2,1)S(1)} %all-to-all-done), channel_id=1, source_target_pairs={{0,128},{64,192},{128,0},{192,64},{1,129},{65,193},{129,1},{193,65... | collective-permute-start | bytes 393224 | tf_op jit(solution)/shard_map/left_reduce/ppermute | solution.py:42
  88.4 6.1 %collective-permute-start.13 = (bf16[16,16,256]{2,1,0:T(8,128)(2,1)S(1)}, bf16[16,16,256]{2,1,0:T(8,128)(2,1)S(1)}, u32[]{:S(2)}, u32[]{:S(2)}) collective-permute-start(bf16[16,16,256]{2,1,0:T(8,128)(2,1)S(1)} %all-to-all-done), channel_id=1, source_target_pairs={{0,64},{64,0},{128,192},{192,128},{1,65},{65,1},{129,193},{193,129... | collective-permute-start | bytes 393224 | tf_op jit(solution)/shard_map/left_reduce/ppermute | solution.py:42
  94.4 2.3 %collective-permute-done.14 = bf16[16,16,256]{2,1,0:T(8,128)(2,1)S(1)} collective-permute-done((bf16[16,16,256]{2,1,0:T(8,128)(2,1)S(1)}, bf16[16,16,256]{2,1,0:T(8,128)(2,1)S(1)}, u32[]{:S(2)}, u32[]{:S(2)}) %collective-permute-start.14) | collective-permute-done | bytes 131104 | tf_op jit(solution)/shard_map/left_reduce/ppermute | solution.py:42
  96.7 2.7 %collective-permute-done.13 = bf16[16,16,256]{2,1,0:T(8,128)(2,1)S(1)} collective-permute-done((bf16[16,16,256]{2,1,0:T(8,128)(2,1)S(1)}, bf16[16,16,256]{2,1,0:T(8,128)(2,1)S(1)}, u32[]{:S(2)}, u32[]{:S(2)}) %collective-permute-start.13) | collective-permute-done | bytes 131104 | tf_op jit(solution)/shard_map/left_reduce/ppermute | solution.py:42
  103.9 3.2 %collective-permute-start.17 = (bf16[64,896]{1,0:T(8,128)(2,1)S(1)}, bf16[64,896]{1,0:T(8,128)(2,1)S(1)}, u32[]{:S(2)}, u32[]{:S(2)}) collective-permute-start(bf16[64,896]{1,0:T(8,128)(2,1)S(1)} %get-tuple-element.71), channel_id=1, source_target_pairs={{0,128},{64,192},{128,0},{192,64},{1,129},{65,193},{129,1},{193,65... | collective-permute-start | bytes 344072 | tf_op jit(solution)/shard_map/left_reduce/ppermute | solution.py:286
  107.0 3.6 %collective-permute-start.18 = (bf16[64,896]{1,0:T(8,128)(2,1)S(1)}, bf16[64,896]{1,0:T(8,128)(2,1)S(1)}, u32[]{:S(2)}, u32[]{:S(2)}) collective-permute-start(bf16[64,896]{1,0:T(8,128)(2,1)S(1)} %get-tuple-element.72), channel_id=1, source_target_pairs={{0,192},{64,128},{128,64},{192,0},{1,193},{65,129},{129,65},{193,1... | collective-permute-start | bytes 344072 | tf_op jit(solution)/shard_map/left_reduce/ppermute | solution.py:286
  110.6 3.2 %collective-permute-done.17 = bf16[64,896]{1,0:T(8,128)(2,1)S(1)} collective-permute-done((bf16[64,896]{1,0:T(8,128)(2,1)S(1)}, bf16[64,896]{1,0:T(8,128)(2,1)S(1)}, u32[]{:S(2)}, u32[]{:S(2)}) %collective-permute-start.17) | collective-permute-done | bytes 114720 | tf_op jit(solution)/shard_map/left_reduce/ppermute | solution.py:286
  113.8 2.5 %collective-permute-done.18 = bf16[64,896]{1,0:T(8,128)(2,1)S(1)} collective-permute-done((bf16[64,896]{1,0:T(8,128)(2,1)S(1)}, bf16[64,896]{1,0:T(8,128)(2,1)S(1)}, u32[]{:S(2)}, u32[]{:S(2)}) %collective-permute-start.18) | collective-permute-done | bytes 114720 | tf_op jit(solution)/shard_map/left_reduce/ppermute | solution.py:286
  118.3 2.2 %collective-permute-start.23 = (bf16[64,896]{1,0:T(8,128)(2,1)S(1)}, bf16[64,896]{1,0:T(8,128)(2,1)S(1)}, u32[]{:S(2)}, u32[]{:S(2)}) collective-permute-start(bf16[64,896]{1,0:T(8,128)(2,1)S(1)} %multiply_convert_fusion), channel_id=1, source_target_pairs={{0,192},{64,128},{128,64},{192,0},{1,193},{65,129},{129,65},{193,1... | collective-permute-start | bytes 344072 | tf_op jit(solution)/shard_map/left_gather/ppermute | solution.py:42
  120.5 3.6 %collective-permute-start.22 = (bf16[64,896]{1,0:T(8,128)(2,1)S(1)}, bf16[64,896]{1,0:T(8,128)(2,1)S(1)}, u32[]{:S(2)}, u32[]{:S(2)}) collective-permute-start(bf16[64,896]{1,0:T(8,128)(2,1)S(1)} %multiply_convert_fusion), channel_id=1, source_target_pairs={{0,128},{64,192},{128,0},{192,64},{1,129},{65,193},{129,1},{193,65... | collective-permute-start | bytes 344072 | tf_op jit(solution)/shard_map/left_gather/ppermute | solution.py:42
  125.8 6.1 %collective-permute-done.22 = bf16[64,896]{1,0:T(8,128)(2,1)S(1)} collective-permute-done((bf16[64,896]{1,0:T(8,128)(2,1)S(1)}, bf16[64,896]{1,0:T(8,128)(2,1)S(1)}, u32[]{:S(2)}, u32[]{:S(2)}) %collective-permute-start.22) | collective-permute-done | bytes 114720 | tf_op jit(solution)/shard_map/left_gather/ppermute | solution.py:42
  135.8 9.1 %input_grad.1 = bf16[16,16,896]{2,1,0:T(8,128)(2,1)} custom-call(s32[16]{0:T(128)} %add.183.group, s32[16]{0:T(128)} %pad_add_fusion.1.shard, bf16[4,16,16,256]{3,2,1,0:T(8,128)(2,1)} %pad_maximum_fusion.2.t0, bf16[4,16,16,256]{3,2,1,0:T(8,128)(2,1)} %collective-permute-done.19.t1, bf16[4,16,16,256]{3,2,1,0:T(8,128)(2,1)} %collective-permute-done.24.t2, ...), custom_call_target="tpu_custom_call" | custom-call | flops 1879048192 | bytes 10485760 | tf_op jit(solution)/shard_map/input_grad/input_grad/pallas_call | solution.py:210
  144.9 6.8 %all-to-all-start.1 = ((bf16[16,16,896]{2,1,0:T(8,128)(2,1)}), bf16[16,16,896]{2,1,0:T(8,128)(2,1)S(1)}, u32[]{:S(2)}, u32[]{:S(2)}) async-start(bf16[16,16,896]{2,1,0:T(8,128)(2,1)} %input_grad.1), calls=%async_computation.1 | async-start | bytes 917504 | tf_op jit(solution)/shard_map/input_grad/all_to_all | solution.py:319
  151.7 3.3 %collective-permute-done.27.refs_3_ = bf16[4,64,896]{2,1,0:T(8,128)(2,1)S(1)} collective-permute-done((bf16[4,64,896]{2,1,0:T(8,128)(2,1)S(1)}, bf16[4,64,896]{2,1,0:T(8,128)(2,1)S(1)}, u32[]{:S(2)}, u32[]{:S(2)}) %collective-permute-start.27) | collective-permute-done | bytes 458784 | tf_op jit(solution)/shard_map/left_gather/ppermute | solution.py:38
  155.1 2.3 %collective-permute-done.25.refs_1_ = bf16[4,64,896]{2,1,0:T(8,128)(2,1)} collective-permute-done((bf16[4,64,896]{2,1,0:T(8,128)(2,1)S(1)}, bf16[4,64,896]{2,1,0:T(8,128)(2,1)}, u32[]{:S(2)}, u32[]{:S(2)}) %collective-permute-start.25) | collective-permute-done | bytes 458784 | tf_op jit(solution)/shard_map/left_gather/ppermute | solution.py:38
  158.8 5.2 %stats.1 = (bf16[64,14336]{1,0:T(8,128)(2,1)S(1)}, f32[64,256]{1,0:T(8,128)S(1)}, f32[64,64]{1,0:T(8,128)S(1)}) custom-call(s32[16]{0:T(128)S(1)} %add.163.table, bf16[4,64,896]{2,1,0:T(8,128)(2,1)S(1)} %pad_maximum_fusion.3.refs_0_, bf16[4,64,896]{2,1,0:T(8,128)(2,1)} %collective-permute-done.25.refs_1_, ...), custom_call_target="tpu_custom_call" | custom-call | flops 587202560 | bytes 9306112 | tf_op jit(solution)/shard_map/stats/stats/pallas_call | solution.py:63
  165.3 3.5 %collective-permute-start.29 = (f32[64,256]{1,0:T(8,128)S(1)}, f32[64,256]{1,0:T(8,128)S(1)}, u32[]{:S(2)}, u32[]{:S(2)}) collective-permute-start(f32[64,256]{1,0:T(8,128)S(1)} %get-tuple-element.89), channel_id=1, source_target_pairs={{0,32},{16,48},{32,0},{48,16},{1,33},{17,49},{33,1},{49,17},{2,34}... | collective-permute-start | bytes 196616 | tf_op jit(solution)/shard_map/right/ppermute | solution.py:38
  168.8 2.7 %inverse_upper.1.both = f32[64,128]{1,0:T(8,128)S(1)} custom-call(f32[64,64]{1,0:T(8,128)S(1)} %get-tuple-element.90.gram), custom_call_target="tpu_custom_call" | custom-call | flops 524288 | bytes 16384 | tf_op jit(solution)/shard_map/right/inverse_upper/pallas_call | solution.py:63
  174.7 2.8 %collective-permute-start.31 = (f32[64,256]{1,0:T(8,128)S(1)}, f32[64,256]{1,0:T(8,128)S(1)}, u32[]{:S(2)}, u32[]{:S(2)}) collective-permute-start(f32[64,256]{1,0:T(8,128)S(1)} %add_add_fusion.s0), channel_id=1, source_target_pairs={{0,64},{64,0},{128,192},{192,128},{1,65},{65,1},{129,193},{193,129... | collective-permute-start | bytes 196616 | tf_op jit(solution)/shard_map/right/ppermute | solution.py:42
  177.6 2.9 %inverse_lower.1 = (f32[64,64]{1,0:T(8,128)S(1)}, f32[64,64]{1,0:T(8,128)S(1)}) custom-call(f32[64,128]{1,0:T(8,128)S(1)} %inverse_upper.1.both), custom_call_target="tpu_custom_call" | custom-call | flops 524288 | bytes 32768 | tf_op jit(solution)/shard_map/right/inverse_lower/pallas_call | solution.py:63
  183.5 8.3 %error_new.1 = (f32[64,256]{1,0:T(8,128)}, bf16[14336,256]{1,0:T(8,128)(2,1)}, bf16[16,14336]{1,0:T(8,128)(2,1)}) custom-call(f32[64,64]{1,0:T(8,128)S(1)} %get-tuple-element.92.inverse, f32[64,64]{1,0:T(8,128)S(1)} %get-tuple-element.93.square, f32[64,256]{1,0:T(8,128)S(1)} %add_add_fusion.s0, f32[64,256]{1,0:T(8,128)S(1)} %collective-permute-done.31.s1, ...), custom_call_target="tpu_custom_call" | custom-call | flops 2818572288 | bytes 16515072 | tf_op jit(solution)/shard_map/error_new/error_new/pallas_call | solution.py:171
  (85 shorter events, 41.4 us)
Async XLA Ops:
  7.2 21.1 %collective-permute-start.2 = (bf16[16,14336]{1,0:T(8,128)(2,1)}, bf16[16,14336]{1,0:T(8,128)(2,1)S(1)}, u32[]{:S(2)}, u32[]{:S(2)}) collective-permute-start(bf16[16,14336]{1,0:T(8,128)(2,1)} %bitcast.19), channel_id=1, source_target_pairs={{0,4},{4,8},{8,12},{12,0},{1,5},{5,9},{9,13},{13,1},{2,6},{6,10},{... | collective-permute-start | bytes 1376264 | tf_op jit(solution)/shard_map/hidden_gather/ppermute | solution.py:38
  8.5 21.4 %collective-permute-start.1 = (bf16[16,14336]{1,0:T(8,128)(2,1)}, bf16[16,14336]{1,0:T(8,128)(2,1)S(1)}, u32[]{:S(2)}, u32[]{:S(2)}) collective-permute-start(bf16[16,14336]{1,0:T(8,128)(2,1)} %bitcast.20), channel_id=1, source_target_pairs={{0,8},{4,12},{8,0},{12,4},{1,9},{5,13},{9,1},{13,5},{2,10},{6,14},... | collective-permute-start | bytes 1376264 | tf_op jit(solution)/shard_map/hidden_gather/ppermute | solution.py:38
  9.4 22.9 %collective-permute-start = (bf16[16,14336]{1,0:T(8,128)(2,1)}, bf16[16,14336]{1,0:T(8,128)(2,1)}, u32[]{:S(2)}, u32[]{:S(2)}) collective-permute-start(bf16[16,14336]{1,0:T(8,128)(2,1)} %bitcast.21), channel_id=1, source_target_pairs={{0,12},{4,0},{8,4},{12,8},{1,13},{5,1},{9,5},{13,9},{2,14},{6,2},{... | collective-permute-start | bytes 1376264 | tf_op jit(solution)/shard_map/hidden_gather/ppermute | solution.py:38
  11.9 21.7 %collective-permute-start.3 = (bf16[16,14336]{1,0:T(8,128)(2,1)}, bf16[16,14336]{1,0:T(8,128)(2,1)S(1)}, u32[]{:S(2)}, u32[]{:S(2)}) collective-permute-start(bf16[16,14336]{1,0:T(8,128)(2,1)} %bitcast.22), channel_id=1, source_target_pairs={{0,2},{2,0},{1,3},{3,1},{4,6},{6,4},{5,7},{7,5},{8,10},{10,8},{9,1... | collective-permute-start | bytes 1376264 | tf_op jit(solution)/shard_map/hidden_gather/ppermute | solution.py:245
  17.4 19.4 %all-to-all-start = ((bf16[16,16,256]{2,1,0:T(8,128)(2,1)}), bf16[16,16,256]{2,1,0:T(8,128)(2,1)S(1)}, u32[]{:S(2)}, u32[]{:S(2)}) async-start(bf16[16,16,256]{2,1,0:T(8,128)(2,1)} %bitcast.14), calls=%async_computation | async-start | bytes 262144 | tf_op jit(solution)/shard_map/grad_gather/all_to_all | solution.py:248
  23.9 111.9 %all-gather.5.cloned.1.call-start = ((), (), s32[]{:S(2)}) async-start(), calls=%async_computation.2 | async-start | bytes 4128768 | tf_op jit(solution)/shard_map/weight_gather/all_gather | solution.py:259
  33.6 11.9 %collective-permute-start.6 = (bf16[16,14336]{1,0:T(8,128)(2,1)S(1)}, bf16[16,14336]{1,0:T(8,128)(2,1)S(1)}, u32[]{:S(2)}, u32[]{:S(2)}) collective-permute-start(bf16[16,14336]{1,0:T(8,128)(2,1)S(1)} %collective-permute-done.3), channel_id=1, source_target_pairs={{0,4},{4,8},{8,12},{12,0},{1,5},{5,9},{9,13},{13,1},{2,6},{6,10},{... | collective-permute-start | bytes 1376264 | tf_op jit(solution)/shard_map/hidden_gather/ppermute | solution.py:38
  34.3 20.3 %collective-permute-start.5 = (bf16[16,14336]{1,0:T(8,128)(2,1)S(1)}, bf16[16,14336]{1,0:T(8,128)(2,1)S(1)}, u32[]{:S(2)}, u32[]{:S(2)}) collective-permute-start(bf16[16,14336]{1,0:T(8,128)(2,1)S(1)} %collective-permute-done.3), channel_id=1, source_target_pairs={{0,8},{4,12},{8,0},{12,4},{1,9},{5,13},{9,1},{13,5},{2,10},{6,14},... | collective-permute-start | bytes 1376264 | tf_op jit(solution)/shard_map/hidden_gather/ppermute | solution.py:38
  35.6 20.1 %collective-permute-start.4 = (bf16[16,14336]{1,0:T(8,128)(2,1)S(1)}, bf16[16,14336]{1,0:T(8,128)(2,1)}, u32[]{:S(2)}, u32[]{:S(2)}) collective-permute-start(bf16[16,14336]{1,0:T(8,128)(2,1)S(1)} %collective-permute-done.3), channel_id=1, source_target_pairs={{0,12},{4,0},{8,4},{12,8},{1,13},{5,1},{9,5},{13,9},{2,14},{6,2},{... | collective-permute-start | bytes 1376264 | tf_op jit(solution)/shard_map/hidden_gather/ppermute | solution.py:38
  36.8 29.0 %collective-permute-start.8 = (bf16[64,14336]{1,0:T(8,128)(2,1)S(1)}, bf16[64,14336]{1,0:T(8,128)(2,1)}, u32[]{:S(2)}, u32[]{:S(2)}) collective-permute-start(bf16[64,14336]{1,0:T(8,128)(2,1)S(1)} %pad_maximum_fusion.refs_0_.refs_4_.h0), channel_id=1, source_target_pairs={{0,1},{1,0},{2,3},{3,2},{4,5},{5,4},{6,7},{7,6},{8,9},{9,8},{10,11... | collective-permute-start | bytes 5505032 | tf_op jit(solution)/shard_map/hidden_gather/ppermute | solution.py:255
  36.8 29.0 %collective-permute-start.7 = (bf16[896,256]{1,0:T(8,128)(2,1)}, bf16[896,256]{1,0:T(8,128)(2,1)}, u32[]{:S(2)}, u32[]{:S(2)}) collective-permute-start(bf16[896,256]{1,0:T(8,128)(2,1)} %param.6), channel_id=1, source_target_pairs={{0,2},{2,0},{1,3},{3,1},{4,6},{6,4},{5,7},{7,5},{8,10},{10,8},{9,1... | collective-permute-start | bytes 1376264 | tf_op jit(solution)/shard_map/weight_gather/ppermute | solution.py:251
  65.8 70.0 %all-gather.7.cloned.1.call-start = ((), (), s32[]{:S(2)}) async-start(), calls=%async_computation.3 | async-start | bytes 4128768 | tf_op jit(solution)/shard_map/weight_gather/all_gather | solution.py:260
  75.7 24.6 %collective-permute-start.10 = (bf16[4,64,896]{2,1,0:T(8,128)(2,1)S(1)}, bf16[4,64,896]{2,1,0:T(8,128)(2,1)S(1)}, u32[]{:S(2)}, u32[]{:S(2)}) collective-permute-start(bf16[4,64,896]{2,1,0:T(8,128)(2,1)S(1)} %get-tuple-element.60), channel_id=1, source_target_pairs={{0,16},{16,32},{32,48},{48,0},{1,17},{17,33},{33,49},{49,1},{2,18}... | collective-permute-start | bytes 1376264 | tf_op jit(solution)/shard_map/left_reduce/ppermute | solution.py:272
  77.2 23.1 %collective-permute-start.11 = (bf16[4,64,896]{2,1,0:T(8,128)(2,1)S(1)}, bf16[4,64,896]{2,1,0:T(8,128)(2,1)S(1)}, u32[]{:S(2)}, u32[]{:S(2)}) collective-permute-start(bf16[4,64,896]{2,1,0:T(8,128)(2,1)S(1)} %get-tuple-element.61), channel_id=1, source_target_pairs={{0,32},{16,48},{32,0},{48,16},{1,33},{17,49},{33,1},{49,17},{2,34}... | collective-permute-start | bytes 1376264 | tf_op jit(solution)/shard_map/left_reduce/ppermute | solution.py:272
  79.9 20.4 %collective-permute-start.12 = (bf16[4,64,896]{2,1,0:T(8,128)(2,1)S(1)}, bf16[4,64,896]{2,1,0:T(8,128)(2,1)S(1)}, u32[]{:S(2)}, u32[]{:S(2)}) collective-permute-start(bf16[4,64,896]{2,1,0:T(8,128)(2,1)S(1)} %get-tuple-element.62), channel_id=1, source_target_pairs={{0,48},{16,0},{32,16},{48,32},{1,49},{17,1},{33,17},{49,33},{2,50}... | collective-permute-start | bytes 1376264 | tf_op jit(solution)/shard_map/left_reduce/ppermute | solution.py:272
  81.4 7.0 %collective-permute-start.15 = (bf16[16,16,256]{2,1,0:T(8,128)(2,1)S(1)}, bf16[16,16,256]{2,1,0:T(8,128)(2,1)S(1)}, u32[]{:S(2)}, u32[]{:S(2)}) collective-permute-start(bf16[16,16,256]{2,1,0:T(8,128)(2,1)S(1)} %all-to-all-done), channel_id=1, source_target_pairs={{0,192},{64,128},{128,64},{192,0},{1,193},{65,129},{129,65},{193,1... | collective-permute-start | bytes 393224 | tf_op jit(solution)/shard_map/left_reduce/ppermute | solution.py:42
  81.4 15.3 %collective-permute-start.14 = (bf16[16,16,256]{2,1,0:T(8,128)(2,1)S(1)}, bf16[16,16,256]{2,1,0:T(8,128)(2,1)S(1)}, u32[]{:S(2)}, u32[]{:S(2)}) collective-permute-start(bf16[16,16,256]{2,1,0:T(8,128)(2,1)S(1)} %all-to-all-done), channel_id=1, source_target_pairs={{0,128},{64,192},{128,0},{192,64},{1,129},{65,193},{129,1},{193,65... | collective-permute-start | bytes 393224 | tf_op jit(solution)/shard_map/left_reduce/ppermute | solution.py:42
  88.4 11.0 %collective-permute-start.13 = (bf16[16,16,256]{2,1,0:T(8,128)(2,1)S(1)}, bf16[16,16,256]{2,1,0:T(8,128)(2,1)S(1)}, u32[]{:S(2)}, u32[]{:S(2)}) collective-permute-start(bf16[16,16,256]{2,1,0:T(8,128)(2,1)S(1)} %all-to-all-done), channel_id=1, source_target_pairs={{0,64},{64,0},{128,192},{192,128},{1,65},{65,1},{129,193},{193,129... | collective-permute-start | bytes 393224 | tf_op jit(solution)/shard_map/left_reduce/ppermute | solution.py:42
  100.5 16.2 %collective-permute-start.20 = (bf16[4,16,16,256]{3,2,1,0:T(8,128)(2,1)}, bf16[4,16,16,256]{3,2,1,0:T(8,128)(2,1)}, u32[]{:S(2)}, u32[]{:S(2)}) collective-permute-start(bf16[4,16,16,256]{3,2,1,0:T(8,128)(2,1)} %pad_maximum_fusion.2.t0), channel_id=1, source_target_pairs={{0,16},{16,32},{32,48},{48,0},{1,17},{17,33},{33,49},{49,1},{2,18}... | collective-permute-start | bytes 1572872 | tf_op jit(solution)/shard_map/left_reduce/ppermute | solution.py:284
  102.0 14.7 %collective-permute-start.19 = (bf16[4,16,16,256]{3,2,1,0:T(8,128)(2,1)}, bf16[4,16,16,256]{3,2,1,0:T(8,128)(2,1)}, u32[]{:S(2)}, u32[]{:S(2)}) collective-permute-start(bf16[4,16,16,256]{3,2,1,0:T(8,128)(2,1)} %pad_maximum_fusion.2.t0), channel_id=1, source_target_pairs={{0,48},{16,0},{32,16},{48,32},{1,49},{17,1},{33,17},{49,33},{2,50}... | collective-permute-start | bytes 1572872 | tf_op jit(solution)/shard_map/left_reduce/ppermute | solution.py:284
  103.9 10.0 %collective-permute-start.17 = (bf16[64,896]{1,0:T(8,128)(2,1)S(1)}, bf16[64,896]{1,0:T(8,128)(2,1)S(1)}, u32[]{:S(2)}, u32[]{:S(2)}) collective-permute-start(bf16[64,896]{1,0:T(8,128)(2,1)S(1)} %get-tuple-element.71), channel_id=1, source_target_pairs={{0,128},{64,192},{128,0},{192,64},{1,129},{65,193},{129,1},{193,65... | collective-permute-start | bytes 344072 | tf_op jit(solution)/shard_map/left_reduce/ppermute | solution.py:286
  107.0 9.3 %collective-permute-start.18 = (bf16[64,896]{1,0:T(8,128)(2,1)S(1)}, bf16[64,896]{1,0:T(8,128)(2,1)S(1)}, u32[]{:S(2)}, u32[]{:S(2)}) collective-permute-start(bf16[64,896]{1,0:T(8,128)(2,1)S(1)} %get-tuple-element.72), channel_id=1, source_target_pairs={{0,192},{64,128},{128,64},{192,0},{1,193},{65,129},{129,65},{193,1... | collective-permute-start | bytes 344072 | tf_op jit(solution)/shard_map/left_reduce/ppermute | solution.py:286
  116.7 15.2 %collective-permute-start.24 = (bf16[4,16,16,256]{3,2,1,0:T(8,128)(2,1)}, bf16[4,16,16,256]{3,2,1,0:T(8,128)(2,1)}, u32[]{:S(2)}, u32[]{:S(2)}) collective-permute-start(bf16[4,16,16,256]{3,2,1,0:T(8,128)(2,1)} %pad_maximum_fusion.2.t0), channel_id=1, source_target_pairs={{0,32},{16,48},{32,0},{48,16},{1,33},{17,49},{33,1},{49,17},{2,34}... | collective-permute-start | bytes 1572872 | tf_op jit(solution)/shard_map/left_gather/ppermute | solution.py:289
  118.3 7.5 %collective-permute-start.23 = (bf16[64,896]{1,0:T(8,128)(2,1)S(1)}, bf16[64,896]{1,0:T(8,128)(2,1)S(1)}, u32[]{:S(2)}, u32[]{:S(2)}) collective-permute-start(bf16[64,896]{1,0:T(8,128)(2,1)S(1)} %multiply_convert_fusion), channel_id=1, source_target_pairs={{0,192},{64,128},{128,64},{192,0},{1,193},{65,129},{129,65},{193,1... | collective-permute-start | bytes 344072 | tf_op jit(solution)/shard_map/left_gather/ppermute | solution.py:42
  120.5 11.4 %collective-permute-start.22 = (bf16[64,896]{1,0:T(8,128)(2,1)S(1)}, bf16[64,896]{1,0:T(8,128)(2,1)S(1)}, u32[]{:S(2)}, u32[]{:S(2)}) collective-permute-start(bf16[64,896]{1,0:T(8,128)(2,1)S(1)} %multiply_convert_fusion), channel_id=1, source_target_pairs={{0,128},{64,192},{128,0},{192,64},{1,129},{65,193},{129,1},{193,65... | collective-permute-start | bytes 344072 | tf_op jit(solution)/shard_map/left_gather/ppermute | solution.py:42
  124.1 7.7 %collective-permute-start.21 = (bf16[64,896]{1,0:T(8,128)(2,1)S(1)}, bf16[64,896]{1,0:T(8,128)(2,1)S(1)}, u32[]{:S(2)}, u32[]{:S(2)}) collective-permute-start(bf16[64,896]{1,0:T(8,128)(2,1)S(1)} %multiply_convert_fusion), channel_id=1, source_target_pairs={{0,64},{64,0},{128,192},{192,128},{1,65},{65,1},{129,193},{193,129... | collective-permute-start | bytes 344072 | tf_op jit(solution)/shard_map/left_gather/ppermute | solution.py:42
  132.0 23.1 %collective-permute-start.27 = (bf16[4,64,896]{2,1,0:T(8,128)(2,1)S(1)}, bf16[4,64,896]{2,1,0:T(8,128)(2,1)S(1)}, u32[]{:S(2)}, u32[]{:S(2)}) collective-permute-start(bf16[4,64,896]{2,1,0:T(8,128)(2,1)S(1)} %pad_maximum_fusion.3.refs_0_), channel_id=1, source_target_pairs={{0,16},{16,32},{32,48},{48,0},{1,17},{17,33},{33,49},{49,1},{2,18}... | collective-permute-start | bytes 1376264 | tf_op jit(solution)/shard_map/left_gather/ppermute | solution.py:38
  133.0 22.0 %collective-permute-start.26 = (bf16[4,64,896]{2,1,0:T(8,128)(2,1)S(1)}, bf16[4,64,896]{2,1,0:T(8,128)(2,1)}, u32[]{:S(2)}, u32[]{:S(2)}) collective-permute-start(bf16[4,64,896]{2,1,0:T(8,128)(2,1)S(1)} %pad_maximum_fusion.3.refs_0_), channel_id=1, source_target_pairs={{0,32},{16,48},{32,0},{48,16},{1,33},{17,49},{33,1},{49,17},{2,34}... | collective-permute-start | bytes 1376264 | tf_op jit(solution)/shard_map/left_gather/ppermute | solution.py:38
  135.1 22.2 %collective-permute-start.25 = (bf16[4,64,896]{2,1,0:T(8,128)(2,1)S(1)}, bf16[4,64,896]{2,1,0:T(8,128)(2,1)}, u32[]{:S(2)}, u32[]{:S(2)}) collective-permute-start(bf16[4,64,896]{2,1,0:T(8,128)(2,1)S(1)} %pad_maximum_fusion.3.refs_0_), channel_id=1, source_target_pairs={{0,48},{16,0},{32,16},{48,32},{1,49},{17,1},{33,17},{49,33},{2,50}... | collective-permute-start | bytes 1376264 | tf_op jit(solution)/shard_map/left_gather/ppermute | solution.py:38
  144.9 35.5 %all-to-all-start.1 = ((bf16[16,16,896]{2,1,0:T(8,128)(2,1)}), bf16[16,16,896]{2,1,0:T(8,128)(2,1)S(1)}, u32[]{:S(2)}, u32[]{:S(2)}) async-start(bf16[16,16,896]{2,1,0:T(8,128)(2,1)} %input_grad.1), calls=%async_computation.1 | async-start | bytes 917504 | tf_op jit(solution)/shard_map/input_grad/all_to_all | solution.py:319
  173.1 7.4 %collective-permute-start.33 = (f32[64,256]{1,0:T(8,128)S(1)}, f32[64,256]{1,0:T(8,128)S(1)}, u32[]{:S(2)}, u32[]{:S(2)}) collective-permute-start(f32[64,256]{1,0:T(8,128)S(1)} %add_add_fusion.s0), channel_id=1, source_target_pairs={{0,192},{64,128},{128,64},{192,0},{1,193},{65,129},{129,65},{193,1... | collective-permute-start | bytes 196616 | tf_op jit(solution)/shard_map/right/ppermute | solution.py:42
  173.2 7.3 %collective-permute-start.32 = (f32[64,256]{1,0:T(8,128)S(1)}, f32[64,256]{1,0:T(8,128)S(1)}, u32[]{:S(2)}, u32[]{:S(2)}) collective-permute-start(f32[64,256]{1,0:T(8,128)S(1)} %add_add_fusion.s0), channel_id=1, source_target_pairs={{0,128},{64,192},{128,0},{192,64},{1,129},{65,193},{129,1},{193,65... | collective-permute-start | bytes 196616 | tf_op jit(solution)/shard_map/right/ppermute | solution.py:42
  (13 other events, 41.9 us)
Sparse Core Ops, SparseCore 0:
  65.9 35.0 all-gather.4
  102.8 32.4 all-gather.6
